TPU v7x, 32 devices: a whole 2x2x4 slice. The times are simulated.
32 devices in a mesh: cells: 16 (over z, y, core), genes: 2 (over x).
Axes of the slice: x: 2, y: 2, z: 4, core: 2. Of those that a mesh axis runs over, the one named last changes fastest.
Arguments:
- data: bfloat16 [16384, 2000], P('cells', 'genes'), may hold values from -6 to 6
- start: float32 [2000, 64], P('genes'), may hold values from -6 to 6
- link_dev: int32 [64, 8], P('cells'), may hold values from 0 to 15, all different within a row; in each aligned block of 4 rows (0 to 3, 4 to 7, ...) at most 4 rows name the same one
- link_slot: int32 [64, 8], P('cells'), may hold values from 0 to 3
- link_weight: int32 [64, 8], P('cells'), may hold values from 1 to 8
Outputs:
- loadings: float32 [2000, 64], P('genes')
- smoothed: bfloat16 [64, 16384], P('genes', 'cells')
Inputs may be any that keep to these rules, and one draw needn't show every extreme that they name: `link_dev`: each row names 8 different devices; the tiles of one device name any one device in at most 4 links, and some device in exactly 4.
All inputs are finite; a program needn't handle non-finite values.
Results may differ from a plain program's by a relative error of at most 0.017.
Values may be sent and summed in bfloat16 or wider, within the bound.
No kernel may reach another device: no remote copies, remote signals or barrier semaphores. Data moves between devices by JAX's collectives and lax.ppermute only.
A program may use at most 64 MiB of HBM per device.

v0:
```python
import math

import jax
import jax.numpy as jnp
from jax import lax
from jax.sharding import PartitionSpec as P

ITERS = 3


self_weight = 8.0


def per_device(data, start, link_dev, link_slot, link_weight):
    devices = lax.axis_size("cells")
    groups = lax.axis_size("genes")
    tiles_here, neighbours = link_dev.shape
    tile_cells = data.shape[0] // tiles_here
    genes_total = data.shape[1] * groups
    width = start.shape[1]
    part_width = width // groups
    capacity = max(2, 2 * tiles_here * neighbours // devices)
    slot_count = devices * capacity
    links = tiles_here * neighbours
    columns = part_width * tile_cells
    flat_dev = link_dev.reshape(links)
    flat_slot = link_slot.reshape(links)
    flat_weight = link_weight.reshape(links)
    dev_hits = (flat_dev[:, None] == jnp.arange(devices, dtype=jnp.int32)[None, :]).astype(
        jnp.int32
    )
    earlier = jnp.cumsum(dev_hits, axis=0) - dev_hits
    ranking = jnp.sum(earlier * dev_hits, axis=1)
    position = flat_dev * capacity + ranking
    placed = (position[:, None] == jnp.arange(slot_count, dtype=jnp.int32)[None, :]).astype(
        jnp.int32
    )
    wanted = jnp.sum(placed * (flat_slot + 1)[:, None], axis=0).reshape(devices, capacity)
    wanted_weight = jnp.sum(placed * flat_weight[:, None], axis=0).reshape(devices, capacity)
    asked_pair = (
        lax.all_to_all(wanted, "cells", split_axis=0, concat_axis=0, tiled=True),
        lax.all_to_all(wanted_weight, "cells", split_axis=0, concat_axis=0, tiled=True),
    )
    asked = asked_pair[0].reshape(slot_count)
    asked_weight = asked_pair[1].reshape(slot_count)
    tile_ids = jnp.arange(tiles_here, dtype=jnp.int32)
    serve_match = ((asked - 1)[:, None] == tile_ids[None, :]).astype(jnp.int32)
    serve = serve_match.astype(jnp.bfloat16)
    collect = (serve_match * asked_weight[:, None]).T.astype(jnp.bfloat16)
    placed_tiles = placed.reshape(tiles_here, neighbours, slot_count)
    link_matrix = jnp.sum(placed_tiles * link_weight[:, :, None], axis=1).astype(jnp.bfloat16)
    sender = jnp.sum(placed_tiles, axis=1).astype(jnp.bfloat16)
    degree = (self_weight + jnp.sum(link_weight, axis=1).astype(jnp.float32))[:, None]
    loadings = start
    smoothed = jnp.zeros((part_width, tiles_here * tile_cells), jnp.bfloat16)
    for step in range(ITERS):
        narrow = loadings.astype(jnp.bfloat16)
        partial_scores = lax.dot_general(
            narrow, data, (((0,), (1,)), ((), ())), preferred_element_type=jnp.float32
        )
        summed = lax.psum(partial_scores.astype(jnp.bfloat16), "genes").astype(jnp.float32)
        mine = lax.dynamic_slice_in_dim(summed, lax.axis_index("genes") * part_width, part_width, 0)
        scores = (mine / math.sqrt(genes_total)).astype(jnp.bfloat16)
        tiles = (
            scores.reshape(part_width, tiles_here, tile_cells)
            .transpose(1, 0, 2)
            .reshape(tiles_here, columns)
        )
        outgoing = jnp.dot(serve, tiles, preferred_element_type=jnp.float32).astype(jnp.bfloat16)
        linked = jnp.dot(
            link_matrix,
            lax.all_to_all(
                outgoing.reshape(devices, capacity, columns),
                "cells",
                split_axis=0,
                concat_axis=0,
                tiled=True,
            ).reshape(slot_count, -1),
            preferred_element_type=jnp.float32,
        )
        first = lax.optimization_barrier(
            ((self_weight * tiles.astype(jnp.float32) + linked) / degree).astype(jnp.bfloat16)
        )
        spread = lax.optimization_barrier(
            (self_weight * first.astype(jnp.float32) / degree).astype(jnp.bfloat16)
        )
        returning = lax.dot_general(
            sender, spread, (((0,), (0,)), ((), ())), preferred_element_type=jnp.float32
        ).astype(jnp.bfloat16)
        pushed = jnp.dot(
            collect,
            lax.all_to_all(
                returning.reshape(devices, capacity, columns),
                "cells",
                split_axis=0,
                concat_axis=0,
                tiled=True,
            ).reshape(slot_count, -1),
            preferred_element_type=jnp.float32,
        )
        second = (self_weight * spread.astype(jnp.float32) + pushed).astype(jnp.bfloat16)
        smoothed = (
            second.reshape(tiles_here, part_width, tile_cells)
            .transpose(1, 0, 2)
            .reshape(part_width, tiles_here * tile_cells)
        )
        update = lax.dot_general(
            data,
            lax.all_gather(smoothed, "genes", axis=0, tiled=True),
            (((0,), (1,)), ((), ())),
            preferred_element_type=jnp.float32,
        )
        update = lax.psum(update, "cells")
        gram_part = jnp.dot(
            update.T, update, precision=lax.Precision.HIGHEST, preferred_element_type=jnp.float32
        )
        gram = lax.psum(gram_part, "genes") / genes_total
        factor = jnp.linalg.cholesky(gram)
        loadings = lax.linalg.triangular_solve(
            factor, update, left_side=False, lower=True, transpose_a=True
        )
    return (loadings, smoothed)


def solution(mesh):
    placed = (
        P("cells", "genes"),
        P("genes", None),
        P("cells", None),
        P("cells", None),
        P("cells", None),
    )
    return jax.shard_map(
        per_device,
        mesh=mesh,
        in_specs=placed,
        out_specs=(P("genes", None), P("genes", "cells")),
        check_vma=False,
    )
```

profile of v0, /device:TPU:0, one launch (start us, length us, event | category | flops | bytes accessed | tf_op | source)
XLA Modules:
  0.0 657.3 jit_solution(18252619915090422057)
XLA Ops:
  8.7 2.2 convolution_convert_fusion.8
  12.3 7.4 %all-to-all-start = ((s32[16,1,4]{2,1,0:T(1,128)}), s32[16,1,4]{2,1,0:T(1,128)S(1)}, u32[]{:S(2)}, u32[]{:S(2)}) async-start(s32[16,1,4]{2,1,0:T(1,128)} %bitcast.2), calls=%async_computation | async-start | bytes 16384 | tf_op jit(solution)/shard_map/all_to_all | solution.py:41
  19.7 6.3 all-to-all-done
  26.2 9.1 %all-reduce.7.cloned.1.call-done = bf16[64,1024]{1,0:T(8,128)(2,1)} async-done(((bf16[64,1024]{1,0:T(8,128)(2,1)}), bf16[64,1024]{1,0:T(8,128)(2,1)}) %all-reduce.7.cloned.1.call-update) | async-done | bytes 131088 | tf_op jit(solution)/shard_map/psum | solution.py:61
  37.8 5.6 all-to-all-start.1
  44.4 21.9 %all-to-all-done.1 = bf16[16,4,8192]{2,1,0:T(4,128)(2,1)S(1)} async-done(((bf16[16,4,8192]{2,1,0:T(4,128)(2,1)}), bf16[16,4,8192]{2,1,0:T(4,128)(2,1)S(1)}, u32[]{:S(2)}, u32[]{:S(2)}) %all-to-all-start.1) | async-done | bytes 1048608 | tf_op jit(solution)/shard_map/all_to_all | solution.py:72
  66.4 6.9 %all-to-all-start.2 = ((s32[16,1,4]{2,1,0:T(1,128)}), s32[16,1,4]{2,1,0:T(1,128)S(1)}, u32[]{:S(2)}, u32[]{:S(2)}) async-start(s32[16,1,4]{2,1,0:T(1,128)} %bitcast.4), calls=%async_computation.2 | async-start | bytes 16384 | tf_op jit(solution)/shard_map/all_to_all | solution.py:42
  77.7 1.9 all-to-all-done.2
  79.6 4.1 all-to-all-start.3
  85.0 21.6 %all-to-all-done.3 = bf16[16,4,8192]{2,1,0:T(4,128)(2,1)S(1)} async-done(((bf16[16,4,8192]{2,1,0:T(4,128)(2,1)}), bf16[16,4,8192]{2,1,0:T(4,128)(2,1)S(1)}, u32[]{:S(2)}, u32[]{:S(2)}) %all-to-all-start.3) | async-done | bytes 1048608 | tf_op jit(solution)/shard_map/all_to_all | solution.py:92
  109.3 5.3 all_gather.9
  116.0 89.9 %all-reduce.9.cloned.1.call-done = f32[1000,64]{0,1:T(8,128)} async-done(((f32[1000,64]{0,1:T(8,128)}), f32[1000,64]{0,1:T(8,128)}) %all-reduce.9.cloned.1.call-update) | async-done | bytes 256016 | tf_op jit(solution)/shard_map/psum | solution.py:113
  207.3 8.3 %psum.65 = f32[64,64]{0,1:T(8,128)S(1)} all-reduce(f32[64,64]{0,1:T(8,128)S(1)} %fusion.50), channel_id=1, replica_groups=mesh['cells'=16,'genes'=2] {'genes'}, use_global_device_ids=true, to_apply=%region_9.10 | all-reduce | flops 4096 | bytes 32768 | tf_op jit(solution)/shard_map/psum | solution.py:117
  215.7 5.8 cholesky.59
  222.9 4.9 custom-call.7
  230.5 21.1 %all-reduce.11.cloned.1.call-done = bf16[64,1024]{1,0:T(8,128)(2,1)} async-done(((bf16[64,1024]{1,0:T(8,128)(2,1)}), bf16[64,1024]{1,0:T(8,128)(2,1)}) %all-reduce.11.cloned.1.call-update) | async-done | bytes 131088 | tf_op jit(solution)/shard_map/psum | solution.py:61
  255.4 30.4 %all_to_all.48 = bf16[16,4,8192]{2,1,0:T(4,128)(2,1)} all-to-all(bf16[16,4,8192]{2,1,0:T(4,128)(2,1)S(1)} %reshape.150), channel_id=1, replica_groups=mesh['cells'=16,'genes'=2] {'cells'}, dimensions={0} | all-to-all | bytes 2097152 | tf_op jit(solution)/shard_map/all_to_all | solution.py:72
  290.5 29.7 %all_to_all.49 = bf16[16,4,8192]{2,1,0:T(4,128)(2,1)} all-to-all(bf16[16,4,8192]{2,1,0:T(4,128)(2,1)S(1)} %reshape.152), channel_id=1, replica_groups=mesh['cells'=16,'genes'=2] {'cells'}, dimensions={0} | all-to-all | bytes 2097152 | tf_op jit(solution)/shard_map/all_to_all | solution.py:92
  321.8 5.4 all_gather.10
  328.8 87.8 %all-reduce.13.cloned.1.call-done = f32[1000,64]{0,1:T(8,128)} async-done(((f32[1000,64]{0,1:T(8,128)}), f32[1000,64]{0,1:T(8,128)}) %all-reduce.13.cloned.1.call-update) | async-done | bytes 256016 | tf_op jit(solution)/shard_map/psum | solution.py:113
  418.0 8.5 %psum.68 = f32[64,64]{0,1:T(8,128)S(1)} all-reduce(f32[64,64]{0,1:T(8,128)S(1)} %fusion.51), channel_id=1, replica_groups=mesh['cells'=16,'genes'=2] {'genes'}, use_global_device_ids=true, to_apply=%region_14.17 | all-reduce | flops 4096 | bytes 32768 | tf_op jit(solution)/shard_map/psum | solution.py:117
  426.6 5.8 cholesky.70
  433.8 4.9 custom-call.8
  441.4 21.1 %all-reduce.15.cloned.1.call-done = bf16[64,1024]{1,0:T(8,128)(2,1)} async-done(((bf16[64,1024]{1,0:T(8,128)(2,1)}), bf16[64,1024]{1,0:T(8,128)(2,1)}) %all-reduce.15.cloned.1.call-update) | async-done | bytes 131088 | tf_op jit(solution)/shard_map/psum | solution.py:61
  466.3 30.4 %all_to_all.50 = bf16[16,4,8192]{2,1,0:T(4,128)(2,1)} all-to-all(bf16[16,4,8192]{2,1,0:T(4,128)(2,1)S(1)} %reshape.158), channel_id=1, replica_groups=mesh['cells'=16,'genes'=2] {'cells'}, dimensions={0} | all-to-all | bytes 2097152 | tf_op jit(solution)/shard_map/all_to_all | solution.py:72
  500.1 29.9 %all_to_all.51 = bf16[16,4,8192]{2,1,0:T(4,128)(2,1)} all-to-all(bf16[16,4,8192]{2,1,0:T(4,128)(2,1)} %reshape.160), channel_id=1, replica_groups=mesh['cells'=16,'genes'=2] {'cells'}, dimensions={0} | all-to-all | bytes 2097152 | tf_op jit(solution)/shard_map/all_to_all | solution.py:92
  531.7 5.4 all_gather.11
  538.6 87.9 %all-reduce.17.cloned.1.call-done = f32[1000,64]{0,1:T(8,128)} async-done(((f32[1000,64]{0,1:T(8,128)}), f32[1000,64]{0,1:T(8,128)}) %all-reduce.17.cloned.1.call-update) | async-done | bytes 256016 | tf_op jit(solution)/shard_map/psum | solution.py:113
  627.9 8.3 %psum.71 = f32[64,64]{0,1:T(8,128)S(1)} all-reduce(f32[64,64]{0,1:T(8,128)S(1)} %fusion.52), channel_id=1, replica_groups=mesh['cells'=16,'genes'=2] {'genes'}, use_global_device_ids=true, to_apply=%region_17.20 | all-reduce | flops 4096 | bytes 32768 | tf_op jit(solution)/shard_map/psum | solution.py:117
  636.3 5.8 cholesky.81
  643.5 4.9 custom-call.9
  648.4 2.1 convolution_bitcast_fusion
  (108 shorter events, 52.0 us)
Async XLA Ops:
  7.2 1.6 copy-start
  7.2 3.7 copy-start.3
  7.2 3.8 copy-start.2
  7.2 3.9 copy-start.4
  7.2 28.0 %all-reduce.7.cloned.1.call-start = ((), (), s32[]{:S(2)}) async-start(), calls=%async_computation.8 | async-start | bytes 262144 | tf_op jit(solution)/shard_map/psum | solution.py:61
  12.3 13.7 %all-to-all-start = ((s32[16,1,4]{2,1,0:T(1,128)}), s32[16,1,4]{2,1,0:T(1,128)S(1)}, u32[]{:S(2)}, u32[]{:S(2)}) async-start(s32[16,1,4]{2,1,0:T(1,128)} %bitcast.2), calls=%async_computation | async-start | bytes 16384 | tf_op jit(solution)/shard_map/all_to_all | solution.py:41
  37.8 28.6 %all-to-all-start.1 = ((bf16[16,4,8192]{2,1,0:T(4,128)(2,1)}), bf16[16,4,8192]{2,1,0:T(4,128)(2,1)S(1)}, u32[]{:S(2)}, u32[]{:S(2)}) async-start(bf16[16,4,8192]{2,1,0:T(4,128)(2,1)} %reshape.142), calls=%async_computation.1 | async-start | bytes 2097152 | tf_op jit(solution)/shard_map/all_to_all | solution.py:72
  66.4 13.2 %all-to-all-start.2 = ((s32[16,1,4]{2,1,0:T(1,128)}), s32[16,1,4]{2,1,0:T(1,128)S(1)}, u32[]{:S(2)}, u32[]{:S(2)}) async-start(s32[16,1,4]{2,1,0:T(1,128)} %bitcast.4), calls=%async_computation.2 | async-start | bytes 16384 | tf_op jit(solution)/shard_map/all_to_all | solution.py:42
  79.6 27.1 %all-to-all-start.3 = ((bf16[16,4,8192]{2,1,0:T(4,128)(2,1)}), bf16[16,4,8192]{2,1,0:T(4,128)(2,1)S(1)}, u32[]{:S(2)}, u32[]{:S(2)}) async-start(bf16[16,4,8192]{2,1,0:T(4,128)(2,1)} %reshape.144), calls=%async_computation.3 | async-start | bytes 2097152 | tf_op jit(solution)/shard_map/all_to_all | solution.py:92
  83.7 122.2 %all-reduce.9.cloned.1.call-start = ((), (), s32[]{:S(2)}) async-start(), calls=%async_computation.9 | async-start | bytes 524288 | tf_op jit(solution)/shard_map/psum | solution.py:113
  116.0 135.6 %all-reduce.11.cloned.1.call-start = ((), (), s32[]{:S(2)}) async-start(), calls=%async_computation.10 | async-start | bytes 262144 | tf_op jit(solution)/shard_map/psum | solution.py:61
  230.5 186.1 %all-reduce.13.cloned.1.call-start = ((), (), s32[]{:S(2)}) async-start(), calls=%async_computation.11 | async-start | bytes 524288 | tf_op jit(solution)/shard_map/psum | solution.py:113
  328.7 133.8 %all-reduce.15.cloned.1.call-start = ((), (), s32[]{:S(2)}) async-start(), calls=%async_computation.12 | async-start | bytes 262144 | tf_op jit(solution)/shard_map/psum | solution.py:61
  441.3 185.1 %all-reduce.17.cloned.1.call-start = ((), (), s32[]{:S(2)}) async-start(), calls=%async_computation.13 | async-start | bytes 524288 | tf_op jit(solution)/shard_map/psum | solution.py:113
  531.7 118.8 %copy-start.1 = (bf16[4,4,8,256]{3,2,0,1:T(8,128)(2,1)}, bf16[4,4,8,256]{3,2,0,1:T(8,128)(2,1)S(1)}, u32[]{:S(2)}) copy-start(bf16[4,4,8,256]{3,2,0,1:T(8,128)(2,1)S(1)} %copy.48) | copy-start | bytes 196612
Sparse Core Ops, SparseCore 0:
  11.0 24.1 all-reduce.6
  116.1 89.7 all-reduce.8
  230.6 20.9 all-reduce.10
  328.8 87.6 all-reduce.12
  441.4 20.9 all-reduce.14
  538.7 87.7 all-reduce.16
where the time goes:
time: 659 us; the launch traced here: 657 us
  waiting for transfers between devices  369 us (56%)
  blocking collectives  162 us (25%)
  other arithmetic  40.4 us (6%)
  matrix products  27.7 us (4%)
  starting transfers between devices  24.2 us (4%)
  local copies, waits for them, and re-layouts  19.9 us (3%)
  between operations  14.6 us (2%)
    psum x3, waiting for transfers between devices, per_device(): update = lax.psum(update, 'cells')  266 us
    all_to_all x2, blocking collectives, per_device(): lax.all_to_all(outgoing.reshape(devices, capacity, columns), 'cells', spl...  60.7 us
    all_to_all x2, blocking collectives, per_device(): lax.all_to_all(returning.reshape(devices, capacity, columns), 'cells', sp...  59.7 us
    psum x3, waiting for transfers between devices, per_device(): lax.psum(partial_scores.astype(jnp.bfloat16), 'genes').astype(jnp.float32)  51.3 us
    psum x3, blocking collectives, per_device(): gram = lax.psum(gram_part, 'genes') / genes_total  25.2 us
    all_to_all x1, waiting for transfers between devices, per_device(): lax.all_to_all(outgoing.reshape(devices, capacity, columns), 'cells', spl...  21.9 us
    all_to_all x1, waiting for transfers between devices, per_device(): lax.all_to_all(returning.reshape(devices, capacity, columns), 'cells', sp...  21.6 us
    another operation x9, other arithmetic, per_device(): factor = jnp.linalg.cholesky(gram)  19.6 us
  transfers between devices with their start and end apart: 10, of which 10 were waited for; matrix products, arithmetic and copies ran while one was open for 1% of the time, Pallas kernels for 0%

commit v1 on v0

--- a/solution.py
+++ b/solution.py
@@ -1,17 +1,276 @@
+import functools
 import math
 
 import jax
 import jax.numpy as jnp
 from jax import lax
+from jax.experimental import pallas as pl
+from jax.experimental.pallas import tpu as pltpu
 from jax.sharding import PartitionSpec as P
 
 ITERS = 3
-
+LANES = 128
 
 self_weight = 8.0
-
-
-def per_device(data, start, link_dev, link_slot, link_weight):
+HIGHEST = lax.Precision.HIGHEST
+
+
+def inverse_factor(gram):
+    width = gram.shape[0]
+    rows = lax.broadcasted_iota(jnp.int32, (width, width), 0)
+    cols = lax.broadcasted_iota(jnp.int32, (width, width), 1)
+    eye = (rows == cols).astype(jnp.float32)
+    state = jnp.concatenate([eye, gram], axis=1)
+    strips = [state[at : at + 8] for at in range(0, width, 8)]
+    place = lax.broadcasted_iota(jnp.int32, (8, 2 * width), 0)
+    for k in range(width - 1):
+        own, within = divmod(k, 8)
+        row = strips[own][within : within + 1]
+        scaled = row / row[:, width + k : width + k + 1]
+        for strip in range(own, width // 8):
+            factor = strips[strip][:, width + k : width + k + 1]
+            if strip == own:
+                factor = jnp.where(place > within, factor, 0.0)
+            strips[strip] = strips[strip] - factor * scaled
+    state = jnp.concatenate(strips, axis=0)
+    pivots = jnp.sum(eye * state[:, width:], axis=1, keepdims=True)
+    return state[:, :width] * lax.rsqrt(pivots)
+
+
+def link_matrix(packed, tiles, neighbours, slots, rows_of):
+    own_dev, own_slot, own_weight = packed[:, 0:1], packed[:, 1:2], packed[:, 2:3]
+    target = own_dev * slots + own_slot
+    lane = lax.broadcasted_iota(jnp.int32, (tiles * neighbours, tiles), 1).astype(jnp.float32)
+    hits = jnp.where(lane == target, own_weight, 0.0)
+    weights = jnp.sum(hits.reshape(tiles, neighbours, tiles), axis=1)
+    tile_row = lax.broadcasted_iota(jnp.int32, (tiles, tiles), 0)
+    tile_col = lax.broadcasted_iota(jnp.int32, (tiles, tiles), 1)
+    weights = weights + jnp.where(tile_row == tile_col, self_weight, 0.0)
+    cells = tiles * rows_of
+    tile_of = lax.broadcasted_iota(jnp.int32, (cells, tiles), 0) // rows_of
+    expand = (tile_of == lax.broadcasted_iota(jnp.int32, (cells, tiles), 1)).astype(jnp.bfloat16)
+    tall = jnp.dot(expand, weights.astype(jnp.bfloat16), preferred_element_type=jnp.float32)
+    full = lax.dot_general(
+        tall.astype(jnp.bfloat16),
+        expand,
+        (((1,), (1,)), ((), ())),
+        preferred_element_type=jnp.float32,
+    )
+    same = (
+        lax.broadcasted_iota(jnp.int32, (cells, cells), 0) % rows_of
+        == lax.broadcasted_iota(jnp.int32, (cells, cells), 1) % rows_of
+    )
+    full = jnp.where(same, full, 0.0).astype(jnp.bfloat16)
+    ones = jnp.ones((8, cells), jnp.bfloat16)
+    degree = lax.dot_general(
+        ones, full, (((1,), (1,)), ((), ())), preferred_element_type=jnp.float32
+    )
+    return full, degree
+
+
+def diffuse(scores, links, degree):
+    scores = scores.astype(jnp.bfloat16)
+    total = lax.dot_general(
+        scores, links, (((1,), (1,)), ((), ())), preferred_element_type=jnp.float32
+    )
+    first = (total / degree).astype(jnp.bfloat16).astype(jnp.float32)
+    spread = (self_weight * first / degree).astype(jnp.bfloat16)
+    return jnp.dot(spread, links, preferred_element_type=jnp.float32).astype(jnp.bfloat16)
+
+
+def block(data_ref, group):
+    part = data_ref[:, group]
+    return part.reshape(part.shape[0] * part.shape[1], part.shape[2])
+
+
+def push_update(genes_here, data_ref, second, out_ref):
+    groups, padded = data_ref.shape[1], data_ref.shape[3]
+    chunk = out_ref.shape[1]
+    halves = second.shape[0] // chunk
+    blocks = padded // LANES
+    for group in range(groups):
+        update = jnp.dot(second, block(data_ref, group), preferred_element_type=jnp.float32)
+        lane = lax.broadcasted_iota(jnp.int32, update.shape, 1)
+        update = jnp.where(lane < genes_here, update, 0.0).astype(jnp.bfloat16)
+        for at in range(blocks):
+            for half in range(halves):
+                out_ref[(group * blocks + at) * halves + half] = update[
+                    half * chunk : (half + 1) * chunk, at * LANES : (at + 1) * LANES
+                ]
+
+
+def pull_update(chunks_ref, update_ref):
+    groups, width, padded = update_ref.shape
+    chunk = chunks_ref.shape[1]
+    halves = width // chunk
+    blocks = padded // LANES
+    for group in range(groups):
+        for at in range(blocks):
+            for half in range(halves):
+                update_ref[
+                    group, half * chunk : (half + 1) * chunk, at * LANES : (at + 1) * LANES
+                ] = chunks_ref[(group * blocks + at) * halves + half]
+
+
+def gram_of(update_ref, genes_total):
+    gram = None
+    for group in range(update_ref.shape[0]):
+        update = update_ref[group]
+        part = lax.dot_general(
+            update, update, (((1,), (1,)), ((), ())), preferred_element_type=jnp.float32
+        )
+        gram = part if gram is None else gram + part
+    return gram / genes_total
+
+
+def first_kernel(
+    genes_here, slots, neighbours, own_ref, data_ref, start_ref, out_ref, links_ref, degree_ref
+):
+    devices, groups, rows, padded = data_ref.shape
+    tiles = devices * slots
+    packed = data_ref[:, 0][:, : slots * neighbours, padded - LANES :].astype(jnp.float32)
+    packed = packed.reshape(tiles * neighbours, LANES)
+    offset = genes_here - (padded - LANES)
+    links, degree = link_matrix(
+        packed[:, offset : offset + 3], tiles, neighbours, slots, rows // slots
+    )
+    links_ref[...] = links
+    degree_ref[...] = degree
+    scores = None
+    for shift in range(groups):
+        group = lax.rem(own_ref[0] + groups - shift, groups)
+        part = lax.dot_general(
+            start_ref[shift],
+            block(data_ref, group),
+            (((1,), (1,)), ((), ())),
+            preferred_element_type=jnp.float32,
+        )
+        scores = part if scores is None else scores + part
+    scores = scores / math.sqrt(genes_here * groups)
+    push_update(genes_here, data_ref, diffuse(scores, links, degree[:1]), out_ref)
+
+
+def next_kernel(
+    genes_here, chunks_ref, data_ref, links_ref, degree_ref, out_ref, second_ref, update_ref
+):
+    groups = data_ref.shape[1]
+    genes_total = genes_here * groups
+    pull_update(chunks_ref, update_ref)
+    inverse = inverse_factor(gram_of(update_ref, genes_total))
+    scores = None
+    for group in range(groups):
+        part = lax.dot_general(
+            update_ref[group],
+            block(data_ref, group),
+            (((1,), (1,)), ((), ())),
+            preferred_element_type=jnp.float32,
+        )
+        scores = part if scores is None else scores + part
+    scores = jnp.dot(
+        inverse, scores, precision=HIGHEST, preferred_element_type=jnp.float32
+    ) / math.sqrt(genes_total)
+    second = diffuse(scores, links_ref[...], degree_ref[:1])
+    second_ref[...] = second
+    push_update(genes_here, data_ref, second, out_ref)
+
+
+def last_kernel(genes_here, own_ref, chunks_ref, out_ref, update_ref):
+    pull_update(chunks_ref, update_ref)
+    genes_total = genes_here * update_ref.shape[0]
+    inverse = inverse_factor(gram_of(update_ref, genes_total))
+    mine = update_ref[own_ref[0]].astype(jnp.float32)
+    loadings = jnp.dot(inverse, mine, precision=HIGHEST, preferred_element_type=jnp.float32)
+    out_ref[...] = loadings.T[:genes_here]
+
+
+def sum_kernel(chunks_ref, out_ref):
+    total = jnp.sum(chunks_ref[...].astype(jnp.float32), axis=0).astype(jnp.bfloat16)
+    out_ref[...] = jnp.broadcast_to(total[None], out_ref.shape)
+
+
+def call(kernel, out_shape, scratch=(), scalars=0, arrays=0):
+    in_specs = [pl.BlockSpec(memory_space=pltpu.SMEM)] * scalars
+    in_specs += [pl.BlockSpec(memory_space=pltpu.VMEM)] * arrays
+    return pl.pallas_call(
+        kernel,
+        out_shape=out_shape,
+        in_specs=in_specs,
+        out_specs=jax.tree.map(lambda _: pl.BlockSpec(memory_space=pltpu.VMEM), out_shape),
+        scratch_shapes=list(scratch),
+        compiler_params=pltpu.CompilerParams(vmem_limit_bytes=32 * 1024 * 1024),
+    )
+
+
+def by_cell(data, start, link_dev, link_slot, link_weight):
+    axes = ("cells", "genes")
+    devices, groups = lax.axis_size("cells"), lax.axis_size("genes")
+    parts = devices * groups
+    slots, neighbours = link_dev.shape
+    genes_here, width = data.shape[1], start.shape[1]
+    tile_cells = data.shape[0] // slots
+    rows_of = tile_cells // parts
+    rows = slots * rows_of
+    padded = -(-genes_here // LANES) * LANES
+    cells = devices * rows
+    chunk = groups * width * padded // (parts * LANES)
+    own = lax.axis_index("genes").astype(jnp.int32).reshape(1)
+
+    packed = jnp.stack([link_dev, link_slot, link_weight], axis=-1).astype(jnp.bfloat16)
+    packed = packed.reshape(slots * neighbours, 3)
+    packed = jnp.pad(packed, ((0, rows - slots * neighbours), (0, padded - genes_here - 3)))
+    moved = data.reshape(slots, parts, rows_of, genes_here).transpose(1, 0, 2, 3)
+    moved = moved.reshape(parts, rows, genes_here)
+    moved = jnp.concatenate(
+        [moved, jnp.broadcast_to(packed[None], (parts, rows, padded - genes_here))], axis=2
+    )
+    moved = lax.all_to_all(moved, axes, 0, 0, tiled=True).reshape(devices, groups, rows, padded)
+    narrow = jnp.pad(start.astype(jnp.bfloat16).T, ((0, 0), (0, padded - genes_here)))
+    starts = [narrow]
+    for shift in range(1, groups):
+        pairs = [(at, (at + shift) % groups) for at in range(groups)]
+        starts.append(lax.ppermute(narrow, "genes", pairs))
+    starts = jnp.stack(starts)
+
+    chunks = jax.ShapeDtypeStruct((parts, chunk, LANES), jnp.bfloat16)
+    update = pltpu.VMEM((groups, width, padded), jnp.bfloat16)
+    links = jax.ShapeDtypeStruct((cells, cells), jnp.bfloat16)
+    degree = jax.ShapeDtypeStruct((8, cells), jnp.float32)
+    second = jax.ShapeDtypeStruct((width, cells), jnp.bfloat16)
+
+    def everywhere(pushed):
+        summed = call(sum_kernel, chunks, arrays=1)(
+            lax.all_to_all(pushed, axes, 0, 0, tiled=True)
+        )
+        return lax.all_to_all(summed, axes, 0, 0, tiled=True)
+
+    pushed, links, degree = call(
+        functools.partial(first_kernel, genes_here, slots, neighbours),
+        (chunks, links, degree),
+        scalars=1,
+        arrays=2,
+    )(own, moved, starts)
+    for step in range(1, ITERS):
+        pushed, diffused = call(
+            functools.partial(next_kernel, genes_here), (chunks, second), (update,), arrays=4
+        )(everywhere(pushed), moved, links, degree)
+    loadings = call(
+        functools.partial(last_kernel, genes_here),
+        jax.ShapeDtypeStruct((genes_here, width), jnp.float32),
+        (update,),
+        scalars=1,
+        arrays=1,
+    )(own, everywhere(pushed))
+
+    part_width = width // groups
+    smoothed = diffused.reshape(groups, part_width, devices, rows).transpose(2, 0, 1, 3)
+    smoothed = lax.all_to_all(
+        smoothed.reshape(parts, part_width, rows), axes, 0, 0, tiled=True
+    )
+    smoothed = smoothed.reshape(parts, part_width, slots, rows_of).transpose(1, 2, 0, 3)
+    return loadings, smoothed.reshape(part_width, slots * tile_cells)
+
+
+def by_tile(data, start, link_dev, link_slot, link_weight):
     devices = lax.axis_size("cells")
     groups = lax.axis_size("genes")
     tiles_here, neighbours = link_dev.shape
@@ -122,6 +381,25 @@
     return (loadings, smoothed)
 
 
+def per_device(data, start, link_dev, link_slot, link_weight):
+    parts = lax.axis_size("cells") * lax.axis_size("genes")
+    slots, neighbours = link_dev.shape
+    tile_cells = data.shape[0] // slots
+    genes_here, width = data.shape[1], start.shape[1]
+    padded = -(-genes_here // LANES) * LANES
+    rows = slots * tile_cells // parts
+    fits = (
+        tile_cells % (8 * parts) == 0
+        and rows % 16 == 0
+        and rows >= slots * neighbours
+        and slots * neighbours % 16 == 0
+        and padded - genes_here >= 3
+        and width * padded * lax.axis_size("genes") % (parts * LANES * 16) == 0
+    )
+    way = by_cell if fits else by_tile
+    return way(data, start, link_dev, link_slot, link_weight)
+
+
 def solution(mesh):
     placed = (
         P("cells", "genes"),

time: 659 us -> 178 us (0.27)
  waiting for transfers between devices: 369 us -> 72.8 us
  blocking collectives: 162 us -> 52.6 us
  other arithmetic: 40.4 us -> 1.73 us
  matrix products: 27.7 us -> 0 us
  Pallas kernels: 0 us -> 23.8 us
  between operations: 14.6 us -> 0.79 us
  local copies, waits for them, and re-layouts: 19.9 us -> 9.42 us
  starting transfers between devices: 24.2 us -> 16.9 us
    psum x6 -> x0, waiting for transfers between devices: 317 us -> none  [the longest x3 266 us: per_device(): update = lax.psum(update, 'cells')]
    all_to_all x4, blocking collectives: 120 us -> 52.6 us  [the longest x2 26.9 us: everywhere(): lax.all_to_all(pushed, axes, 0, 0, tiled=True)]
    another operation x16 -> x5, other arithmetic: 36.3 us -> 0.05 us  [the longest x1 0.03 us: by_cell(): starts = jnp.stack(starts)]
    psum x3 -> x0, blocking collectives: 25.2 us -> none  [per_device(): gram = lax.psum(gram_part, 'genes') / genes_total]
    pallas_call x0 -> x7, Pallas kernels: none -> 23.8 us  [the longest x2 14.5 us: by_cell(): call(functools.partial(next_kernel, genes_here), (chunks, second), (updat...]
    dot_general x21 -> x0, matrix products: 22.9 us -> none  [the longest x3 4.59 us: per_device(): lax.dot_general(narrow, data, (((0,), (1,)), ((), ())), preferred_element...]
    ppermute x0 -> x1, waiting for transfers between devices: none -> 19.2 us  [by_cell(): starts.append(lax.ppermute(narrow, 'genes', pairs))]
    all_gather x3 -> x0, blocking collectives: 16.2 us -> none  [per_device(): lax.all_gather(smoothed, 'genes', axis=0, tiled=True)]
  transfers between devices with their start and end apart: 10 -> 5, of which waited for: 10 -> 5; matrix products, arithmetic and copies ran while one was open for 1% -> 1% of each run, Pallas kernels for 0% -> 0%
where the time goes in v1:
time: 178 us
  waiting for transfers between devices  72.8 us (41%)
  blocking collectives  52.6 us (30%)
  Pallas kernels  23.8 us (13%)
  starting transfers between devices  16.9 us (9%)
  local copies, waits for them, and re-layouts  9.42 us (5%)
    all_to_all x1, waiting for transfers between devices, by_cell(): lax.all_to_all(moved, axes, 0, 0, tiled=True)  27.6 us
    all_to_all x2, blocking collectives, everywhere(): lax.all_to_all(pushed, axes, 0, 0, tiled=True)  26.9 us
    all_to_all x2, blocking collectives, everywhere(): return lax.all_to_all(summed, axes, 0, 0, tiled=True)  25.6 us
    ppermute x1, waiting for transfers between devices, by_cell(): starts.append(lax.ppermute(narrow, 'genes', pairs))  19.2 us
    pallas_call x2, Pallas kernels, by_cell(): call(functools.partial(next_kernel, genes_here), (chunks, second), (updat...  14.5 us
    all_to_all x1, waiting for transfers between devices, everywhere(): lax.all_to_all(pushed, axes, 0, 0, tiled=True)  9.57 us
    all_to_all x1, waiting for transfers between devices, everywhere(): return lax.all_to_all(summed, axes, 0, 0, tiled=True)  9.52 us
    all_to_all x1, starting transfers between devices, by_cell(): lax.all_to_all(moved, axes, 0, 0, tiled=True)  7.3 us
  transfers between devices with their start and end apart: 5, of which 5 were waited for; matrix products, arithmetic and copies ran while one was open for 1% of the time, Pallas kernels for 0%

profile of v1, /device:TPU:0, one launch (start us, length us, event | category | flops | bytes accessed | tf_op | source)
XLA Modules:
  0.0 178.0 jit_solution(4243047223809792806)
XLA Ops:
  0.6 4.0 %copy.17 = bf16[1024,1000]{1,0:T(8,128)(2,1)} copy(bf16[1024,1000]{0,1:T(8,128)(2,1)} %param.5) | data formatting | bytes 4096000 | tf_op args[0]
  4.6 1.9 %copy.27 = bf16[32,4,8,1000]{3,2,1,0:T(8,128)(2,1)S(1)} copy(bf16[32,4,8,1000]{3,2,0,1:T(8,128)(2,1)} %bitcast.24) | data formatting | bytes 4096000 | tf_op jit(solution)/shard_map/transpose | solution.py:221
  6.5 0.1 stack.21
  6.6 0.1 stack.22
  6.7 0.1 stack.23
  6.8 0.1 copy.25
  6.9 1.7 pad_maximum_fusion
  8.6 7.3 %all-to-all-start = ((bf16[32,32,1024]{2,1,0:T(8,128)(2,1)}), bf16[32,32,1024]{2,1,0:T(8,128)(2,1)S(1)}, u32[]{:S(2)}, u32[]{:S(2)}) async-start(bf16[32,32,1024]{2,1,0:T(8,128)(2,1)} %pad_maximum_fusion), calls=%async_computation | async-start | bytes 4194304 | tf_op jit(solution)/shard_map/all_to_all | solution.py:226
  16.0 1.8 %collective-permute-start = (bf16[64,1024]{1,0:T(8,128)(2,1)S(1)}, bf16[64,1024]{1,0:T(8,128)(2,1)S(1)}, u32[]{:S(2)}, u32[]{:S(2)}) collective-permute-start(bf16[64,1024]{1,0:T(8,128)(2,1)S(1)} %get-tuple-element.21), channel_id=1, source_target_pairs={{0,1},{1,0},{2,3},{3,2},{4,5},{5,4},{6,7},{7,6},{8,9},{9,8},{10,11... | collective-permute-start | bytes 393224 | tf_op jit(solution)/shard_map/ppermute | solution.py:231
  17.8 19.2 %collective-permute-done = bf16[64,1024]{1,0:T(8,128)(2,1)S(1)} collective-permute-done((bf16[64,1024]{1,0:T(8,128)(2,1)S(1)}, bf16[64,1024]{1,0:T(8,128)(2,1)S(1)}, u32[]{:S(2)}, u32[]{:S(2)}) %collective-permute-start) | collective-permute-done | bytes 131104 | tf_op jit(solution)/shard_map/ppermute | solution.py:231
  37.0 27.6 %all-to-all-done = bf16[32,32,1024]{2,1,0:T(8,128)(2,1)S(1)} async-done(((bf16[32,32,1024]{2,1,0:T(8,128)(2,1)}), bf16[32,32,1024]{2,1,0:T(8,128)(2,1)S(1)}, u32[]{:S(2)}, u32[]{:S(2)}) %all-to-all-start) | async-done | bytes 2097184 | tf_op jit(solution)/shard_map/all_to_all | solution.py:226
  64.7 2.2 %shard_map.68 = (bf16[32,32,128]{2,1,0:T(8,128)(2,1)S(1)}, bf16[512,512]{1,0:T(8,128)(2,1)S(1)}, f32[8,512]{1,0:T(8,128)S(1)}) custom-call(s32[1]{0:T(128)} %bitcast.own_ref, bf16[16,2,32,1024]{3,2,1,0:T(8,128)(2,1)S(1)} %bitcast.20, bf16[2,64,1024]{2,1,0:T(8,128)(2,1)S(1)} %pad_maximum_fusion.1.start_ref), custom_call_target="tpu_custom_call" | custom-call | tf_op jit(solution)/shard_map/pallas_call | solution.py:246
  66.9 14.1 %all_to_all.40.chunks_ref = bf16[32,32,128]{2,1,0:T(8,128)(2,1)S(1)} all-to-all(bf16[32,32,128]{2,1,0:T(8,128)(2,1)S(1)} %get-tuple-element.8), channel_id=1, replica_groups=mesh['cells'=16,'genes'=2] {'cells','genes'}, dimensions={0} | all-to-all | bytes 524288 | tf_op jit(solution)/shard_map/all_to_all | solution.py:242
  81.1 12.8 %all_to_all.41.chunks_ref = bf16[32,32,128]{2,1,0:T(8,128)(2,1)S(1)} all-to-all(bf16[32,32,128]{2,1,0:T(8,128)(2,1)S(1)} %shard_map.69), channel_id=1, replica_groups=mesh['cells'=16,'genes'=2] {'cells','genes'}, dimensions={0} | all-to-all | bytes 524288 | tf_op jit(solution)/shard_map/all_to_all | solution.py:244
  93.9 7.0 %shard_map.70 = (bf16[32,32,128]{2,1,0:T(8,128)(2,1)S(1)}, bf16[64,512]{1,0:T(8,128)(2,1)}) custom-call(bf16[32,32,128]{2,1,0:T(8,128)(2,1)S(1)} %all_to_all.41.chunks_ref, bf16[16,2,32,1024]{3,2,1,0:T(8,128)(2,1)S(1)} %bitcast.21, bf16[512,512]{1,0:T(8,128)(2,1)S(1)} %get-tuple-element.9.links_ref, f32[8,512]{1,0:T(8,128)S(1)} %get-tuple-element.10.degree_ref), custom_call_target="tpu_custom_call" | custom-call | tf_op jit(solution)/shard_map/pallas_call | solution.py:253
  101.0 12.8 %all_to_all.42.chunks_ref = bf16[32,32,128]{2,1,0:T(8,128)(2,1)S(1)} all-to-all(bf16[32,32,128]{2,1,0:T(8,128)(2,1)S(1)} %get-tuple-element.11), channel_id=1, replica_groups=mesh['cells'=16,'genes'=2] {'cells','genes'}, dimensions={0} | all-to-all | bytes 524288 | tf_op jit(solution)/shard_map/all_to_all | solution.py:242
  113.8 12.8 %all_to_all.43.chunks_ref = bf16[32,32,128]{2,1,0:T(8,128)(2,1)S(1)} all-to-all(bf16[32,32,128]{2,1,0:T(8,128)(2,1)S(1)} %shard_map.71), channel_id=1, replica_groups=mesh['cells'=16,'genes'=2] {'cells','genes'}, dimensions={0} | all-to-all | bytes 524288 | tf_op jit(solution)/shard_map/all_to_all | solution.py:244
  126.6 7.5 %shard_map.72 = (bf16[32,32,128]{2,1,0:T(8,128)(2,1)}, bf16[64,512]{1,0:T(8,128)(2,1)S(1)}) custom-call(bf16[32,32,128]{2,1,0:T(8,128)(2,1)S(1)} %all_to_all.43.chunks_ref, bf16[16,2,32,1024]{3,2,1,0:T(8,128)(2,1)S(1)} %bitcast.22, bf16[512,512]{1,0:T(8,128)(2,1)S(1)} %get-tuple-element.9.links_ref, f32[8,512]{1,0:T(8,128)S(1)} %get-tuple-element.10.degree_ref), custom_call_target="tpu_custom_call" | custom-call | tf_op jit(solution)/shard_map/pallas_call | solution.py:253
  134.1 2.6 %all-to-all-start.5 = ((bf16[32,32,128]{2,1,0:T(8,128)(2,1)}), bf16[32,32,128]{2,1,0:T(8,128)(2,1)S(1)}, u32[]{:S(2)}, u32[]{:S(2)}) async-start(bf16[32,32,128]{2,1,0:T(8,128)(2,1)} %get-tuple-element.12), calls=%async_computation.5 | async-start | bytes 524288 | tf_op jit(solution)/shard_map/all_to_all | solution.py:242
  136.7 0.2 reshape.43
  137.0 0.9 reshape.47
  137.8 9.6 %all-to-all-done.5.chunks_ref = bf16[32,32,128]{2,1,0:T(8,128)(2,1)S(1)} async-done(((bf16[32,32,128]{2,1,0:T(8,128)(2,1)}), bf16[32,32,128]{2,1,0:T(8,128)(2,1)S(1)}, u32[]{:S(2)}, u32[]{:S(2)}) %all-to-all-start.5) | async-done | bytes 262176 | tf_op jit(solution)/shard_map/all_to_all | solution.py:242
  147.4 2.6 %all-to-all-start.7 = ((bf16[32,2,512]{2,1,0:T(2,128)(2,1)}), bf16[32,2,512]{2,1,0:T(2,128)(2,1)S(1)}, u32[]{:S(2)}, u32[]{:S(2)}) async-start(bf16[32,2,512]{2,1,0:T(2,128)(2,1)} %reshape.47), calls=%async_computation.7 | async-start | bytes 131072 | tf_op jit(solution)/shard_map/all_to_all | solution.py:266
  150.0 0.8 shard_map.73
  150.7 6.9 %all-to-all-done.7 = bf16[32,2,512]{2,1,0:T(2,128)(2,1)S(1)} async-done(((bf16[32,2,512]{2,1,0:T(2,128)(2,1)}), bf16[32,2,512]{2,1,0:T(2,128)(2,1)S(1)}, u32[]{:S(2)}, u32[]{:S(2)}) %all-to-all-start.7) | async-done | bytes 65568 | tf_op jit(solution)/shard_map/all_to_all | solution.py:266
  157.6 2.6 %all-to-all-start.6 = ((bf16[32,32,128]{2,1,0:T(8,128)(2,1)}), bf16[32,32,128]{2,1,0:T(8,128)(2,1)S(1)}, u32[]{:S(2)}, u32[]{:S(2)}) async-start(bf16[32,32,128]{2,1,0:T(8,128)(2,1)} %shard_map.73), calls=%async_computation.6 | async-start | bytes 524288 | tf_op jit(solution)/shard_map/all_to_all | solution.py:244
  160.2 0.2 reshape.48
  160.4 0.2 copy.21
  160.6 0.8 copy.24
  161.4 9.5 %all-to-all-done.6.chunks_ref = bf16[32,32,128]{2,1,0:T(8,128)(2,1)S(1)} async-done(((bf16[32,32,128]{2,1,0:T(8,128)(2,1)}), bf16[32,32,128]{2,1,0:T(8,128)(2,1)S(1)}, u32[]{:S(2)}, u32[]{:S(2)}) %all-to-all-start.6) | async-done | bytes 262176 | tf_op jit(solution)/shard_map/all_to_all | solution.py:244
  170.9 6.2 %shard_map.74 = f32[1000,64]{1,0:T(8,128)S(1)} custom-call(s32[1]{0:T(128)} %bitcast.own_ref, bf16[32,32,128]{2,1,0:T(8,128)(2,1)S(1)} %all-to-all-done.6.chunks_ref), custom_call_target="tpu_custom_call" | custom-call | tf_op jit(solution)/shard_map/pallas_call | solution.py:256
  177.1 0.9 copy.23
  (21 shorter events, 0.4 us)
Async XLA Ops:
  4.6 1.9 %copy-start.1 = (s32[4,8]{1,0:T(4,128)S(1)}, s32[4,8]{1,0:T(4,128)}, u32[]{:S(2)}) copy-start(s32[4,8]{1,0:T(4,128)} %param.7) | copy-start | bytes 388
  4.6 2.0 %copy-start.2 = (s32[4,8]{1,0:T(4,128)S(1)}, s32[4,8]{1,0:T(4,128)}, u32[]{:S(2)}) copy-start(s32[4,8]{1,0:T(4,128)} %param.8) | copy-start | bytes 388
  4.6 2.1 %copy-start.3 = (s32[4,8]{1,0:T(4,128)S(1)}, s32[4,8]{1,0:T(4,128)}, u32[]{:S(2)}) copy-start(s32[4,8]{1,0:T(4,128)} %param.9) | copy-start | bytes 388
  8.6 7.3 %copy-start = (f32[1000,64]{0,1:T(8,128)S(1)}, f32[1000,64]{0,1:T(8,128)}, u32[]{:S(2)}) copy-start(f32[1000,64]{0,1:T(8,128)} %param.6) | copy-start | bytes 768004
  8.6 56.1 %all-to-all-start = ((bf16[32,32,1024]{2,1,0:T(8,128)(2,1)}), bf16[32,32,1024]{2,1,0:T(8,128)(2,1)S(1)}, u32[]{:S(2)}, u32[]{:S(2)}) async-start(bf16[32,32,1024]{2,1,0:T(8,128)(2,1)} %pad_maximum_fusion), calls=%async_computation | async-start | bytes 4194304 | tf_op jit(solution)/shard_map/all_to_all | solution.py:226
  16.0 21.0 %collective-permute-start = (bf16[64,1024]{1,0:T(8,128)(2,1)S(1)}, bf16[64,1024]{1,0:T(8,128)(2,1)S(1)}, u32[]{:S(2)}, u32[]{:S(2)}) collective-permute-start(bf16[64,1024]{1,0:T(8,128)(2,1)S(1)} %get-tuple-element.21), channel_id=1, source_target_pairs={{0,1},{1,0},{2,3},{3,2},{4,5},{5,4},{6,7},{7,6},{8,9},{9,8},{10,11... | collective-permute-start | bytes 393224 | tf_op jit(solution)/shard_map/ppermute | solution.py:231
  134.1 13.3 %all-to-all-start.5 = ((bf16[32,32,128]{2,1,0:T(8,128)(2,1)}), bf16[32,32,128]{2,1,0:T(8,128)(2,1)S(1)}, u32[]{:S(2)}, u32[]{:S(2)}) async-start(bf16[32,32,128]{2,1,0:T(8,128)(2,1)} %get-tuple-element.12), calls=%async_computation.5 | async-start | bytes 524288 | tf_op jit(solution)/shard_map/all_to_all | solution.py:242
  147.4 10.2 %all-to-all-start.7 = ((bf16[32,2,512]{2,1,0:T(2,128)(2,1)}), bf16[32,2,512]{2,1,0:T(2,128)(2,1)S(1)}, u32[]{:S(2)}, u32[]{:S(2)}) async-start(bf16[32,2,512]{2,1,0:T(2,128)(2,1)} %reshape.47), calls=%async_computation.7 | async-start | bytes 131072 | tf_op jit(solution)/shard_map/all_to_all | solution.py:266
  157.6 13.3 %all-to-all-start.6 = ((bf16[32,32,128]{2,1,0:T(8,128)(2,1)}), bf16[32,32,128]{2,1,0:T(8,128)(2,1)S(1)}, u32[]{:S(2)}, u32[]{:S(2)}) async-start(bf16[32,32,128]{2,1,0:T(8,128)(2,1)} %shard_map.73), calls=%async_computation.6 | async-start | bytes 524288 | tf_op jit(solution)/shard_map/all_to_all | solution.py:244

commit v2 on v1

--- a/solution.py
+++ b/solution.py
@@ -83,9 +83,8 @@
     return part.reshape(part.shape[0] * part.shape[1], part.shape[2])
 
 
-def push_update(genes_here, data_ref, second, out_ref):
+def push_update(genes_here, data_ref, second, out_ref, chunk):
     groups, padded = data_ref.shape[1], data_ref.shape[3]
-    chunk = out_ref.shape[1]
     halves = second.shape[0] // chunk
     blocks = padded // LANES
     for group in range(groups):
@@ -94,7 +93,7 @@
         update = jnp.where(lane < genes_here, update, 0.0).astype(jnp.bfloat16)
         for at in range(blocks):
             for half in range(halves):
-                out_ref[(group * blocks + at) * halves + half] = update[
+                out_ref[(group * blocks + at) * halves + half, :chunk] = update[
                     half * chunk : (half + 1) * chunk, at * LANES : (at + 1) * LANES
                 ]
 
@@ -123,16 +122,65 @@
     return gram / genes_total
 
 
+def regroup_kernel(rows_of, data_ref, links_ref, out_ref):
+    genes_here = data_ref.shape[0]
+    parts, rows, padded = out_ref.shape
+    tile_cells = parts * rows_of
+    joined = max(1, 16 // rows_of)
+    span, share = joined * tile_cells, joined * rows_of
+    to = lax.broadcasted_iota(jnp.int32, (span, span), 0)
+    at = lax.broadcasted_iota(jnp.int32, (span, span), 1)
+    source = (to % share // rows_of) * tile_cells + to // share * rows_of + to % rows_of
+    order = (source == at).astype(jnp.bfloat16)
+    whole = padded - LANES
+
+    def moved(part):
+        taken = lax.dot_general(
+            order, part, (((1,), (1,)), ((), ())), preferred_element_type=jnp.float32
+        )
+        return taken.astype(jnp.bfloat16).reshape(parts, share, part.shape[0])
+
+    for turn in range(rows // share):
+        cells = slice(turn * span, (turn + 1) * span)
+        keep = slice(turn * share, (turn + 1) * share)
+        out_ref[:, keep, :whole] = moved(data_ref[:whole, cells])
+        rest = data_ref[whole:genes_here, cells].astype(jnp.float32)
+        rest = jnp.concatenate([rest, links_ref[:, cells]], axis=0)
+        out_ref[:, keep, whole:] = moved(rest.astype(jnp.bfloat16))
+
+
+def share_second(second, out_ref, chunk, groups):
+    width, cells = second.shape
+    rows = cells * groups // out_ref.shape[0]
+    tall = out_ref.shape[1] - chunk
+    slabs = width // groups // tall
+    lane = lax.broadcasted_iota(jnp.int32, (tall, LANES), 1)
+    for at in range(cells // LANES):
+        wide = second[:, at * LANES : (at + 1) * LANES].astype(jnp.float32)
+        for group in range(groups):
+            for device in range(LANES // rows):
+                share = jnp.zeros((tall, LANES), jnp.float32)
+                for slab in range(slabs):
+                    first_row = (group * slabs + slab) * tall
+                    turned = pltpu.roll(
+                        wide[first_row : first_row + tall],
+                        (slab - device) * rows % LANES,
+                        1,
+                    )
+                    share = jnp.where(lane // rows == slab, turned, share)
+                to = (at * (LANES // rows) + device) * groups + group
+                out_ref[to, chunk:] = share.astype(jnp.bfloat16)
+
+
 def first_kernel(
-    genes_here, slots, neighbours, own_ref, data_ref, start_ref, out_ref, links_ref, degree_ref
+    genes_here, slots, own_ref, data_ref, start_ref, out_ref, links_ref, degree_ref
 ):
     devices, groups, rows, padded = data_ref.shape
     tiles = devices * slots
-    packed = data_ref[:, 0][:, : slots * neighbours, padded - LANES :].astype(jnp.float32)
-    packed = packed.reshape(tiles * neighbours, LANES)
+    packed = block(data_ref, 0)[:, padded - LANES :].astype(jnp.float32)
     offset = genes_here - (padded - LANES)
     links, degree = link_matrix(
-        packed[:, offset : offset + 3], tiles, neighbours, slots, rows // slots
+        packed[:, offset : offset + 3], tiles, rows // slots, slots, rows // slots
     )
     links_ref[...] = links
     degree_ref[...] = degree
@@ -147,12 +195,12 @@
         )
         scores = part if scores is None else scores + part
     scores = scores / math.sqrt(genes_here * groups)
-    push_update(genes_here, data_ref, diffuse(scores, links, degree[:1]), out_ref)
-
-
-def next_kernel(
-    genes_here, chunks_ref, data_ref, links_ref, degree_ref, out_ref, second_ref, update_ref
-):
+    second = diffuse(scores, links, degree[:1])
+    push_update(genes_here, data_ref, second, out_ref, out_ref.shape[1])
+
+
+def next_kernel(genes_here, chunks_ref, data_ref, links_ref, degree_ref, out_ref, update_ref):
+    chunk = chunks_ref.shape[1]
     groups = data_ref.shape[1]
     genes_total = genes_here * groups
     pull_update(chunks_ref, update_ref)
@@ -170,8 +218,9 @@
         inverse, scores, precision=HIGHEST, preferred_element_type=jnp.float32
     ) / math.sqrt(genes_total)
     second = diffuse(scores, links_ref[...], degree_ref[:1])
-    second_ref[...] = second
-    push_update(genes_here, data_ref, second, out_ref)
+    push_update(genes_here, data_ref, second, out_ref, chunk)
+    if out_ref.shape[1] > chunk:
+        share_second(second, out_ref, chunk, groups)
 
 
 def last_kernel(genes_here, own_ref, chunks_ref, out_ref, update_ref):
@@ -180,11 +229,12 @@
     inverse = inverse_factor(gram_of(update_ref, genes_total))
     mine = update_ref[own_ref[0]].astype(jnp.float32)
     loadings = jnp.dot(inverse, mine, precision=HIGHEST, preferred_element_type=jnp.float32)
-    out_ref[...] = loadings.T[:genes_here]
+    out_ref[...] = loadings[:, :genes_here]
 
 
 def sum_kernel(chunks_ref, out_ref):
-    total = jnp.sum(chunks_ref[...].astype(jnp.float32), axis=0).astype(jnp.bfloat16)
+    parts = chunks_ref[:, : out_ref.shape[1]].astype(jnp.float32)
+    total = jnp.sum(parts, axis=0).astype(jnp.bfloat16)
     out_ref[...] = jnp.broadcast_to(total[None], out_ref.shape)
 
 
@@ -215,14 +265,15 @@
     chunk = groups * width * padded // (parts * LANES)
     own = lax.axis_index("genes").astype(jnp.int32).reshape(1)
 
-    packed = jnp.stack([link_dev, link_slot, link_weight], axis=-1).astype(jnp.bfloat16)
-    packed = packed.reshape(slots * neighbours, 3)
-    packed = jnp.pad(packed, ((0, rows - slots * neighbours), (0, padded - genes_here - 3)))
-    moved = data.reshape(slots, parts, rows_of, genes_here).transpose(1, 0, 2, 3)
-    moved = moved.reshape(parts, rows, genes_here)
-    moved = jnp.concatenate(
-        [moved, jnp.broadcast_to(packed[None], (parts, rows, padded - genes_here))], axis=2
-    )
+    links = jnp.stack([link_dev, link_slot, link_weight]).astype(jnp.float32)
+    links = jnp.pad(links, ((0, padded - genes_here - 3), (0, 0), (0, rows_of - neighbours)))
+    links = jnp.broadcast_to(links[:, :, None], (links.shape[0], slots, parts, rows_of))
+    links = links.reshape(links.shape[0], slots * tile_cells)
+    moved = call(
+        functools.partial(regroup_kernel, rows_of),
+        jax.ShapeDtypeStruct((parts, rows, padded), jnp.bfloat16),
+        arrays=2,
+    )(data.T, links)
     moved = lax.all_to_all(moved, axes, 0, 0, tiled=True).reshape(devices, groups, rows, padded)
     narrow = jnp.pad(start.astype(jnp.bfloat16).T, ((0, 0), (0, padded - genes_here)))
     starts = [narrow]
@@ -235,39 +286,40 @@
     update = pltpu.VMEM((groups, width, padded), jnp.bfloat16)
     links = jax.ShapeDtypeStruct((cells, cells), jnp.bfloat16)
     degree = jax.ShapeDtypeStruct((8, cells), jnp.float32)
-    second = jax.ShapeDtypeStruct((width, cells), jnp.bfloat16)
-
-    def everywhere(pushed):
-        summed = call(sum_kernel, chunks, arrays=1)(
-            lax.all_to_all(pushed, axes, 0, 0, tiled=True)
-        )
+    extra = jax.ShapeDtypeStruct((parts, chunk + 16, LANES), jnp.bfloat16)
+
+    def gather(arrived):
+        summed = call(sum_kernel, chunks, arrays=1)(arrived)
         return lax.all_to_all(summed, axes, 0, 0, tiled=True)
 
     pushed, links, degree = call(
-        functools.partial(first_kernel, genes_here, slots, neighbours),
+        functools.partial(first_kernel, genes_here, slots),
         (chunks, links, degree),
         scalars=1,
         arrays=2,
     )(own, moved, starts)
+    arrived = lax.all_to_all(pushed, axes, 0, 0, tiled=True)
     for step in range(1, ITERS):
-        pushed, diffused = call(
-            functools.partial(next_kernel, genes_here), (chunks, second), (update,), arrays=4
-        )(everywhere(pushed), moved, links, degree)
+        pushed = call(
+            functools.partial(next_kernel, genes_here),
+            extra if step == ITERS - 1 else chunks,
+            (update,),
+            arrays=4,
+        )(gather(arrived), moved, links, degree)
+        arrived = lax.all_to_all(pushed, axes, 0, 0, tiled=True)
     loadings = call(
         functools.partial(last_kernel, genes_here),
-        jax.ShapeDtypeStruct((genes_here, width), jnp.float32),
+        jax.ShapeDtypeStruct((width, genes_here), jnp.float32),
         (update,),
         scalars=1,
         arrays=1,
-    )(own, everywhere(pushed))
+    )(own, gather(arrived))
 
     part_width = width // groups
-    smoothed = diffused.reshape(groups, part_width, devices, rows).transpose(2, 0, 1, 3)
-    smoothed = lax.all_to_all(
-        smoothed.reshape(parts, part_width, rows), axes, 0, 0, tiled=True
-    )
-    smoothed = smoothed.reshape(parts, part_width, slots, rows_of).transpose(1, 2, 0, 3)
-    return loadings, smoothed.reshape(part_width, slots * tile_cells)
+    slabs = part_width // 16
+    smoothed = arrived[:, chunk:, : slabs * rows].reshape(parts, 16, slabs, slots, rows_of)
+    smoothed = smoothed.transpose(2, 1, 3, 0, 4)
+    return loadings.T, smoothed.reshape(part_width, slots * tile_cells)
 
 
 def by_tile(data, start, link_dev, link_slot, link_weight):
@@ -382,7 +434,8 @@
 
 
 def per_device(data, start, link_dev, link_slot, link_weight):
-    parts = lax.axis_size("cells") * lax.axis_size("genes")
+    groups = lax.axis_size("genes")
+    parts = lax.axis_size("cells") * groups
     slots, neighbours = link_dev.shape
     tile_cells = data.shape[0] // slots
     genes_here, width = data.shape[1], start.shape[1]
@@ -390,11 +443,14 @@
     rows = slots * tile_cells // parts
     fits = (
         tile_cells % (8 * parts) == 0
+        and neighbours <= tile_cells // parts
         and rows % 16 == 0
-        and rows >= slots * neighbours
-        and slots * neighbours % 16 == 0
+        and LANES % rows == 0
+        and (genes_here - padded + LANES) % 8 == 0
         and padded - genes_here >= 3
-        and width * padded * lax.axis_size("genes") % (parts * LANES * 16) == 0
+        and width % (16 * groups) == 0
+        and width // groups // 16 * rows <= LANES
+        and width * padded * groups % (parts * LANES * 16) == 0
     )
     way = by_cell if fits else by_tile
     return way(data, start, link_dev, link_slot, link_weight)

time: 178 us -> 167 us (0.938)
  waiting for transfers between devices: 72.8 us -> 55.7 us
  blocking collectives: 52.6 us -> 67.4 us
  starting transfers between devices: 16.9 us -> 12.2 us
  local copies, waits for them, and re-layouts: 9.42 us -> 5.11 us
    all_to_all x3 -> x1, waiting for transfers between devices: 25.9 us -> 8.81 us  [gather(): return lax.all_to_all(summed, axes, 0, 0, tiled=True)]
    all_to_all x4 -> x5, blocking collectives: 52.6 us -> 67.4 us  [the longest x3 41.8 us: by_cell(): arrived = lax.all_to_all(pushed, axes, 0, 0, tiled=True)]
    all_to_all x3 -> x1, starting transfers between devices: 7.74 us -> 3.06 us  [gather(): return lax.all_to_all(summed, axes, 0, 0, tiled=True)]
    unnamed x14 -> x8, local copies, waits for them, and re-layouts: 6.76 us -> 3.78 us
    pallas_call x7 -> x8, Pallas kernels: 23.8 us -> 25.1 us  [the longest x2 13.6 us: by_cell(): call(functools.partial(next_kernel, genes_here), extra if step == ITERS -...]
  transfers between devices with their start and end apart: 5 -> 3, of which waited for: 5 -> 3; matrix products, arithmetic and copies ran while one was open for 1% -> 1% of each run, Pallas kernels for 0% -> 0%
where the time goes in v2:
time: 167 us
  blocking collectives  67.4 us (40%)
  waiting for transfers between devices  55.7 us (33%)
  Pallas kernels  25.1 us (15%)
  starting transfers between devices  12.2 us (7%)
  local copies, waits for them, and re-layouts  5.11 us (3%)
    all_to_all x3, blocking collectives, by_cell(): arrived = lax.all_to_all(pushed, axes, 0, 0, tiled=True)  41.8 us
    all_to_all x1, waiting for transfers between devices, by_cell(): lax.all_to_all(moved, axes, 0, 0, tiled=True)  27.6 us
    all_to_all x2, blocking collectives, gather(): return lax.all_to_all(summed, axes, 0, 0, tiled=True)  25.6 us
    ppermute x1, waiting for transfers between devices, by_cell(): starts.append(lax.ppermute(narrow, 'genes', pairs))  19.2 us
    pallas_call x2, Pallas kernels, by_cell(): call(functools.partial(next_kernel, genes_here), extra if step == ITERS -...  13.6 us
    all_to_all x1, waiting for transfers between devices, gather(): return lax.all_to_all(summed, axes, 0, 0, tiled=True)  8.81 us
    all_to_all x1, starting transfers between devices, by_cell(): lax.all_to_all(moved, axes, 0, 0, tiled=True)  7.3 us
    pallas_call x1, Pallas kernels, by_cell(): call(functools.partial(last_kernel, genes_here), jax.ShapeDtypeStruct((wi...  6.83 us
  transfers between devices with their start and end apart: 3, of which 3 were waited for; matrix products, arithmetic and copies ran while one was open for 1% of the time, Pallas kernels for 0%

profile of v2, /device:TPU:0, one launch (start us, length us, event | category | flops | bytes accessed | tf_op | source)
XLA Modules:
  0.0 167.0 jit_solution(9906298787451043641)
XLA Ops:
  0.6 0.7 add_convert_fusion
  1.4 0.1 copy.13
  1.5 0.2 copy.9.links_ref
  1.7 0.0 copy-start.1
  1.7 1.6 copy-done.1
  3.3 1.6 shard_map.68
  4.8 0.0 copy-start
  4.9 1.3 copy-done
  6.2 0.0 copy-start.2
  6.2 7.3 %all-to-all-start = ((bf16[32,32,1024]{2,1,0:T(8,128)(2,1)}), bf16[32,32,1024]{2,1,0:T(8,128)(2,1)S(1)}, u32[]{:S(2)}, u32[]{:S(2)}) async-start(bf16[32,32,1024]{2,1,0:T(8,128)(2,1)} %copy-done), calls=%async_computation | async-start | bytes 4194304 | tf_op jit(solution)/shard_map/all_to_all | solution.py:277
  13.5 0.0 copy-done.2
  13.6 1.8 %collective-permute-start = (bf16[64,1024]{1,0:T(8,128)(2,1)S(1)}, bf16[64,1024]{1,0:T(8,128)(2,1)S(1)}, u32[]{:S(2)}, u32[]{:S(2)}) collective-permute-start(bf16[64,1024]{1,0:T(8,128)(2,1)S(1)} %get-tuple-element.11), channel_id=1, source_target_pairs={{0,1},{1,0},{2,3},{3,2},{4,5},{5,4},{6,7},{7,6},{8,9},{9,8},{10,11... | collective-permute-start | bytes 393224 | tf_op jit(solution)/shard_map/ppermute | solution.py:282
  15.4 19.2 %collective-permute-done = bf16[64,1024]{1,0:T(8,128)(2,1)S(1)} collective-permute-done((bf16[64,1024]{1,0:T(8,128)(2,1)S(1)}, bf16[64,1024]{1,0:T(8,128)(2,1)S(1)}, u32[]{:S(2)}, u32[]{:S(2)}) %collective-permute-start) | collective-permute-done | bytes 131104 | tf_op jit(solution)/shard_map/ppermute | solution.py:282
  34.6 27.6 %all-to-all-done = bf16[32,32,1024]{2,1,0:T(8,128)(2,1)S(1)} async-done(((bf16[32,32,1024]{2,1,0:T(8,128)(2,1)}), bf16[32,32,1024]{2,1,0:T(8,128)(2,1)S(1)}, u32[]{:S(2)}, u32[]{:S(2)}) %all-to-all-start) | async-done | bytes 2097184 | tf_op jit(solution)/shard_map/all_to_all | solution.py:277
  62.3 2.2 %shard_map.69 = (bf16[32,32,128]{2,1,0:T(8,128)(2,1)S(1)}, bf16[512,512]{1,0:T(8,128)(2,1)S(1)}, f32[8,512]{1,0:T(8,128)S(1)}) custom-call(s32[1]{0:T(128)} %bitcast.own_ref, bf16[16,2,32,1024]{3,2,1,0:T(8,128)(2,1)S(1)} %bitcast.18, bf16[2,64,1024]{2,1,0:T(8,128)(2,1)S(1)} %pad_maximum_fusion.start_ref), custom_call_target="tpu_custom_call" | custom-call | tf_op jit(solution)/shard_map/pallas_call | solution.py:295
  64.5 14.1 %all_to_all.35.chunks_ref = bf16[32,32,128]{2,1,0:T(8,128)(2,1)S(1)} all-to-all(bf16[32,32,128]{2,1,0:T(8,128)(2,1)S(1)} %get-tuple-element.5), channel_id=1, replica_groups=mesh['cells'=16,'genes'=2] {'cells','genes'}, dimensions={0} | all-to-all | bytes 524288 | tf_op jit(solution)/shard_map/all_to_all | solution.py:301
  78.6 0.1 shard_map.70
  78.7 12.8 %all_to_all.36.chunks_ref = bf16[32,32,128]{2,1,0:T(8,128)(2,1)S(1)} all-to-all(bf16[32,32,128]{2,1,0:T(8,128)(2,1)S(1)} %shard_map.70), channel_id=1, replica_groups=mesh['cells'=16,'genes'=2] {'cells','genes'}, dimensions={0} | all-to-all | bytes 524288 | tf_op jit(solution)/shard_map/all_to_all | solution.py:293
  91.5 6.8 %shard_map.71 = bf16[32,32,128]{2,1,0:T(8,128)(2,1)S(1)} custom-call(bf16[32,32,128]{2,1,0:T(8,128)(2,1)S(1)} %all_to_all.36.chunks_ref, bf16[16,2,32,1024]{3,2,1,0:T(8,128)(2,1)S(1)} %bitcast.19, bf16[512,512]{1,0:T(8,128)(2,1)S(1)} %get-tuple-element.6.links_ref, f32[8,512]{1,0:T(8,128)S(1)} %get-tuple-element.7.degree_ref), custom_call_target="tpu_custom_call" | custom-call | tf_op jit(solution)/shard_map/pallas_call | solution.py:303
  98.3 12.8 %all_to_all.37.chunks_ref = bf16[32,32,128]{2,1,0:T(8,128)(2,1)S(1)} all-to-all(bf16[32,32,128]{2,1,0:T(8,128)(2,1)S(1)} %shard_map.71), channel_id=1, replica_groups=mesh['cells'=16,'genes'=2] {'cells','genes'}, dimensions={0} | all-to-all | bytes 524288 | tf_op jit(solution)/shard_map/all_to_all | solution.py:309
  111.1 0.1 shard_map.72
  111.2 12.8 %all_to_all.38.chunks_ref = bf16[32,32,128]{2,1,0:T(8,128)(2,1)S(1)} all-to-all(bf16[32,32,128]{2,1,0:T(8,128)(2,1)S(1)} %shard_map.72), channel_id=1, replica_groups=mesh['cells'=16,'genes'=2] {'cells','genes'}, dimensions={0} | all-to-all | bytes 524288 | tf_op jit(solution)/shard_map/all_to_all | solution.py:293
  124.0 6.8 %shard_map.73 = bf16[32,48,128]{2,1,0:T(8,128)(2,1)S(1)} custom-call(bf16[32,32,128]{2,1,0:T(8,128)(2,1)S(1)} %all_to_all.38.chunks_ref, bf16[16,2,32,1024]{3,2,1,0:T(8,128)(2,1)S(1)} %bitcast.20, bf16[512,512]{1,0:T(8,128)(2,1)S(1)} %get-tuple-element.6.links_ref, f32[8,512]{1,0:T(8,128)S(1)} %get-tuple-element.7.degree_ref), custom_call_target="tpu_custom_call" | custom-call | tf_op jit(solution)/shard_map/pallas_call | solution.py:303
  130.8 14.9 %all_to_all.39.chunks_ref = bf16[32,48,128]{2,1,0:T(8,128)(2,1)S(1)} all-to-all(bf16[32,48,128]{2,1,0:T(8,128)(2,1)S(1)} %shard_map.73), channel_id=1, replica_groups=mesh['cells'=16,'genes'=2] {'cells','genes'}, dimensions={0} | all-to-all | bytes 786432 | tf_op jit(solution)/shard_map/all_to_all | solution.py:309
  145.6 0.8 shard_map.74
  146.4 3.1 %all-to-all-start.6 = ((bf16[32,32,128]{2,1,0:T(8,128)(2,1)}), bf16[32,32,128]{2,1,0:T(8,128)(2,1)S(1)}, u32[]{:S(2)}, u32[]{:S(2)}) async-start(bf16[32,32,128]{2,1,0:T(8,128)(2,1)} %shard_map.74), calls=%async_computation.6 | async-start | bytes 524288 | tf_op jit(solution)/shard_map/all_to_all | solution.py:293
  149.5 0.2 copy.10
  149.7 0.6 copy.11
  150.3 0.2 reshape.24
  150.6 0.8 copy.12
  151.3 8.8 %all-to-all-done.6.chunks_ref = bf16[32,32,128]{2,1,0:T(8,128)(2,1)S(1)} async-done(((bf16[32,32,128]{2,1,0:T(8,128)(2,1)}), bf16[32,32,128]{2,1,0:T(8,128)(2,1)S(1)}, u32[]{:S(2)}, u32[]{:S(2)}) %all-to-all-start.6) | async-done | bytes 262176 | tf_op jit(solution)/shard_map/all_to_all | solution.py:293
  160.1 6.8 %shard_map.75 = f32[64,1000]{1,0:T(8,128)} custom-call(s32[1]{0:T(128)} %bitcast.own_ref, bf16[32,32,128]{2,1,0:T(8,128)(2,1)S(1)} %all-to-all-done.6.chunks_ref), custom_call_target="tpu_custom_call" | custom-call | tf_op jit(solution)/shard_map/pallas_call | solution.py:310
  (6 shorter events, 0.1 us)
Async XLA Ops:
  1.7 1.6 copy-start.1
  4.8 1.3 copy-start
  6.2 7.3 %copy-start.2 = (f32[1000,64]{0,1:T(8,128)S(1)}, f32[1000,64]{0,1:T(8,128)}, u32[]{:S(2)}) copy-start(f32[1000,64]{0,1:T(8,128)} %param.6) | copy-start | bytes 768004
  6.2 56.1 %all-to-all-start = ((bf16[32,32,1024]{2,1,0:T(8,128)(2,1)}), bf16[32,32,1024]{2,1,0:T(8,128)(2,1)S(1)}, u32[]{:S(2)}, u32[]{:S(2)}) async-start(bf16[32,32,1024]{2,1,0:T(8,128)(2,1)} %copy-done), calls=%async_computation | async-start | bytes 4194304 | tf_op jit(solution)/shard_map/all_to_all | solution.py:277
  13.6 21.0 %collective-permute-start = (bf16[64,1024]{1,0:T(8,128)(2,1)S(1)}, bf16[64,1024]{1,0:T(8,128)(2,1)S(1)}, u32[]{:S(2)}, u32[]{:S(2)}) collective-permute-start(bf16[64,1024]{1,0:T(8,128)(2,1)S(1)} %get-tuple-element.11), channel_id=1, source_target_pairs={{0,1},{1,0},{2,3},{3,2},{4,5},{5,4},{6,7},{7,6},{8,9},{9,8},{10,11... | collective-permute-start | bytes 393224 | tf_op jit(solution)/shard_map/ppermute | solution.py:282
  146.4 13.8 %all-to-all-start.6 = ((bf16[32,32,128]{2,1,0:T(8,128)(2,1)}), bf16[32,32,128]{2,1,0:T(8,128)(2,1)S(1)}, u32[]{:S(2)}, u32[]{:S(2)}) async-start(bf16[32,32,128]{2,1,0:T(8,128)(2,1)} %shard_map.74), calls=%async_computation.6 | async-start | bytes 524288 | tf_op jit(solution)/shard_map/all_to_all | solution.py:293

commit v3 on v2

--- a/solution.py
+++ b/solution.py
@@ -19,22 +19,59 @@
     width = gram.shape[0]
     rows = lax.broadcasted_iota(jnp.int32, (width, width), 0)
     cols = lax.broadcasted_iota(jnp.int32, (width, width), 1)
-    eye = (rows == cols).astype(jnp.float32)
-    state = jnp.concatenate([eye, gram], axis=1)
+    diagonal = jnp.where(rows == cols, gram, 0.0)
+    down = lax.rsqrt(jnp.sum(diagonal, axis=1, keepdims=True))
+    along = lax.rsqrt(jnp.sum(diagonal, axis=0, keepdims=True))
+    scaled = gram * down * along
+    state = jnp.concatenate([jnp.where(rows == cols, along, 0.0), scaled], axis=1)
     strips = [state[at : at + 8] for at in range(0, width, 8)]
-    place = lax.broadcasted_iota(jnp.int32, (8, 2 * width), 0)
-    for k in range(width - 1):
-        own, within = divmod(k, 8)
-        row = strips[own][within : within + 1]
-        scaled = row / row[:, width + k : width + k + 1]
-        for strip in range(own, width // 8):
-            factor = strips[strip][:, width + k : width + k + 1]
-            if strip == own:
-                factor = jnp.where(place > within, factor, 0.0)
-            strips[strip] = strips[strip] - factor * scaled
-    state = jnp.concatenate(strips, axis=0)
-    pivots = jnp.sum(eye * state[:, width:], axis=1, keepdims=True)
-    return state[:, :width] * lax.rsqrt(pivots)
+    shape = strips[0].shape
+    place = lax.broadcasted_iota(jnp.int32, shape, 0)
+    done = []
+    for panel, strip in enumerate(strips):
+        base = width + 8 * panel
+
+        def column(of, j):
+            return jnp.broadcast_to(of[:, base + j : base + j + 1], shape)
+
+        columns = [column(strip, j) for j in range(8)]
+        core = {
+            (i, j): jnp.broadcast_to(columns[j][i : i + 1], shape)
+            for j in range(8)
+            for i in range(j, 8)
+        }
+        lines = [jnp.broadcast_to(strip[j : j + 1], shape) for j in range(8)]
+        factor, solved = {}, [None] * 8
+        for j in range(0, 8, 2):
+            a, b, c = core[j, j], core[j + 1, j], core[j + 1, j + 1]
+            inverse = 1.0 / (a * c - b * b)
+            step = b * (1.0 / a)
+            ia, ib, ic = c * inverse, b * inverse, a * inverse
+            for i in range(j + 2, 8):
+                factor[i, j] = core[i, j] * ia - core[i, j + 1] * ib
+                factor[i, j + 1] = core[i, j + 1] * ic - core[i, j] * ib
+            for i in range(j + 2, 8):
+                for m in range(j + 2, i + 1):
+                    core[i, m] -= factor[i, j] * core[m, j] + factor[i, j + 1] * core[m, j + 1]
+                lines[i] -= factor[i, j] * lines[j] + factor[i, j + 1] * lines[j + 1]
+            solved[j] = ia * lines[j] - ib * lines[j + 1]
+            solved[j + 1] = ic * lines[j + 1] - ib * lines[j]
+            lines[j + 1] -= step * lines[j]
+            core[j + 1, j + 1] = c - step * b
+        for j in reversed(range(0, 8, 2)):
+            for i in range(j + 2, 8):
+                solved[j] -= factor[i, j] * solved[i]
+                solved[j + 1] -= factor[i, j + 1] * solved[i]
+        for later in range(panel + 1, len(strips)):
+            terms = [column(strips[later], j) * solved[j] for j in range(8)]
+            while len(terms) > 1:
+                terms = [terms[at] + terms[at + 1] for at in range(0, len(terms), 2)]
+            strips[later] = strips[later] - terms[0]
+        final = lines[0] * lax.rsqrt(core[0, 0])
+        for j in range(1, 8):
+            final = jnp.where(place == j, lines[j] * lax.rsqrt(core[j, j]), final)
+        done.append(final)
+    return jnp.concatenate(done, axis=0)[:, :width]
 
 
 def link_matrix(packed, tiles, neighbours, slots, rows_of):
@@ -122,31 +159,41 @@
     return gram / genes_total
 
 
-def regroup_kernel(rows_of, data_ref, links_ref, out_ref):
-    genes_here = data_ref.shape[0]
-    parts, rows, padded = out_ref.shape
+def regroup_kernel(rows_of, genes_here, data_ref, links_ref, out_ref, order_ref):
+    parts, rows, genes = out_ref.shape
     tile_cells = parts * rows_of
-    joined = max(1, 16 // rows_of)
-    span, share = joined * tile_cells, joined * rows_of
-    to = lax.broadcasted_iota(jnp.int32, (span, span), 0)
-    at = lax.broadcasted_iota(jnp.int32, (span, span), 1)
-    source = (to % share // rows_of) * tile_cells + to // share * rows_of + to % rows_of
-    order = (source == at).astype(jnp.bfloat16)
-    whole = padded - LANES
-
-    def moved(part):
-        taken = lax.dot_general(
-            order, part, (((1,), (1,)), ((), ())), preferred_element_type=jnp.float32
-        )
-        return taken.astype(jnp.bfloat16).reshape(parts, share, part.shape[0])
-
-    for turn in range(rows // share):
-        cells = slice(turn * span, (turn + 1) * span)
-        keep = slice(turn * share, (turn + 1) * share)
-        out_ref[:, keep, :whole] = moved(data_ref[:whole, cells])
-        rest = data_ref[whole:genes_here, cells].astype(jnp.float32)
-        rest = jnp.concatenate([rest, links_ref[:, cells]], axis=0)
-        out_ref[:, keep, whole:] = moved(rest.astype(jnp.bfloat16))
+    span = order_ref.shape[0]
+    share = span // parts
+    last = pl.num_programs(0) - 1
+    here = genes_here % genes
+
+    @pl.when(pl.program_id(0) == 0)
+    def _():
+        to = lax.broadcasted_iota(jnp.int32, (span, span), 0)
+        at = lax.broadcasted_iota(jnp.int32, (span, span), 1)
+        source = (to % share // rows_of) * tile_cells + to // share * rows_of + to % rows_of
+        order_ref[...] = (source == at).astype(jnp.bfloat16)
+
+    def move(data):
+        for turn in range(rows // share):
+            taken = lax.dot_general(
+                order_ref[...],
+                data[:, turn * span : (turn + 1) * span],
+                (((1,), (1,)), ((), ())),
+                preferred_element_type=jnp.float32,
+            )
+            out_ref[:, turn * share : (turn + 1) * share] = taken.astype(jnp.bfloat16).reshape(
+                parts, share, genes
+            )
+
+    @pl.when(pl.program_id(0) < last)
+    def _():
+        move(data_ref[...])
+
+    @pl.when(pl.program_id(0) == last)
+    def _():
+        data = data_ref[:here].astype(jnp.float32)
+        move(jnp.concatenate([data, links_ref[...]], axis=0).astype(jnp.bfloat16))
 
 
 def share_second(second, out_ref, chunk, groups):
@@ -260,7 +307,7 @@
     tile_cells = data.shape[0] // slots
     rows_of = tile_cells // parts
     rows = slots * rows_of
-    padded = -(-genes_here // LANES) * LANES
+    padded = -(-genes_here // (2 * LANES)) * 2 * LANES
     cells = devices * rows
     chunk = groups * width * padded // (parts * LANES)
     own = lax.axis_index("genes").astype(jnp.int32).reshape(1)
@@ -269,10 +316,19 @@
     links = jnp.pad(links, ((0, padded - genes_here - 3), (0, 0), (0, rows_of - neighbours)))
     links = jnp.broadcast_to(links[:, :, None], (links.shape[0], slots, parts, rows_of))
     links = links.reshape(links.shape[0], slots * tile_cells)
-    moved = call(
-        functools.partial(regroup_kernel, rows_of),
-        jax.ShapeDtypeStruct((parts, rows, padded), jnp.bfloat16),
-        arrays=2,
+    span = max(1, 16 // rows_of) * tile_cells
+    genes = 2 * LANES
+    moved = pl.pallas_call(
+        functools.partial(regroup_kernel, rows_of, genes_here),
+        grid=(padded // genes,),
+        out_shape=jax.ShapeDtypeStruct((parts, rows, padded), jnp.bfloat16),
+        in_specs=[
+            pl.BlockSpec((genes, slots * tile_cells), lambda at: (at, 0)),
+            pl.BlockSpec(links.shape, lambda at: (0, 0)),
+        ],
+        out_specs=pl.BlockSpec((parts, rows, genes), lambda at: (0, 0, at)),
+        scratch_shapes=[pltpu.VMEM((span, span), jnp.bfloat16)],
+        compiler_params=pltpu.CompilerParams(vmem_limit_bytes=60 * 1024 * 1024),
     )(data.T, links)
     moved = lax.all_to_all(moved, axes, 0, 0, tiled=True).reshape(devices, groups, rows, padded)
     narrow = jnp.pad(start.astype(jnp.bfloat16).T, ((0, 0), (0, padded - genes_here)))
@@ -439,15 +495,15 @@
     slots, neighbours = link_dev.shape
     tile_cells = data.shape[0] // slots
     genes_here, width = data.shape[1], start.shape[1]
-    padded = -(-genes_here // LANES) * LANES
+    padded = -(-genes_here // (2 * LANES)) * 2 * LANES
     rows = slots * tile_cells // parts
     fits = (
         tile_cells % (8 * parts) == 0
         and neighbours <= tile_cells // parts
         and rows % 16 == 0
         and LANES % rows == 0
-        and (genes_here - padded + LANES) % 8 == 0
-        and padded - genes_here >= 3
+        and genes_here % 8 == 0
+        and 3 <= padded - genes_here <= LANES
         and width % (16 * groups) == 0
         and width // groups // 16 * rows <= LANES
         and width * padded * groups % (parts * LANES * 16) == 0

time: 167 us -> 160 us (0.958)
  Pallas kernels: 25.1 us -> 19.6 us
  local copies, waits for them, and re-layouts: 5.11 us -> 2.84 us
    pallas_call x2, Pallas kernels: 13.6 us -> 7.68 us  [by_cell(): call(functools.partial(next_kernel, genes_here), extra if step == ITERS -...]
    pallas_call x1, Pallas kernels: 1.59 us -> 4.96 us  [by_cell(): pl.pallas_call(functools.partial(regroup_kernel, rows_of, genes_here), gr...]
    pallas_call x1, Pallas kernels: 6.83 us -> 3.9 us  [by_cell(): call(functools.partial(last_kernel, genes_here), jax.ShapeDtypeStruct((wi...]
    unnamed x8 -> x4, local copies, waits for them, and re-layouts: 3.78 us -> 0.86 us
where the time goes in v3:
time: 160 us; the launch traced here: 159 us
  blocking collectives  67.4 us (42%)
  waiting for transfers between devices  55.7 us (35%)
  Pallas kernels  19.6 us (12%)
  starting transfers between devices  12.2 us (8%)
  local copies, waits for them, and re-layouts  2.84 us (2%)
    all_to_all x3, blocking collectives, by_cell(): arrived = lax.all_to_all(pushed, axes, 0, 0, tiled=True)  41.8 us
    all_to_all x1, waiting for transfers between devices, by_cell(): lax.all_to_all(moved, axes, 0, 0, tiled=True)  27.6 us
    all_to_all x2, blocking collectives, gather(): return lax.all_to_all(summed, axes, 0, 0, tiled=True)  25.6 us
    ppermute x1, waiting for transfers between devices, by_cell(): starts.append(lax.ppermute(narrow, 'genes', pairs))  19.2 us
    all_to_all x1, waiting for transfers between devices, gather(): return lax.all_to_all(summed, axes, 0, 0, tiled=True)  8.81 us
    pallas_call x2, Pallas kernels, by_cell(): call(functools.partial(next_kernel, genes_here), extra if step == ITERS -...  7.68 us
    all_to_all x1, starting transfers between devices, by_cell(): lax.all_to_all(moved, axes, 0, 0, tiled=True)  7.31 us
    pallas_call x1, Pallas kernels, by_cell(): pl.pallas_call(functools.partial(regroup_kernel, rows_of, genes_here), gr...  4.96 us
  transfers between devices with their start and end apart: 3, of which 3 were waited for; matrix products, arithmetic and copies ran while one was open for 1% of the time, Pallas kernels for 0%

profile of v3, /device:TPU:0, one launch (start us, length us, event | category | flops | bytes accessed | tf_op | source)
XLA Modules:
  0.0 159.3 jit_solution(15372876337702806958)
XLA Ops:
  0.6 0.7 add_convert_fusion
  1.4 0.1 copy.13
  1.5 0.8 copy.9.links_ref
  2.3 5.0 %shard_map.68 = bf16[32,32,1024]{2,1,0:T(8,128)(2,1)} custom-call(bf16[1000,1024]{1,0:T(8,128)(2,1)} %bitcast.22, f32[24,1024]{1,0:T(8,128)} %copy.9.links_ref), custom_call_target="tpu_custom_call" | custom-call | tf_op jit(solution)/shard_map/pallas_call | solution.py:321
  7.3 0.0 copy-start
  7.3 7.3 %all-to-all-start = ((bf16[32,32,1024]{2,1,0:T(8,128)(2,1)}), bf16[32,32,1024]{2,1,0:T(8,128)(2,1)S(1)}, u32[]{:S(2)}, u32[]{:S(2)}) async-start(bf16[32,32,1024]{2,1,0:T(8,128)(2,1)} %shard_map.68), calls=%async_computation | async-start | bytes 4194304 | tf_op jit(solution)/shard_map/all_to_all | solution.py:333
  14.6 0.0 copy-done
  14.7 1.8 %collective-permute-start = (bf16[64,1024]{1,0:T(8,128)(2,1)S(1)}, bf16[64,1024]{1,0:T(8,128)(2,1)S(1)}, u32[]{:S(2)}, u32[]{:S(2)}) collective-permute-start(bf16[64,1024]{1,0:T(8,128)(2,1)S(1)} %get-tuple-element.11), channel_id=1, source_target_pairs={{0,1},{1,0},{2,3},{3,2},{4,5},{5,4},{6,7},{7,6},{8,9},{9,8},{10,11... | collective-permute-start | bytes 393224 | tf_op jit(solution)/shard_map/ppermute | solution.py:338
  16.5 19.2 %collective-permute-done = bf16[64,1024]{1,0:T(8,128)(2,1)S(1)} collective-permute-done((bf16[64,1024]{1,0:T(8,128)(2,1)S(1)}, bf16[64,1024]{1,0:T(8,128)(2,1)S(1)}, u32[]{:S(2)}, u32[]{:S(2)}) %collective-permute-start) | collective-permute-done | bytes 131104 | tf_op jit(solution)/shard_map/ppermute | solution.py:338
  35.7 27.6 %all-to-all-done = bf16[32,32,1024]{2,1,0:T(8,128)(2,1)S(1)} async-done(((bf16[32,32,1024]{2,1,0:T(8,128)(2,1)}), bf16[32,32,1024]{2,1,0:T(8,128)(2,1)S(1)}, u32[]{:S(2)}, u32[]{:S(2)}) %all-to-all-start) | async-done | bytes 2097184 | tf_op jit(solution)/shard_map/all_to_all | solution.py:333
  63.4 2.2 %shard_map.69 = (bf16[32,32,128]{2,1,0:T(8,128)(2,1)S(1)}, bf16[512,512]{1,0:T(8,128)(2,1)S(1)}, f32[8,512]{1,0:T(8,128)S(1)}) custom-call(s32[1]{0:T(128)} %bitcast.own_ref, bf16[16,2,32,1024]{3,2,1,0:T(8,128)(2,1)S(1)} %bitcast.18, bf16[2,64,1024]{2,1,0:T(8,128)(2,1)S(1)} %pad_maximum_fusion.start_ref), custom_call_target="tpu_custom_call" | custom-call | tf_op jit(solution)/shard_map/pallas_call | solution.py:351
  65.6 14.1 %all_to_all.35.chunks_ref = bf16[32,32,128]{2,1,0:T(8,128)(2,1)S(1)} all-to-all(bf16[32,32,128]{2,1,0:T(8,128)(2,1)S(1)} %get-tuple-element.5), channel_id=1, replica_groups=mesh['cells'=16,'genes'=2] {'cells','genes'}, dimensions={0} | all-to-all | bytes 524288 | tf_op jit(solution)/shard_map/all_to_all | solution.py:357
  79.7 0.1 shard_map.70
  79.8 12.8 %all_to_all.36.chunks_ref = bf16[32,32,128]{2,1,0:T(8,128)(2,1)S(1)} all-to-all(bf16[32,32,128]{2,1,0:T(8,128)(2,1)S(1)} %shard_map.70), channel_id=1, replica_groups=mesh['cells'=16,'genes'=2] {'cells','genes'}, dimensions={0} | all-to-all | bytes 524288 | tf_op jit(solution)/shard_map/all_to_all | solution.py:349
  92.6 3.8 %shard_map.71 = bf16[32,32,128]{2,1,0:T(8,128)(2,1)S(1)} custom-call(bf16[32,32,128]{2,1,0:T(8,128)(2,1)S(1)} %all_to_all.36.chunks_ref, bf16[16,2,32,1024]{3,2,1,0:T(8,128)(2,1)S(1)} %bitcast.19, bf16[512,512]{1,0:T(8,128)(2,1)S(1)} %get-tuple-element.6.links_ref, f32[8,512]{1,0:T(8,128)S(1)} %get-tuple-element.7.degree_ref), custom_call_target="tpu_custom_call" | custom-call | tf_op jit(solution)/shard_map/pallas_call | solution.py:359
  96.5 12.8 %all_to_all.37.chunks_ref = bf16[32,32,128]{2,1,0:T(8,128)(2,1)S(1)} all-to-all(bf16[32,32,128]{2,1,0:T(8,128)(2,1)S(1)} %shard_map.71), channel_id=1, replica_groups=mesh['cells'=16,'genes'=2] {'cells','genes'}, dimensions={0} | all-to-all | bytes 524288 | tf_op jit(solution)/shard_map/all_to_all | solution.py:365
  109.3 0.1 shard_map.72
  109.3 12.8 %all_to_all.38.chunks_ref = bf16[32,32,128]{2,1,0:T(8,128)(2,1)S(1)} all-to-all(bf16[32,32,128]{2,1,0:T(8,128)(2,1)S(1)} %shard_map.72), channel_id=1, replica_groups=mesh['cells'=16,'genes'=2] {'cells','genes'}, dimensions={0} | all-to-all | bytes 524288 | tf_op jit(solution)/shard_map/all_to_all | solution.py:349
  122.1 3.8 %shard_map.73 = bf16[32,48,128]{2,1,0:T(8,128)(2,1)S(1)} custom-call(bf16[32,32,128]{2,1,0:T(8,128)(2,1)S(1)} %all_to_all.38.chunks_ref, bf16[16,2,32,1024]{3,2,1,0:T(8,128)(2,1)S(1)} %bitcast.20, bf16[512,512]{1,0:T(8,128)(2,1)S(1)} %get-tuple-element.6.links_ref, f32[8,512]{1,0:T(8,128)S(1)} %get-tuple-element.7.degree_ref), custom_call_target="tpu_custom_call" | custom-call | tf_op jit(solution)/shard_map/pallas_call | solution.py:359
  126.0 14.9 %all_to_all.39.chunks_ref = bf16[32,48,128]{2,1,0:T(8,128)(2,1)S(1)} all-to-all(bf16[32,48,128]{2,1,0:T(8,128)(2,1)S(1)} %shard_map.73), channel_id=1, replica_groups=mesh['cells'=16,'genes'=2] {'cells','genes'}, dimensions={0} | all-to-all | bytes 786432 | tf_op jit(solution)/shard_map/all_to_all | solution.py:365
  140.9 0.8 shard_map.74
  141.6 3.1 %all-to-all-start.6 = ((bf16[32,32,128]{2,1,0:T(8,128)(2,1)}), bf16[32,32,128]{2,1,0:T(8,128)(2,1)S(1)}, u32[]{:S(2)}, u32[]{:S(2)}) async-start(bf16[32,32,128]{2,1,0:T(8,128)(2,1)} %shard_map.74), calls=%async_computation.6 | async-start | bytes 524288 | tf_op jit(solution)/shard_map/all_to_all | solution.py:349
  144.7 0.2 copy.10
  144.9 0.6 copy.11
  145.5 0.2 reshape.24
  145.8 0.8 copy.12
  146.6 8.8 %all-to-all-done.6.chunks_ref = bf16[32,32,128]{2,1,0:T(8,128)(2,1)S(1)} async-done(((bf16[32,32,128]{2,1,0:T(8,128)(2,1)}), bf16[32,32,128]{2,1,0:T(8,128)(2,1)S(1)}, u32[]{:S(2)}, u32[]{:S(2)}) %all-to-all-start.6) | async-done | bytes 262176 | tf_op jit(solution)/shard_map/all_to_all | solution.py:349
  155.4 3.9 %shard_map.75 = f32[64,1000]{1,0:T(8,128)} custom-call(s32[1]{0:T(128)} %bitcast.own_ref, bf16[32,32,128]{2,1,0:T(8,128)(2,1)S(1)} %all-to-all-done.6.chunks_ref), custom_call_target="tpu_custom_call" | custom-call | tf_op jit(solution)/shard_map/pallas_call | solution.py:366
  (6 shorter events, 0.1 us)
Async XLA Ops:
  7.3 7.3 %copy-start = (f32[1000,64]{0,1:T(8,128)S(1)}, f32[1000,64]{0,1:T(8,128)}, u32[]{:S(2)}) copy-start(f32[1000,64]{0,1:T(8,128)} %param.6) | copy-start | bytes 768004
  7.3 56.1 %all-to-all-start = ((bf16[32,32,1024]{2,1,0:T(8,128)(2,1)}), bf16[32,32,1024]{2,1,0:T(8,128)(2,1)S(1)}, u32[]{:S(2)}, u32[]{:S(2)}) async-start(bf16[32,32,1024]{2,1,0:T(8,128)(2,1)} %shard_map.68), calls=%async_computation | async-start | bytes 4194304 | tf_op jit(solution)/shard_map/all_to_all | solution.py:333
  14.7 21.0 %collective-permute-start = (bf16[64,1024]{1,0:T(8,128)(2,1)S(1)}, bf16[64,1024]{1,0:T(8,128)(2,1)S(1)}, u32[]{:S(2)}, u32[]{:S(2)}) collective-permute-start(bf16[64,1024]{1,0:T(8,128)(2,1)S(1)} %get-tuple-element.11), channel_id=1, source_target_pairs={{0,1},{1,0},{2,3},{3,2},{4,5},{5,4},{6,7},{7,6},{8,9},{9,8},{10,11... | collective-permute-start | bytes 393224 | tf_op jit(solution)/shard_map/ppermute | solution.py:338
  141.6 13.8 %all-to-all-start.6 = ((bf16[32,32,128]{2,1,0:T(8,128)(2,1)}), bf16[32,32,128]{2,1,0:T(8,128)(2,1)S(1)}, u32[]{:S(2)}, u32[]{:S(2)}) async-start(bf16[32,32,128]{2,1,0:T(8,128)(2,1)} %shard_map.74), calls=%async_computation.6 | async-start | bytes 524288 | tf_op jit(solution)/shard_map/all_to_all | solution.py:349

commit v4 on v3

--- a/solution.py
+++ b/solution.py
@@ -6,6 +6,7 @@
 from jax import lax
 from jax.experimental import pallas as pl
 from jax.experimental.pallas import tpu as pltpu
+from jax.sharding import Mesh
 from jax.sharding import PartitionSpec as P
 
 ITERS = 3
@@ -120,38 +121,41 @@
     return part.reshape(part.shape[0] * part.shape[1], part.shape[2])
 
 
-def push_update(genes_here, data_ref, second, out_ref, chunk):
+def push_update(genes_here, data_ref, second, cut_ref):
     groups, padded = data_ref.shape[1], data_ref.shape[3]
-    halves = second.shape[0] // chunk
+    cores = cut_ref.shape[0]
+    chunk = second.shape[0] // cores
     blocks = padded // LANES
     for group in range(groups):
         update = jnp.dot(second, block(data_ref, group), preferred_element_type=jnp.float32)
         lane = lax.broadcasted_iota(jnp.int32, update.shape, 1)
         update = jnp.where(lane < genes_here, update, 0.0).astype(jnp.bfloat16)
         for at in range(blocks):
-            for half in range(halves):
-                out_ref[(group * blocks + at) * halves + half, :chunk] = update[
-                    half * chunk : (half + 1) * chunk, at * LANES : (at + 1) * LANES
+            for core in range(cores):
+                cut_ref[core, group * blocks + at, :chunk] = update[
+                    core * chunk : (core + 1) * chunk, at * LANES : (at + 1) * LANES
                 ]
 
 
-def pull_update(chunks_ref, update_ref):
-    groups, width, padded = update_ref.shape
-    chunk = chunks_ref.shape[1]
-    halves = width // chunk
+def pull_update(core, mine_ref, other_ref, update_ref):
+    groups, _, _, padded = update_ref.shape
     blocks = padded // LANES
     for group in range(groups):
         for at in range(blocks):
-            for half in range(halves):
-                update_ref[
-                    group, half * chunk : (half + 1) * chunk, at * LANES : (at + 1) * LANES
-                ] = chunks_ref[(group * blocks + at) * halves + half]
+            lanes = slice(at * LANES, (at + 1) * LANES)
+            update_ref[group, core, :, lanes] = mine_ref[group * blocks + at]
+            update_ref[group, 1 - core, :, lanes] = other_ref[group * blocks + at]
+
+
+def columns_of(update_ref, group):
+    update = update_ref[group]
+    return update.reshape(update.shape[0] * update.shape[1], update.shape[2])
 
 
 def gram_of(update_ref, genes_total):
     gram = None
     for group in range(update_ref.shape[0]):
-        update = update_ref[group]
+        update = columns_of(update_ref, group)
         part = lax.dot_general(
             update, update, (((1,), (1,)), ((), ())), preferred_element_type=jnp.float32
         )
@@ -159,49 +163,76 @@
     return gram / genes_total
 
 
-def regroup_kernel(rows_of, genes_here, data_ref, links_ref, out_ref, order_ref):
-    parts, rows, genes = out_ref.shape
-    tile_cells = parts * rows_of
-    span = order_ref.shape[0]
-    share = span // parts
-    last = pl.num_programs(0) - 1
-    here = genes_here % genes
-
-    @pl.when(pl.program_id(0) == 0)
-    def _():
-        to = lax.broadcasted_iota(jnp.int32, (span, span), 0)
-        at = lax.broadcasted_iota(jnp.int32, (span, span), 1)
-        source = (to % share // rows_of) * tile_cells + to // share * rows_of + to % rows_of
-        order_ref[...] = (source == at).astype(jnp.bfloat16)
-
-    def move(data):
-        for turn in range(rows // share):
-            taken = lax.dot_general(
-                order_ref[...],
-                data[:, turn * span : (turn + 1) * span],
-                (((1,), (1,)), ((), ())),
-                preferred_element_type=jnp.float32,
+def regroup_kernel(
+    rows_of, data_any, dev_any, slot_any, weight_any, out_ref, data_ref, link_ref, data_sem, link_sem
+):
+    genes_here, cells = data_ref.shape
+    parts, rows, padded = out_ref.shape
+    slots, neighbours = link_ref.shape[1:]
+    tile_cells = cells // slots
+    share = max(16, rows_of)
+    span = share * parts
+    turns = rows // share
+    link_copies = [
+        pltpu.make_async_copy(source, link_ref.at[at], link_sem.at[at])
+        for at, source in enumerate((dev_any, slot_any, weight_any))
+    ]
+    for copy in link_copies:
+        copy.start()
+    data_copies = []
+    for turn in range(turns):
+        part = pl.ds(turn * span, span)
+        data_copies.append(
+            pltpu.make_async_copy(
+                data_any.at[:, part], data_ref.at[:, part], data_sem.at[turn]
             )
-            out_ref[:, turn * share : (turn + 1) * share] = taken.astype(jnp.bfloat16).reshape(
-                parts, share, genes
-            )
-
-    @pl.when(pl.program_id(0) < last)
-    def _():
-        move(data_ref[...])
-
-    @pl.when(pl.program_id(0) == last)
-    def _():
-        data = data_ref[:here].astype(jnp.float32)
-        move(jnp.concatenate([data, links_ref[...]], axis=0).astype(jnp.bfloat16))
-
-
-def share_second(second, out_ref, chunk, groups):
+        )
+        data_copies[turn].start()
+
+    to = lax.broadcasted_iota(jnp.int32, (span, span), 0)
+    at = lax.broadcasted_iota(jnp.int32, (span, span), 1)
+    source = (to % share // rows_of) * tile_cells + to // share * rows_of + to % rows_of
+    order = (source == at).astype(jnp.bfloat16)
+    spread = (
+        lax.broadcasted_iota(jnp.int32, (neighbours, cells), 0)
+        == lax.broadcasted_iota(jnp.int32, (neighbours, cells), 1) % rows_of
+    ).astype(jnp.float32)
+    tile = lax.broadcasted_iota(jnp.int32, (slots, cells), 0)
+    own_tile = tile == lax.broadcasted_iota(jnp.int32, (slots, cells), 1) // tile_cells
+    row = lax.broadcasted_iota(jnp.int32, (padded - genes_here, cells), 0)
+    links = jnp.zeros((padded - genes_here, cells), jnp.float32)
+    for at, copy in enumerate(link_copies):
+        copy.wait()
+        wide = jnp.dot(
+            link_ref[at].astype(jnp.float32), spread, preferred_element_type=jnp.float32
+        )
+        wide = jnp.sum(jnp.where(own_tile, wide, 0.0), axis=0, keepdims=True)
+        links = jnp.where(row == at, wide, links)
+    whole = padded - LANES
+
+    def moved(part):
+        taken = lax.dot_general(
+            order, part, (((1,), (1,)), ((), ())), preferred_element_type=jnp.float32
+        )
+        return taken.astype(jnp.bfloat16).reshape(parts, share, part.shape[0])
+
+    for turn in range(turns):
+        part = slice(turn * span, (turn + 1) * span)
+        keep = slice(turn * share, (turn + 1) * share)
+        data_copies[turn].wait()
+        out_ref[:, keep, :whole] = moved(data_ref[:whole, part])
+        rest = data_ref[whole:genes_here, part].astype(jnp.float32)
+        rest = jnp.concatenate([rest, links[:, part]], axis=0)
+        out_ref[:, keep, whole:] = moved(rest.astype(jnp.bfloat16))
+
+
+def share_second(core, second, cut_ref, chunk, groups):
     width, cells = second.shape
-    rows = cells * groups // out_ref.shape[0]
-    tall = out_ref.shape[1] - chunk
+    cores, blocks, tall = cut_ref.shape[:3]
+    rows = cells * groups // (cores * blocks)
+    tall = tall - chunk
     slabs = width // groups // tall
-    lane = lax.broadcasted_iota(jnp.int32, (tall, LANES), 1)
+    lane = lax.broadcasted_iota(jnp.int32, (tall, LANES), 1) // rows - core * slabs
     for at in range(cells // LANES):
         wide = second[:, at * LANES : (at + 1) * LANES].astype(jnp.float32)
         for group in range(groups):
@@ -209,21 +240,59 @@
                 share = jnp.zeros((tall, LANES), jnp.float32)
                 for slab in range(slabs):
                     first_row = (group * slabs + slab) * tall
-                    turned = pltpu.roll(
-                        wide[first_row : first_row + tall],
-                        (slab - device) * rows % LANES,
-                        1,
-                    )
-                    share = jnp.where(lane // rows == slab, turned, share)
-                to = (at * (LANES // rows) + device) * groups + group
-                out_ref[to, chunk:] = share.astype(jnp.bfloat16)
+                    for turn in range(cores):
+                        turned = pltpu.roll(
+                            wide[first_row : first_row + tall],
+                            (turn * slabs + slab - device) * rows % LANES,
+                            1,
+                        )
+                        share = jnp.where((lane == slab) & (core == turn), turned, share)
+                chip, to = divmod(at * (LANES // rows) + device, cores)
+                cut_ref[to, chip * groups + group, chunk:] = share.astype(jnp.bfloat16)
+
+
+def order_shares(arrived_ref, chunk, out_ref, groups, cores, slots):
+    part_width, cells = out_ref.shape
+    blocks, tall = arrived_ref.shape[:2]
+    tall = tall - chunk
+    parts = blocks * cores
+    rows_of = cells // (slots * parts)
+    rows = slots * rows_of
+    slabs = part_width // tall
+    together = LANES // rows_of
+    lane = lax.broadcasted_iota(jnp.int32, (tall, LANES), 1) // rows_of
+    for slab in range(slabs):
+        for slot in range(slots):
+            for first in range(0, parts, together):
+                whole = jnp.zeros((tall, LANES), jnp.float32)
+                for at in range(together):
+                    chip, rest = divmod(first + at, cores * groups)
+                    core, group = divmod(rest, groups)
+                    source = (core * slabs + slab) * rows + slot * rows_of
+                    share = arrived_ref[chip * groups + group, chunk:].astype(jnp.float32)
+                    turned = pltpu.roll(share, (at * rows_of - source) % LANES, 1)
+                    whole = jnp.where(lane == at, turned, whole)
+                to = (slot * parts + first) * rows_of
+                out_ref[slab * tall : (slab + 1) * tall, to : to + LANES] = whole.astype(
+                    jnp.bfloat16
+                )
 
 
 def first_kernel(
-    genes_here, slots, own_ref, data_ref, start_ref, out_ref, links_ref, degree_ref
+    genes_here,
+    slots,
+    place_ref,
+    data_ref,
+    start_ref,
+    mine_ref,
+    other_ref,
+    links_ref,
+    degree_ref,
+    cut_ref,
 ):
     devices, groups, rows, padded = data_ref.shape
     tiles = devices * slots
+    core, own = place_ref[0], place_ref[1]
     packed = block(data_ref, 0)[:, padded - LANES :].astype(jnp.float32)
     offset = genes_here - (padded - LANES)
     links, degree = link_matrix(
@@ -233,7 +302,7 @@
     degree_ref[...] = degree
     scores = None
     for shift in range(groups):
-        group = lax.rem(own_ref[0] + groups - shift, groups)
+        group = lax.rem(own + groups - shift, groups)
         part = lax.dot_general(
             start_ref[shift],
             block(data_ref, group),
@@ -243,19 +312,34 @@
         scores = part if scores is None else scores + part
     scores = scores / math.sqrt(genes_here * groups)
     second = diffuse(scores, links, degree[:1])
-    push_update(genes_here, data_ref, second, out_ref, out_ref.shape[1])
-
-
-def next_kernel(genes_here, chunks_ref, data_ref, links_ref, degree_ref, out_ref, update_ref):
-    chunk = chunks_ref.shape[1]
+    push_update(genes_here, data_ref, second, cut_ref)
+    mine_ref[...] = cut_ref[core]
+    other_ref[...] = cut_ref[1 - core]
+
+
+def next_kernel(
+    genes_here,
+    place_ref,
+    half_ref,
+    rest_ref,
+    data_ref,
+    links_ref,
+    degree_ref,
+    mine_ref,
+    other_ref,
+    update_ref,
+    cut_ref,
+):
+    core = place_ref[0]
     groups = data_ref.shape[1]
+    chunk = half_ref.shape[1]
     genes_total = genes_here * groups
-    pull_update(chunks_ref, update_ref)
+    pull_update(core, half_ref, rest_ref, update_ref)
     inverse = inverse_factor(gram_of(update_ref, genes_total))
     scores = None
     for group in range(groups):
         part = lax.dot_general(
-            update_ref[group],
+            columns_of(update_ref, group),
             block(data_ref, group),
             (((1,), (1,)), ((), ())),
             preferred_element_type=jnp.float32,
@@ -265,24 +349,40 @@
         inverse, scores, precision=HIGHEST, preferred_element_type=jnp.float32
     ) / math.sqrt(genes_total)
     second = diffuse(scores, links_ref[...], degree_ref[:1])
-    push_update(genes_here, data_ref, second, out_ref, chunk)
-    if out_ref.shape[1] > chunk:
-        share_second(second, out_ref, chunk, groups)
-
-
-def last_kernel(genes_here, own_ref, chunks_ref, out_ref, update_ref):
-    pull_update(chunks_ref, update_ref)
-    genes_total = genes_here * update_ref.shape[0]
+    push_update(genes_here, data_ref, second, cut_ref)
+    if cut_ref.shape[2] > chunk:
+        share_second(core, second, cut_ref, chunk, groups)
+    mine_ref[...] = cut_ref[core]
+    other_ref[...] = cut_ref[1 - core]
+
+
+def last_kernel(
+    genes_here, slots, place_ref, half_ref, rest_ref, arrived_ref, out_ref, smoothed_ref, update_ref
+):
+    core, own = place_ref[0], place_ref[1]
+    groups, cores = update_ref.shape[:2]
+    pull_update(core, half_ref, rest_ref, update_ref)
+    genes_total = genes_here * groups
     inverse = inverse_factor(gram_of(update_ref, genes_total))
-    mine = update_ref[own_ref[0]].astype(jnp.float32)
+    mine = columns_of(update_ref, own).astype(jnp.float32)
     loadings = jnp.dot(inverse, mine, precision=HIGHEST, preferred_element_type=jnp.float32)
     out_ref[...] = loadings[:, :genes_here]
+    order_shares(arrived_ref, half_ref.shape[1], smoothed_ref, groups, cores, slots)
+
+
+def add_kernel(mine_ref, arrived_ref, out_ref):
+    total = mine_ref[...].astype(jnp.float32) + arrived_ref[...].astype(jnp.float32)
+    out_ref[...] = total.astype(jnp.bfloat16)
 
 
 def sum_kernel(chunks_ref, out_ref):
     parts = chunks_ref[:, : out_ref.shape[1]].astype(jnp.float32)
     total = jnp.sum(parts, axis=0).astype(jnp.bfloat16)
     out_ref[...] = jnp.broadcast_to(total[None], out_ref.shape)
+
+
+def like(array):
+    return jax.ShapeDtypeStruct(array.shape, array.dtype)
 
 
 def call(kernel, out_shape, scratch=(), scalars=0, arrays=0):
@@ -299,83 +399,96 @@
 
 
 def by_cell(data, start, link_dev, link_slot, link_weight):
-    axes = ("cells", "genes")
-    devices, groups = lax.axis_size("cells"), lax.axis_size("genes")
+    cores, groups = lax.axis_size("core"), lax.axis_size("genes")
+    devices = lax.axis_size("chips") * cores
     parts = devices * groups
+    blocks = parts // cores
     slots, neighbours = link_dev.shape
     genes_here, width = data.shape[1], start.shape[1]
     tile_cells = data.shape[0] // slots
     rows_of = tile_cells // parts
     rows = slots * rows_of
-    padded = -(-genes_here // (2 * LANES)) * 2 * LANES
+    padded = -(-genes_here // LANES) * LANES
     cells = devices * rows
-    chunk = groups * width * padded // (parts * LANES)
-    own = lax.axis_index("genes").astype(jnp.int32).reshape(1)
-
-    links = jnp.stack([link_dev, link_slot, link_weight]).astype(jnp.float32)
-    links = jnp.pad(links, ((0, padded - genes_here - 3), (0, 0), (0, rows_of - neighbours)))
-    links = jnp.broadcast_to(links[:, :, None], (links.shape[0], slots, parts, rows_of))
-    links = links.reshape(links.shape[0], slots * tile_cells)
-    span = max(1, 16 // rows_of) * tile_cells
-    genes = 2 * LANES
-    moved = pl.pallas_call(
-        functools.partial(regroup_kernel, rows_of, genes_here),
-        grid=(padded // genes,),
-        out_shape=jax.ShapeDtypeStruct((parts, rows, padded), jnp.bfloat16),
-        in_specs=[
-            pl.BlockSpec((genes, slots * tile_cells), lambda at: (at, 0)),
-            pl.BlockSpec(links.shape, lambda at: (0, 0)),
-        ],
-        out_specs=pl.BlockSpec((parts, rows, genes), lambda at: (0, 0, at)),
-        scratch_shapes=[pltpu.VMEM((span, span), jnp.bfloat16)],
-        compiler_params=pltpu.CompilerParams(vmem_limit_bytes=60 * 1024 * 1024),
-    )(data.T, links)
-    moved = lax.all_to_all(moved, axes, 0, 0, tiled=True).reshape(devices, groups, rows, padded)
+    chunk = width // cores
+    place = jnp.stack([lax.axis_index("core"), lax.axis_index("genes")]).astype(jnp.int32)
+
+    def exchange(array):
+        return lax.all_to_all(array, ("chips", "genes"), 0, 0, tiled=True)
+
+    def swap(array):
+        return lax.ppermute(array, "core", [(0, 1), (1, 0)])
+
     narrow = jnp.pad(start.astype(jnp.bfloat16).T, ((0, 0), (0, padded - genes_here)))
     starts = [narrow]
     for shift in range(1, groups):
         pairs = [(at, (at + shift) % groups) for at in range(groups)]
         starts.append(lax.ppermute(narrow, "genes", pairs))
     starts = jnp.stack(starts)
-
-    chunks = jax.ShapeDtypeStruct((parts, chunk, LANES), jnp.bfloat16)
-    update = pltpu.VMEM((groups, width, padded), jnp.bfloat16)
+    moved = pl.pallas_call(
+        functools.partial(regroup_kernel, rows_of),
+        out_shape=jax.ShapeDtypeStruct((parts, rows, padded), jnp.bfloat16),
+        in_specs=[pl.BlockSpec(memory_space=pl.ANY)] * 4,
+        out_specs=pl.BlockSpec(memory_space=pltpu.VMEM),
+        scratch_shapes=[
+            pltpu.VMEM((genes_here, slots * tile_cells), jnp.bfloat16),
+            pltpu.VMEM((3, slots, neighbours), jnp.int32),
+            pltpu.SemaphoreType.DMA((rows // max(16, rows_of),)),
+            pltpu.SemaphoreType.DMA((3,)),
+        ],
+        compiler_params=pltpu.CompilerParams(vmem_limit_bytes=32 * 1024 * 1024),
+    )(data.T, link_dev, link_slot, link_weight)
+    moved, starts = lax.optimization_barrier((moved, starts))
+    moved = lax.all_to_all(moved, ("chips", "core", "genes"), 0, 0, tiled=True)
+    moved = moved.reshape(devices, groups, rows, padded)
+
+    def cut(tall):
+        return (
+            jax.ShapeDtypeStruct((blocks, tall, LANES), jnp.bfloat16),
+            pltpu.VMEM((cores, blocks, tall, LANES), jnp.bfloat16),
+        )
+
+    update = pltpu.VMEM((groups, cores, chunk, padded), jnp.bfloat16)
     links = jax.ShapeDtypeStruct((cells, cells), jnp.bfloat16)
     degree = jax.ShapeDtypeStruct((8, cells), jnp.float32)
-    extra = jax.ShapeDtypeStruct((parts, chunk + 16, LANES), jnp.bfloat16)
+
+    def reduce(mine, other):
+        return exchange(call(add_kernel, like(mine), arrays=2)(mine, swap(other)))
 
     def gather(arrived):
-        summed = call(sum_kernel, chunks, arrays=1)(arrived)
-        return lax.all_to_all(summed, axes, 0, 0, tiled=True)
-
-    pushed, links, degree = call(
+        half = exchange(call(sum_kernel, cut(chunk)[0], arrays=1)(arrived))
+        return half, swap(half)
+
+    share, scratch = cut(chunk)
+    mine, other, links, degree = call(
         functools.partial(first_kernel, genes_here, slots),
-        (chunks, links, degree),
+        (share, share, links, degree),
+        (scratch,),
         scalars=1,
         arrays=2,
-    )(own, moved, starts)
-    arrived = lax.all_to_all(pushed, axes, 0, 0, tiled=True)
+    )(place, moved, starts)
+    arrived = reduce(mine, other)
     for step in range(1, ITERS):
-        pushed = call(
+        share, scratch = cut(chunk + 16 if step == ITERS - 1 else chunk)
+        mine, other = call(
             functools.partial(next_kernel, genes_here),
-            extra if step == ITERS - 1 else chunks,
-            (update,),
-            arrays=4,
-        )(gather(arrived), moved, links, degree)
-        arrived = lax.all_to_all(pushed, axes, 0, 0, tiled=True)
-    loadings = call(
-        functools.partial(last_kernel, genes_here),
-        jax.ShapeDtypeStruct((width, genes_here), jnp.float32),
+            (share, share),
+            (update, scratch),
+            scalars=1,
+            arrays=5,
+        )(place, *gather(arrived), moved, links, degree)
+        arrived = reduce(mine, other)
+    loadings, smoothed = call(
+        functools.partial(last_kernel, genes_here, slots),
+        (
+            jax.ShapeDtypeStruct((width, genes_here), jnp.float32),
+            jax.ShapeDtypeStruct((width // groups, slots * tile_cells), jnp.bfloat16),
+        ),
         (update,),
         scalars=1,
-        arrays=1,
-    )(own, gather(arrived))
-
-    part_width = width // groups
-    slabs = part_width // 16
-    smoothed = arrived[:, chunk:, : slabs * rows].reshape(parts, 16, slabs, slots, rows_of)
-    smoothed = smoothed.transpose(2, 1, 3, 0, 4)
-    return loadings.T, smoothed.reshape(part_width, slots * tile_cells)
+        arrays=3,
+    )(place, *gather(arrived), arrived)
+    return loadings.T, smoothed
 
 
 def by_tile(data, start, link_dev, link_slot, link_weight):
@@ -489,41 +602,46 @@
     return (loadings, smoothed)
 
 
-def per_device(data, start, link_dev, link_slot, link_weight):
-    groups = lax.axis_size("genes")
-    parts = lax.axis_size("cells") * groups
-    slots, neighbours = link_dev.shape
-    tile_cells = data.shape[0] // slots
-    genes_here, width = data.shape[1], start.shape[1]
-    padded = -(-genes_here // (2 * LANES)) * 2 * LANES
-    rows = slots * tile_cells // parts
-    fits = (
-        tile_cells % (8 * parts) == 0
-        and neighbours <= tile_cells // parts
+def fits_by_cell(mesh, data, start, link_dev):
+    groups, parts = mesh.shape["genes"], mesh.size
+    slots, neighbours = link_dev.shape[0] * groups // parts, link_dev.shape[1]
+    tile_cells = data.shape[0] // link_dev.shape[0]
+    genes_here, width = data.shape[1] // groups, start.shape[1]
+    padded = -(-genes_here // LANES) * LANES
+    rows_of = tile_cells // parts
+    rows = slots * rows_of
+    return (
+        mesh.shape["cells"] % 2 == 0
+        and tile_cells % (8 * parts) == 0
+        and neighbours <= rows_of
         and rows % 16 == 0
+        and rows % max(16, rows_of) == 0
         and LANES % rows == 0
         and genes_here % 8 == 0
-        and 3 <= padded - genes_here <= LANES
-        and width % (16 * groups) == 0
-        and width // groups // 16 * rows <= LANES
-        and width * padded * groups % (parts * LANES * 16) == 0
-    )
-    way = by_cell if fits else by_tile
-    return way(data, start, link_dev, link_slot, link_weight)
+        and padded - genes_here >= 3
+        and groups * padded // LANES == parts // 2
+        and width % (32 * groups) == 0
+        and width // groups // 16 * rows * 2 <= LANES
+    )
 
 
 def solution(mesh):
-    placed = (
-        P("cells", "genes"),
-        P("genes", None),
-        P("cells", None),
-        P("cells", None),
-        P("cells", None),
-    )
-    return jax.shard_map(
-        per_device,
-        mesh=mesh,
-        in_specs=placed,
-        out_specs=(P("genes", None), P("genes", "cells")),
-        check_vma=False,
-    )
+    chips = Mesh(
+        mesh.devices.reshape(mesh.shape["cells"] // 2, 2, mesh.shape["genes"]),
+        ("chips", "core", "genes"),
+    )
+
+    def program(data, start, link_dev, link_slot, link_weight):
+        if fits_by_cell(mesh, data, start, link_dev):
+            way, over, cells = by_cell, chips, ("chips", "core")
+        else:
+            way, over, cells = by_tile, mesh, "cells"
+        return jax.shard_map(
+            way,
+            mesh=over,
+            in_specs=(P(cells, "genes"), P("genes", None)) + (P(cells, None),) * 3,
+            out_specs=(P("genes", None), P("genes", cells)),
+            check_vma=False,
+        )(data, start, link_dev, link_slot, link_weight)
+
+    return program

time: 160 us -> 159 us (level)
  starting transfers between devices: 12.2 us -> 8.44 us
  local copies, waits for them, and re-layouts: 2.84 us -> 4.97 us
    ppermute x1, waiting for transfers between devices: 19.2 us -> 0.01 us  [by_cell(): starts.append(lax.ppermute(narrow, 'genes', pairs))]
    all_to_all x2 -> x1, waiting for transfers between devices: 36.4 us -> 48.6 us  [by_cell(): moved = lax.all_to_all(moved, ('chips', 'core', 'genes'), 0, 0, tiled=True)]
    ppermute x0 -> x6, waiting for transfers between devices: none -> 7.86 us  [swap(): return lax.ppermute(array, 'core', [(0, 1), (1, 0)])]
    all_to_all x2 -> x1, starting transfers between devices: 10.4 us -> 4.93 us  [by_cell(): moved = lax.all_to_all(moved, ('chips', 'core', 'genes'), 0, 0, tiled=True)]
    unnamed x4 -> x10, local copies, waits for them, and re-layouts: 0.86 us -> 4.95 us
    all_to_all x5 -> x6, blocking collectives: 67.4 us -> 67.1 us  [exchange(): return lax.all_to_all(array, ('chips', 'genes'), 0, 0, tiled=True)]
    pallas_call x8 -> x11, Pallas kernels: 19.6 us -> 19.3 us  [the longest x2 8.93 us: by_cell(): call(functools.partial(next_kernel, genes_here), (share, share), (update,...]
  transfers between devices with their start and end apart: 3 -> 8, of which waited for: 3 -> 7; matrix products, arithmetic and copies ran while one was open for 1% -> 0% of each run, Pallas kernels for 0% -> 2%
where the time goes in v4:
time: 159 us; the launch traced here: 158 us
  blocking collectives  67.1 us (42%)
  waiting for transfers between devices  56.5 us (36%)
  Pallas kernels  19.3 us (12%)
  starting transfers between devices  8.44 us (5%)
  local copies, waits for them, and re-layouts  4.97 us (3%)
    all_to_all x6, blocking collectives, exchange(): return lax.all_to_all(array, ('chips', 'genes'), 0, 0, tiled=True)  67.1 us
    all_to_all x1, waiting for transfers between devices, by_cell(): moved = lax.all_to_all(moved, ('chips', 'core', 'genes'), 0, 0, tiled=True)  48.6 us
    pallas_call x2, Pallas kernels, by_cell(): call(functools.partial(next_kernel, genes_here), (share, share), (update,...  8.93 us
    ppermute x6, waiting for transfers between devices, swap(): return lax.ppermute(array, 'core', [(0, 1), (1, 0)])  7.86 us
    unnamed x10, local copies, waits for them, and re-layouts  4.95 us
    all_to_all x1, starting transfers between devices, by_cell(): moved = lax.all_to_all(moved, ('chips', 'core', 'genes'), 0, 0, tiled=True)  4.93 us
    pallas_call x1, Pallas kernels, by_cell(): call(functools.partial(last_kernel, genes_here, slots), (jax.ShapeDtypeSt...  4.48 us
  transfers between devices with their start and end apart: 8, of which 7 were waited for; matrix products, arithmetic and copies ran while one was open for 0% of the time, Pallas kernels for 2%

profile of v4, /device:TPU:0, one launch (start us, length us, event | category | flops | bytes accessed | tf_op | source)
XLA Modules:
  0.0 158.1 jit_solution(15214294435765906548)
XLA Ops:
  0.6 1.0 convert_bitcast_fusion
  1.6 3.0 %collective-permute-start = (bf16[64,1024]{1,0:T(8,128)(2,1)S(1)}, bf16[64,1024]{1,0:T(8,128)(2,1)S(1)}, u32[]{:S(2)}, u32[]{:S(2)}) collective-permute-start(bf16[64,1024]{1,0:T(8,128)(2,1)S(1)} %get-tuple-element.27), channel_id=1, source_target_pairs={{0,1},{1,0},{2,3},{3,2},{4,5},{5,4},{6,7},{7,6},{8,9},{9,8},{10,11... | collective-permute-start | bytes 393224 | tf_op jit(solution)/shard_map/ppermute | solution.py:426
  4.6 1.6 copy-done.1
  6.2 0.7 copy-done.2
  6.9 0.7 copy-done.3
  7.6 0.7 copy-done.4
  8.2 2.9 %shard_map.68 = bf16[32,32,1024]{2,1,0:T(8,128)(2,1)S(1)} custom-call(bf16[1000,1024]{1,0:T(8,128)(2,1)S(1)} %bitcast.13, s32[4,8]{1,0:T(4,128)S(1)} %copy-done.2, s32[4,8]{1,0:T(4,128)S(1)} %copy-done.3, s32[4,8]{1,0:T(4,128)S(1)} %copy-done.4), custom_call_target="tpu_custom_call" | custom-call | tf_op jit(solution)/shard_map/pallas_call | solution.py:428
  11.2 1.3 copy-done
  12.6 4.9 %all-to-all-start = ((bf16[32,32,1024]{2,1,0:T(8,128)(2,1)}), bf16[32,32,1024]{2,1,0:T(8,128)(2,1)S(1)}, u32[]{:S(2)}, u32[]{:S(2)}) async-start(bf16[32,32,1024]{2,1,0:T(8,128)(2,1)} %copy-done), calls=%async_computation | async-start | bytes 4194304 | tf_op jit(solution)/shard_map/all_to_all | solution.py:442
  17.5 0.1 pad_add_fusion.place_ref
  17.6 48.6 %all-to-all-done = bf16[32,32,1024]{2,1,0:T(8,128)(2,1)S(1)} async-done(((bf16[32,32,1024]{2,1,0:T(8,128)(2,1)}), bf16[32,32,1024]{2,1,0:T(8,128)(2,1)S(1)}, u32[]{:S(2)}, u32[]{:S(2)}) %all-to-all-start) | async-done | bytes 2097184 | tf_op jit(solution)/shard_map/all_to_all | solution.py:442
  66.2 2.8 %shard_map.69 = (bf16[16,32,128]{2,1,0:T(8,128)(2,1)S(1)}, bf16[16,32,128]{2,1,0:T(8,128)(2,1)S(1)}, bf16[512,512]{1,0:T(8,128)(2,1)S(1)}, f32[8,512]{1,0:T(8,128)S(1)}) custom-call(s32[2]{0:T(128)S(1)} %pad_add_fusion.place_ref, bf16[16,2,32,1024]{3,2,1,0:T(8,128)(2,1)S(1)} %bitcast.10, bf16[2,64,1024]{2,1,0:T(8,128)(2,1)S(1)} %pad_maximum_fusion.start_ref), custom_call_target="tpu_custom_call" | custom-call | tf_op jit(solution)/shard_map/pallas_call | solution.py:463
  69.0 0.1 collective-permute-start.1
  69.1 1.3 collective-permute-done.1.arrived_ref
  70.5 12.3 %all_to_all.35.chunks_ref = bf16[16,32,128]{2,1,0:T(8,128)(2,1)S(1)} all-to-all(bf16[16,32,128]{2,1,0:T(8,128)(2,1)S(1)} %shard_map.70), channel_id=1, replica_groups=mesh['chips'=8,'core'=2,'genes'=2] {'chips','genes'}, dimensions={0} | all-to-all | bytes 262144 | tf_op jit(solution)/shard_map/all_to_all | solution.py:417
  82.8 10.7 %all_to_all.36.half_ref = bf16[16,32,128]{2,1,0:T(8,128)(2,1)S(1)} all-to-all(bf16[16,32,128]{2,1,0:T(8,128)(2,1)S(1)} %shard_map.71), channel_id=1, replica_groups=mesh['chips'=8,'core'=2,'genes'=2] {'chips','genes'}, dimensions={0} | all-to-all | bytes 262144 | tf_op jit(solution)/shard_map/all_to_all | solution.py:417
  93.5 0.0 collective-permute-start.2
  93.5 1.3 collective-permute-done.2.rest_ref
  94.9 4.5 %shard_map.72 = (bf16[16,32,128]{2,1,0:T(8,128)(2,1)S(1)}, bf16[16,32,128]{2,1,0:T(8,128)(2,1)S(1)}) custom-call(s32[2]{0:T(128)S(1)} %pad_add_fusion.place_ref, bf16[16,32,128]{2,1,0:T(8,128)(2,1)S(1)} %all_to_all.36.half_ref, bf16[16,32,128]{2,1,0:T(8,128)(2,1)S(1)} %collective-permute-done.2.rest_ref, bf16[16,2,32,1024]{3,2,1,0:T(8,128)(2,1)S(1)} %bitcast.11, ...), custom_call_target="tpu_custom_call" | custom-call | tf_op jit(solution)/shard_map/pallas_call | solution.py:473
  99.3 0.2 collective-permute-start.3
  99.6 1.2 collective-permute-done.3.arrived_ref
  100.8 10.6 %all_to_all.37.chunks_ref = bf16[16,32,128]{2,1,0:T(8,128)(2,1)S(1)} all-to-all(bf16[16,32,128]{2,1,0:T(8,128)(2,1)S(1)} %shard_map.73), channel_id=1, replica_groups=mesh['chips'=8,'core'=2,'genes'=2] {'chips','genes'}, dimensions={0} | all-to-all | bytes 262144 | tf_op jit(solution)/shard_map/all_to_all | solution.py:417
  111.4 10.7 %all_to_all.38.half_ref = bf16[16,32,128]{2,1,0:T(8,128)(2,1)S(1)} all-to-all(bf16[16,32,128]{2,1,0:T(8,128)(2,1)S(1)} %shard_map.74), channel_id=1, replica_groups=mesh['chips'=8,'core'=2,'genes'=2] {'chips','genes'}, dimensions={0} | all-to-all | bytes 262144 | tf_op jit(solution)/shard_map/all_to_all | solution.py:417
  122.1 1.3 collective-permute-done.4.rest_ref
  123.5 4.5 %shard_map.75 = (bf16[16,48,128]{2,1,0:T(8,128)(2,1)S(1)}, bf16[16,48,128]{2,1,0:T(8,128)(2,1)S(1)}) custom-call(s32[2]{0:T(128)S(1)} %pad_add_fusion.place_ref, bf16[16,32,128]{2,1,0:T(8,128)(2,1)S(1)} %all_to_all.38.half_ref, bf16[16,32,128]{2,1,0:T(8,128)(2,1)S(1)} %collective-permute-done.4.rest_ref, bf16[16,2,32,1024]{3,2,1,0:T(8,128)(2,1)S(1)} %bitcast.12, ...), custom_call_target="tpu_custom_call" | custom-call | tf_op jit(solution)/shard_map/pallas_call | solution.py:473
  128.0 0.2 collective-permute-start.5
  128.2 1.3 collective-permute-done.5.arrived_ref
  129.5 11.5 %all_to_all.39.chunks_ref.arrived_ref = bf16[16,48,128]{2,1,0:T(8,128)(2,1)S(1)} all-to-all(bf16[16,48,128]{2,1,0:T(8,128)(2,1)S(1)} %shard_map.76), channel_id=1, replica_groups=mesh['chips'=8,'core'=2,'genes'=2] {'chips','genes'}, dimensions={0} | all-to-all | bytes 393216 | tf_op jit(solution)/shard_map/all_to_all | solution.py:417
  141.1 11.2 %all_to_all.40.half_ref = bf16[16,32,128]{2,1,0:T(8,128)(2,1)S(1)} all-to-all(bf16[16,32,128]{2,1,0:T(8,128)(2,1)S(1)} %shard_map.77), channel_id=1, replica_groups=mesh['chips'=8,'core'=2,'genes'=2] {'chips','genes'}, dimensions={0} | all-to-all | bytes 262144 | tf_op jit(solution)/shard_map/all_to_all | solution.py:417
  152.3 0.0 collective-permute-start.6
  152.3 1.3 collective-permute-done.6.rest_ref
  153.6 4.5 %shard_map.78 = (f32[64,1000]{1,0:T(8,128)}, bf16[32,1024]{1,0:T(8,128)(2,1)}) custom-call(s32[2]{0:T(128)S(1)} %pad_add_fusion.place_ref, bf16[16,32,128]{2,1,0:T(8,128)(2,1)S(1)} %all_to_all.40.half_ref, bf16[16,32,128]{2,1,0:T(8,128)(2,1)S(1)} %collective-permute-done.6.rest_ref, bf16[16,48,128]{2,1,0:T(8,128)(2,1)S(1)} %all_to_all.39.chunks_ref.arrived_ref), custom_call_target="tpu_custom_call" | custom-call | tf_op jit(solution)/shard_map/pallas_call | solution.py:481
  (15 shorter events, 0.3 us)
Async XLA Ops:
  1.6 10.9 %collective-permute-start = (bf16[64,1024]{1,0:T(8,128)(2,1)S(1)}, bf16[64,1024]{1,0:T(8,128)(2,1)S(1)}, u32[]{:S(2)}, u32[]{:S(2)}) collective-permute-start(bf16[64,1024]{1,0:T(8,128)(2,1)S(1)} %get-tuple-element.27), channel_id=1, source_target_pairs={{0,1},{1,0},{2,3},{3,2},{4,5},{5,4},{6,7},{7,6},{8,9},{9,8},{10,11... | collective-permute-start | bytes 393224 | tf_op jit(solution)/shard_map/ppermute | solution.py:426
  4.6 1.6 copy-start.1
  6.2 0.7 copy-start.2
  6.9 0.7 copy-start.3
  7.6 0.7 copy-start.4
  11.2 1.3 copy-start
  12.6 53.7 %all-to-all-start = ((bf16[32,32,1024]{2,1,0:T(8,128)(2,1)}), bf16[32,32,1024]{2,1,0:T(8,128)(2,1)S(1)}, u32[]{:S(2)}, u32[]{:S(2)}) async-start(bf16[32,32,1024]{2,1,0:T(8,128)(2,1)} %copy-done), calls=%async_computation | async-start | bytes 4194304 | tf_op jit(solution)/shard_map/all_to_all | solution.py:442
  69.0 1.4 collective-permute-start.1
  93.5 1.3 collective-permute-start.2
  99.3 1.4 collective-permute-start.3
  122.1 1.3 collective-permute-start.4
  128.0 1.5 collective-permute-start.5
  152.3 1.3 collective-permute-start.6

commit v5 on v4

--- a/solution.py
+++ b/solution.py
@@ -11,6 +11,7 @@
 
 ITERS = 3
 LANES = 128
+AMPLIFIED = 4.0
 
 self_weight = 8.0
 HIGHEST = lax.Precision.HIGHEST
@@ -24,7 +25,7 @@
     down = lax.rsqrt(jnp.sum(diagonal, axis=1, keepdims=True))
     along = lax.rsqrt(jnp.sum(diagonal, axis=0, keepdims=True))
     scaled = gram * down * along
-    state = jnp.concatenate([jnp.where(rows == cols, along, 0.0), scaled], axis=1)
+    state = jnp.concatenate([(rows == cols).astype(jnp.float32), scaled], axis=1)
     strips = [state[at : at + 8] for at in range(0, width, 8)]
     shape = strips[0].shape
     place = lax.broadcasted_iota(jnp.int32, shape, 0)
@@ -42,37 +43,35 @@
             for i in range(j, 8)
         }
         lines = [jnp.broadcast_to(strip[j : j + 1], shape) for j in range(8)]
-        factor, solved = {}, [None] * 8
+        below = range(panel + 1, len(strips))
+        rest = {(at, j): column(strips[at], j) for at in below for j in range(8)}
         for j in range(0, 8, 2):
             a, b, c = core[j, j], core[j + 1, j], core[j + 1, j + 1]
             inverse = 1.0 / (a * c - b * b)
             step = b * (1.0 / a)
             ia, ib, ic = c * inverse, b * inverse, a * inverse
+
+            def factors(first, second):
+                return first * ia - second * ib, second * ic - first * ib
+
             for i in range(j + 2, 8):
-                factor[i, j] = core[i, j] * ia - core[i, j + 1] * ib
-                factor[i, j + 1] = core[i, j + 1] * ic - core[i, j] * ib
-            for i in range(j + 2, 8):
+                first, second = factors(core[i, j], core[i, j + 1])
                 for m in range(j + 2, i + 1):
-                    core[i, m] -= factor[i, j] * core[m, j] + factor[i, j + 1] * core[m, j + 1]
-                lines[i] -= factor[i, j] * lines[j] + factor[i, j + 1] * lines[j + 1]
-            solved[j] = ia * lines[j] - ib * lines[j + 1]
-            solved[j + 1] = ic * lines[j + 1] - ib * lines[j]
+                    core[i, m] -= first * core[m, j] + second * core[m, j + 1]
+                lines[i] -= first * lines[j] + second * lines[j + 1]
+            for at in below:
+                first, second = factors(rest[at, j], rest[at, j + 1])
+                for m in range(j + 2, 8):
+                    rest[at, m] -= first * core[m, j] + second * core[m, j + 1]
+                strips[at] -= first * lines[j] + second * lines[j + 1]
             lines[j + 1] -= step * lines[j]
             core[j + 1, j + 1] = c - step * b
-        for j in reversed(range(0, 8, 2)):
-            for i in range(j + 2, 8):
-                solved[j] -= factor[i, j] * solved[i]
-                solved[j + 1] -= factor[i, j + 1] * solved[i]
-        for later in range(panel + 1, len(strips)):
-            terms = [column(strips[later], j) * solved[j] for j in range(8)]
-            while len(terms) > 1:
-                terms = [terms[at] + terms[at + 1] for at in range(0, len(terms), 2)]
-            strips[later] = strips[later] - terms[0]
         final = lines[0] * lax.rsqrt(core[0, 0])
         for j in range(1, 8):
             final = jnp.where(place == j, lines[j] * lax.rsqrt(core[j, j]), final)
         done.append(final)
-    return jnp.concatenate(done, axis=0)[:, :width]
+    inverse = jnp.concatenate(done, axis=0)[:, :width]
+    return inverse * along, jnp.sum(inverse * inverse, axis=1, keepdims=True)
 
 
 def link_matrix(packed, tiles, neighbours, slots, rows_of):
@@ -129,7 +128,7 @@
     for group in range(groups):
         update = jnp.dot(second, block(data_ref, group), preferred_element_type=jnp.float32)
         lane = lax.broadcasted_iota(jnp.int32, update.shape, 1)
-        update = jnp.where(lane < genes_here, update, 0.0).astype(jnp.bfloat16)
+        update = jnp.where(lane < genes_here, update, 0.0).astype(cut_ref.dtype)
         for at in range(blocks):
             for core in range(cores):
                 cut_ref[core, group * blocks + at, :chunk] = update[
@@ -152,47 +151,68 @@
     return update.reshape(update.shape[0] * update.shape[1], update.shape[2])
 
 
-def gram_of(update_ref, genes_total):
+def normaliser(update_ref, genes_total):
+    exact = update_ref.dtype == jnp.float32
     gram = None
     for group in range(update_ref.shape[0]):
         update = columns_of(update_ref, group)
         part = lax.dot_general(
-            update, update, (((1,), (1,)), ((), ())), preferred_element_type=jnp.float32
+            update,
+            update,
+            (((1,), (1,)), ((), ())),
+            precision=HIGHEST if exact else None,
+            preferred_element_type=jnp.float32,
         )
         gram = part if gram is None else gram + part
-    return gram / genes_total
+    return inverse_factor(gram / genes_total)
+
+
+def score(left, data_ref, groups):
+    total = None
+    for at, group in enumerate(groups):
+        part = lax.dot_general(
+            left(at),
+            block(data_ref, group),
+            (((1,), (1,)), ((), ())),
+            preferred_element_type=jnp.float32,
+        )
+        total = part if total is None else total + part
+    return total
 
 
 def regroup_kernel(
-    rows_of, data_any, dev_any, slot_any, weight_any, out_ref, data_ref, link_ref, data_sem, link_sem
+    rows_of,
+    data_any,
+    dev_any,
+    slot_any,
+    weight_any,
+    out_any,
+    data_ref,
+    link_ref,
+    out_ref,
+    data_sem,
+    link_sem,
+    out_sem,
 ):
     genes_here, cells = data_ref.shape
     parts, rows, padded = out_ref.shape
     slots, neighbours = link_ref.shape[1:]
     tile_cells = cells // slots
     share = max(16, rows_of)
-    span = share * parts
-    turns = rows // share
+    joined = share // rows_of
+    whole = padded - LANES
     link_copies = [
         pltpu.make_async_copy(source, link_ref.at[at], link_sem.at[at])
         for at, source in enumerate((dev_any, slot_any, weight_any))
     ]
-    for copy in link_copies:
+    tile_at = [pl.ds(tile * tile_cells, tile_cells) for tile in range(slots)]
+    data_copies = [
+        pltpu.make_async_copy(data_any.at[:, at], data_ref.at[:, at], data_sem.at[tile])
+        for tile, at in enumerate(tile_at)
+    ]
+    for copy in link_copies + data_copies:
         copy.start()
-    data_copies = []
-    for turn in range(turns):
-        part = pl.ds(turn * span, span)
-        data_copies.append(
-            pltpu.make_async_copy(
-                data_any.at[:, part], data_ref.at[:, part], data_sem.at[turn]
-            )
-        )
-        data_copies[turn].start()
-
-    to = lax.broadcasted_iota(jnp.int32, (span, span), 0)
-    at = lax.broadcasted_iota(jnp.int32, (span, span), 1)
-    source = (to % share // rows_of) * tile_cells + to // share * rows_of + to % rows_of
-    order = (source == at).astype(jnp.bfloat16)
+
     spread = (
         lax.broadcasted_iota(jnp.int32, (neighbours, cells), 0)
         == lax.broadcasted_iota(jnp.int32, (neighbours, cells), 1) % rows_of
@@ -208,22 +228,32 @@
         )
         wide = jnp.sum(jnp.where(own_tile, wide, 0.0), axis=0, keepdims=True)
         links = jnp.where(row == at, wide, links)
-    whole = padded - LANES
-
-    def moved(part):
-        taken = lax.dot_general(
-            order, part, (((1,), (1,)), ((), ())), preferred_element_type=jnp.float32
-        )
-        return taken.astype(jnp.bfloat16).reshape(parts, share, part.shape[0])
-
-    for turn in range(turns):
-        part = slice(turn * span, (turn + 1) * span)
-        keep = slice(turn * share, (turn + 1) * share)
-        data_copies[turn].wait()
-        out_ref[:, keep, :whole] = moved(data_ref[:whole, part])
-        rest = data_ref[whole:genes_here, part].astype(jnp.float32)
-        rest = jnp.concatenate([rest, links[:, part]], axis=0)
-        out_ref[:, keep, whole:] = moved(rest.astype(jnp.bfloat16))
+
+    def turned(part):
+        return part.T.astype(jnp.float32).reshape(parts, rows_of, part.shape[0])
+
+    out_copies = []
+    for first in range(0, slots, joined):
+        main, rest = [], []
+        for tile in range(first, first + joined):
+            data_copies[tile].wait()
+            at = slice(tile * tile_cells, (tile + 1) * tile_cells)
+            main.append(turned(data_ref[:whole, at]))
+            end = data_ref[whole:genes_here, at].astype(jnp.float32)
+            end = jnp.concatenate([end, links[:, at]], axis=0)
+            rest.append(turned(end.astype(jnp.bfloat16)))
+        keep = slice(first * rows_of, first * rows_of + share)
+        out_ref[:, keep, :whole] = jnp.concatenate(main, axis=1).astype(jnp.bfloat16)
+        out_ref[:, keep, whole:] = jnp.concatenate(rest, axis=1).astype(jnp.bfloat16)
+        keep = pl.ds(first * rows_of, share)
+        out_copies.append(
+            pltpu.make_async_copy(
+                out_ref.at[:, keep], out_any.at[:, keep], out_sem.at[first // joined]
+            )
+        )
+        out_copies[-1].start()
+    for copy in out_copies:
+        copy.wait()
 
 
 def share_second(core, second, cut_ref, chunk, groups):
@@ -248,7 +278,7 @@
                         )
                         share = jnp.where((lane == slab) & (core == turn), turned, share)
                 chip, to = divmod(at * (LANES // rows) + device, cores)
-                cut_ref[to, chip * groups + group, chunk:] = share.astype(jnp.bfloat16)
+                cut_ref[to, chip * groups + group, chunk:] = share.astype(cut_ref.dtype)
 
 
 def order_shares(arrived_ref, chunk, out_ref, groups, cores, slots):
@@ -300,16 +330,8 @@
     )
     links_ref[...] = links
     degree_ref[...] = degree
-    scores = None
-    for shift in range(groups):
-        group = lax.rem(own + groups - shift, groups)
-        part = lax.dot_general(
-            start_ref[shift],
-            block(data_ref, group),
-            (((1,), (1,)), ((), ())),
-            preferred_element_type=jnp.float32,
-        )
-        scores = part if scores is None else scores + part
+    order = [lax.rem(own + groups - shift, groups) for shift in range(groups)]
+    scores = score(lambda shift: start_ref[shift], data_ref, order)
     scores = scores / math.sqrt(genes_here * groups)
     second = diffuse(scores, links, degree[:1])
     push_update(genes_here, data_ref, second, cut_ref)
@@ -327,6 +349,7 @@
     degree_ref,
     mine_ref,
     other_ref,
+    worst_ref,
     update_ref,
     cut_ref,
 ):
@@ -335,20 +358,23 @@
     chunk = half_ref.shape[1]
     genes_total = genes_here * groups
     pull_update(core, half_ref, rest_ref, update_ref)
-    inverse = inverse_factor(gram_of(update_ref, genes_total))
-    scores = None
-    for group in range(groups):
-        part = lax.dot_general(
-            columns_of(update_ref, group),
-            block(data_ref, group),
-            (((1,), (1,)), ((), ())),
-            preferred_element_type=jnp.float32,
-        )
-        scores = part if scores is None else scores + part
-    scores = jnp.dot(
-        inverse, scores, precision=HIGHEST, preferred_element_type=jnp.float32
-    ) / math.sqrt(genes_total)
-    second = diffuse(scores, links_ref[...], degree_ref[:1])
+    inverse, amplified = normaliser(update_ref, genes_total)
+    worst_ref[...] = jnp.broadcast_to(amplified, worst_ref.shape)
+
+    def apply(array):
+        return jnp.dot(inverse, array, precision=HIGHEST, preferred_element_type=jnp.float32)
+
+    if update_ref.dtype == jnp.float32:
+        scores = score(
+            lambda group: apply(columns_of(update_ref, group)).astype(jnp.bfloat16),
+            data_ref,
+            range(groups),
+        )
+    else:
+        scores = apply(
+            score(lambda group: columns_of(update_ref, group), data_ref, range(groups))
+        )
+    second = diffuse(scores / math.sqrt(genes_total), links_ref[...], degree_ref[:1])
     push_update(genes_here, data_ref, second, cut_ref)
     if cut_ref.shape[2] > chunk:
         share_second(core, second, cut_ref, chunk, groups)
@@ -357,13 +383,24 @@
 
 
 def last_kernel(
-    genes_here, slots, place_ref, half_ref, rest_ref, arrived_ref, out_ref, smoothed_ref, update_ref
+    genes_here,
+    slots,
+    place_ref,
+    half_ref,
+    rest_ref,
+    arrived_ref,
+    *refs,
 ):
+    *earlier, out_ref, smoothed_ref, good_ref, update_ref = refs
     core, own = place_ref[0], place_ref[1]
     groups, cores = update_ref.shape[:2]
     pull_update(core, half_ref, rest_ref, update_ref)
     genes_total = genes_here * groups
-    inverse = inverse_factor(gram_of(update_ref, genes_total))
+    inverse, amplified = normaliser(update_ref, genes_total)
+    good = amplified <= AMPLIFIED
+    for worst_ref in earlier:
+        good = good & (worst_ref[:, :1] <= AMPLIFIED)
+    good_ref[0] = jnp.min(good.astype(jnp.int32))
     mine = columns_of(update_ref, own).astype(jnp.float32)
     loadings = jnp.dot(inverse, mine, precision=HIGHEST, preferred_element_type=jnp.float32)
     out_ref[...] = loadings[:, :genes_here]
@@ -372,12 +409,12 @@
 
 def add_kernel(mine_ref, arrived_ref, out_ref):
     total = mine_ref[...].astype(jnp.float32) + arrived_ref[...].astype(jnp.float32)
-    out_ref[...] = total.astype(jnp.bfloat16)
+    out_ref[...] = total.astype(out_ref.dtype)
 
 
 def sum_kernel(chunks_ref, out_ref):
     parts = chunks_ref[:, : out_ref.shape[1]].astype(jnp.float32)
-    total = jnp.sum(parts, axis=0).astype(jnp.bfloat16)
+    total = jnp.sum(parts, axis=0).astype(out_ref.dtype)
     out_ref[...] = jnp.broadcast_to(total[None], out_ref.shape)
 
 
@@ -392,13 +429,16 @@
         kernel,
         out_shape=out_shape,
         in_specs=in_specs,
-        out_specs=jax.tree.map(lambda _: pl.BlockSpec(memory_space=pltpu.VMEM), out_shape),
+        out_specs=jax.tree.map(
+            lambda leaf: pl.BlockSpec(memory_space=pltpu.VMEM if leaf.ndim > 1 else pltpu.SMEM),
+            out_shape,
+        ),
         scratch_shapes=list(scratch),
         compiler_params=pltpu.CompilerParams(vmem_limit_bytes=32 * 1024 * 1024),
     )
 
 
-def by_cell(data, start, link_dev, link_slot, link_weight):
+def by_cell(kept, data, start, link_dev, link_slot, link_weight):
     cores, groups = lax.axis_size("core"), lax.axis_size("genes")
     devices = lax.axis_size("chips") * cores
     parts = devices * groups
@@ -429,26 +469,29 @@
         functools.partial(regroup_kernel, rows_of),
         out_shape=jax.ShapeDtypeStruct((parts, rows, padded), jnp.bfloat16),
         in_specs=[pl.BlockSpec(memory_space=pl.ANY)] * 4,
-        out_specs=pl.BlockSpec(memory_space=pltpu.VMEM),
+        out_specs=pl.BlockSpec(memory_space=pl.ANY),
         scratch_shapes=[
             pltpu.VMEM((genes_here, slots * tile_cells), jnp.bfloat16),
             pltpu.VMEM((3, slots, neighbours), jnp.int32),
+            pltpu.VMEM((parts, rows, padded), jnp.bfloat16),
+            pltpu.SemaphoreType.DMA((slots,)),
+            pltpu.SemaphoreType.DMA((3,)),
             pltpu.SemaphoreType.DMA((rows // max(16, rows_of),)),
-            pltpu.SemaphoreType.DMA((3,)),
         ],
-        compiler_params=pltpu.CompilerParams(vmem_limit_bytes=32 * 1024 * 1024),
+        compiler_params=pltpu.CompilerParams(vmem_limit_bytes=60 * 1024 * 1024),
     )(data.T, link_dev, link_slot, link_weight)
-    moved, starts = lax.optimization_barrier((moved, starts))
     moved = lax.all_to_all(moved, ("chips", "core", "genes"), 0, 0, tiled=True)
     moved = moved.reshape(devices, groups, rows, padded)
 
     def cut(tall):
         return (
-            jax.ShapeDtypeStruct((blocks, tall, LANES), jnp.bfloat16),
-            pltpu.VMEM((cores, blocks, tall, LANES), jnp.bfloat16),
-        )
-
-    update = pltpu.VMEM((groups, cores, chunk, padded), jnp.bfloat16)
+            jax.ShapeDtypeStruct((blocks, tall, LANES), kept),
+            pltpu.VMEM((cores, blocks, tall, LANES), kept),
+        )
+
+    update = pltpu.VMEM((groups, cores, chunk, padded), kept)
+    worst = jax.ShapeDtypeStruct((width, LANES), jnp.float32)
+    earlier = []
     links = jax.ShapeDtypeStruct((cells, cells), jnp.bfloat16)
     degree = jax.ShapeDtypeStruct((8, cells), jnp.float32)
 
@@ -470,25 +513,37 @@
     arrived = reduce(mine, other)
     for step in range(1, ITERS):
         share, scratch = cut(chunk + 16 if step == ITERS - 1 else chunk)
-        mine, other = call(
+        mine, other, amplified = call(
             functools.partial(next_kernel, genes_here),
-            (share, share),
+            (share, share, worst),
             (update, scratch),
             scalars=1,
             arrays=5,
         )(place, *gather(arrived), moved, links, degree)
+        earlier.append(amplified)
         arrived = reduce(mine, other)
-    loadings, smoothed = call(
+    loadings, smoothed, good = call(
         functools.partial(last_kernel, genes_here, slots),
         (
             jax.ShapeDtypeStruct((width, genes_here), jnp.float32),
             jax.ShapeDtypeStruct((width // groups, slots * tile_cells), jnp.bfloat16),
+            jax.ShapeDtypeStruct((1,), jnp.int32),
         ),
         (update,),
         scalars=1,
-        arrays=3,
-    )(place, *gather(arrived), arrived)
-    return loadings.T, smoothed
+        arrays=3 + len(earlier),
+    )(place, *gather(arrived), arrived, *earlier)
+    return loadings.T, smoothed, good[0] == 1
+
+
+def by_condition(*arguments):
+    loadings, smoothed, good = by_cell(jnp.bfloat16, *arguments)
+    return lax.cond(
+        good,
+        lambda *_: (loadings, smoothed),
+        lambda *again: by_cell(jnp.float32, *again)[:2],
+        *arguments,
+    )
 
 
 def by_tile(data, start, link_dev, link_slot, link_weight):
@@ -633,7 +688,7 @@
 
     def program(data, start, link_dev, link_slot, link_weight):
         if fits_by_cell(mesh, data, start, link_dev):
-            way, over, cells = by_cell, chips, ("chips", "core")
+            way, over, cells = by_condition, chips, ("chips", "core")
         else:
             way, over, cells = by_tile, mesh, "cells"
         return jax.shard_map(

time: 159 us -> 319 us (2.01)
  blocking collectives: 67.1 us -> 150 us
  waiting for transfers between devices: 56.5 us -> 111 us
  Pallas kernels: 19.3 us -> 40.4 us
  starting transfers between devices: 8.44 us -> 14.6 us
  local copies, waits for them, and re-layouts: 4.97 us -> 0.76 us
    all_to_all x6 -> x12, blocking collectives: 67.1 us -> 150 us  [exchange(): return lax.all_to_all(array, ('chips', 'genes'), 0, 0, tiled=True)]
    ppermute x1 -> x2, waiting for transfers between devices: 0.01 us -> 38.4 us  [by_cell(): starts.append(lax.ppermute(narrow, 'genes', pairs))]
    pallas_call x2 -> x4, Pallas kernels: 8.93 us -> 20 us  [by_cell(): call(functools.partial(next_kernel, genes_here), (share, share, worst), (...]
    ppermute x6 -> x12, waiting for transfers between devices: 7.86 us -> 17 us  [swap(): return lax.ppermute(array, 'core', [(0, 1), (1, 0)])]
    all_to_all x1 -> x2, waiting for transfers between devices: 48.6 us -> 55.3 us  [by_cell(): moved = lax.all_to_all(moved, ('chips', 'core', 'genes'), 0, 0, tiled=True)]
    all_to_all x1 -> x2, starting transfers between devices: 4.93 us -> 10 us  [by_cell(): moved = lax.all_to_all(moved, ('chips', 'core', 'genes'), 0, 0, tiled=True)]
    unnamed x10 -> x12, local copies, waits for them, and re-layouts: 4.95 us -> 0.72 us
    pallas_call x1 -> x2, Pallas kernels: 4.48 us -> 8.18 us  [by_cell(): call(functools.partial(last_kernel, genes_here, slots), (jax.ShapeDtypeSt...]
  transfers between devices with their start and end apart: 8 -> 16, of which waited for: 7 -> 16; matrix products, arithmetic and copies ran while one was open for 0% -> 0% of each run, Pallas kernels for 2% -> 0%
where the time goes in v5:
time: 319 us; the launch traced here: 318 us
  blocking collectives  150 us (47%)
  waiting for transfers between devices  111 us (35%)
  Pallas kernels  40.4 us (13%)
  starting transfers between devices  14.6 us (5%)
    all_to_all x12, blocking collectives, exchange(): return lax.all_to_all(array, ('chips', 'genes'), 0, 0, tiled=True)  150 us
    all_to_all x2, waiting for transfers between devices, by_cell(): moved = lax.all_to_all(moved, ('chips', 'core', 'genes'), 0, 0, tiled=True)  55.3 us
    ppermute x2, waiting for transfers between devices, by_cell(): starts.append(lax.ppermute(narrow, 'genes', pairs))  38.4 us
    pallas_call x4, Pallas kernels, by_cell(): call(functools.partial(next_kernel, genes_here), (share, share, worst), (...  20 us
    ppermute x12, waiting for transfers between devices, swap(): return lax.ppermute(array, 'core', [(0, 1), (1, 0)])  17 us
    all_to_all x2, starting transfers between devices, by_cell(): moved = lax.all_to_all(moved, ('chips', 'core', 'genes'), 0, 0, tiled=True)  10 us
    pallas_call x2, Pallas kernels, by_cell(): call(functools.partial(last_kernel, genes_here, slots), (jax.ShapeDtypeSt...  8.18 us
  transfers between devices with their start and end apart: 16, of which 16 were waited for; matrix products, arithmetic and copies ran while one was open for 0% of the time, Pallas kernels for 0%

profile of v5, /device:TPU:0, one launch (start us, length us, event | category | flops | bytes accessed | tf_op | source)
XLA Modules:
  0.0 318.2 jit_solution(8267663778310038530)
XLA Ops:
  0.6 3.3 %shard_map.70 = bf16[32,32,1024]{2,1,0:T(8,128)(2,1)} custom-call(bf16[1000,1024]{1,0:T(8,128)(2,1)} %bitcast.10.data_any, s32[4,8]{1,0:T(4,128)} %dev_any.1, s32[4,8]{1,0:T(4,128)} %slot_any.1, s32[4,8]{1,0:T(4,128)} %weight_any.1), custom_call_target="tpu_custom_call" | custom-call | tf_op jit(solution)/shard_map/pallas_call | solution.py:468
  3.9 7.3 %all-to-all-start.7 = ((bf16[32,32,1024]{2,1,0:T(8,128)(2,1)}), bf16[32,32,1024]{2,1,0:T(8,128)(2,1)S(1)}, u32[]{:S(2)}, u32[]{:S(2)}) async-start(bf16[32,32,1024]{2,1,0:T(8,128)(2,1)} %shard_map.70), calls=%async_computation.7 | async-start | bytes 4194304 | tf_op jit(solution)/shard_map/all_to_all | solution.py:483
  11.3 1.8 collective-permute-start.7
  13.2 19.1 %collective-permute-done.7 = bf16[64,1024]{1,0:T(8,128)(2,1)S(1)} collective-permute-done((bf16[64,1024]{1,0:T(8,128)(2,1)S(1)}, bf16[64,1024]{1,0:T(8,128)(2,1)S(1)}, u32[]{:S(2)}, u32[]{:S(2)}) %collective-permute-start.7) | collective-permute-done | bytes 131104 | tf_op jit(solution)/shard_map/ppermute | solution.py:466
  32.4 27.6 %all-to-all-done.7 = bf16[32,32,1024]{2,1,0:T(8,128)(2,1)S(1)} async-done(((bf16[32,32,1024]{2,1,0:T(8,128)(2,1)}), bf16[32,32,1024]{2,1,0:T(8,128)(2,1)S(1)}, u32[]{:S(2)}, u32[]{:S(2)}) %all-to-all-start.7) | async-done | bytes 2097184 | tf_op jit(solution)/shard_map/all_to_all | solution.py:483
  60.0 2.8 shard_map.71
  64.2 12.3 %all_to_all.69.chunks_ref = bf16[16,32,128]{2,1,0:T(8,128)(2,1)S(1)} all-to-all(bf16[16,32,128]{2,1,0:T(8,128)(2,1)S(1)} %shard_map.72), channel_id=1, replica_groups=mesh['chips'=8,'core'=2,'genes'=2] {'chips','genes'}, dimensions={0} | all-to-all | bytes 262144 | tf_op jit(solution)/shard_map/all_to_all | solution.py:457
  76.5 10.7 %all_to_all.70.half_ref = bf16[16,32,128]{2,1,0:T(8,128)(2,1)S(1)} all-to-all(bf16[16,32,128]{2,1,0:T(8,128)(2,1)S(1)} %shard_map.73), channel_id=1, replica_groups=mesh['chips'=8,'core'=2,'genes'=2] {'chips','genes'}, dimensions={0} | all-to-all | bytes 262144 | tf_op jit(solution)/shard_map/all_to_all | solution.py:457
  88.6 4.1 %shard_map.74 = (bf16[16,32,128]{2,1,0:T(8,128)(2,1)S(1)}, bf16[16,32,128]{2,1,0:T(8,128)(2,1)S(1)}, f32[64,128]{1,0:T(8,128)S(1)}) custom-call(s32[2]{0:T(128)S(1)} %pad_add_fusion.1.place_ref, bf16[16,32,128]{2,1,0:T(8,128)(2,1)S(1)} %all_to_all.70.half_ref, bf16[16,32,128]{2,1,0:T(8,128)(2,1)S(1)} %collective-permute-done.9.rest_ref, ...), custom_call_target="tpu_custom_call" | custom-call | tf_op jit(solution)/shard_map/pallas_call | solution.py:516
  94.1 10.6 %all_to_all.71.chunks_ref = bf16[16,32,128]{2,1,0:T(8,128)(2,1)S(1)} all-to-all(bf16[16,32,128]{2,1,0:T(8,128)(2,1)S(1)} %shard_map.75), channel_id=1, replica_groups=mesh['chips'=8,'core'=2,'genes'=2] {'chips','genes'}, dimensions={0} | all-to-all | bytes 262144 | tf_op jit(solution)/shard_map/all_to_all | solution.py:457
  104.8 10.7 %all_to_all.72.half_ref = bf16[16,32,128]{2,1,0:T(8,128)(2,1)S(1)} all-to-all(bf16[16,32,128]{2,1,0:T(8,128)(2,1)S(1)} %shard_map.76), channel_id=1, replica_groups=mesh['chips'=8,'core'=2,'genes'=2] {'chips','genes'}, dimensions={0} | all-to-all | bytes 262144 | tf_op jit(solution)/shard_map/all_to_all | solution.py:457
  116.8 4.1 %shard_map.77 = (bf16[16,48,128]{2,1,0:T(8,128)(2,1)S(1)}, bf16[16,48,128]{2,1,0:T(8,128)(2,1)S(1)}, f32[64,128]{1,0:T(8,128)S(1)}) custom-call(s32[2]{0:T(128)S(1)} %pad_add_fusion.1.place_ref, bf16[16,32,128]{2,1,0:T(8,128)(2,1)S(1)} %all_to_all.72.half_ref, bf16[16,32,128]{2,1,0:T(8,128)(2,1)S(1)} %collective-permute-done.11.rest_ref, ...), custom_call_target="tpu_custom_call" | custom-call | tf_op jit(solution)/shard_map/pallas_call | solution.py:516
  122.5 11.5 %all_to_all.73.chunks_ref.arrived_ref = bf16[16,48,128]{2,1,0:T(8,128)(2,1)S(1)} all-to-all(bf16[16,48,128]{2,1,0:T(8,128)(2,1)S(1)} %shard_map.78), channel_id=1, replica_groups=mesh['chips'=8,'core'=2,'genes'=2] {'chips','genes'}, dimensions={0} | all-to-all | bytes 393216 | tf_op jit(solution)/shard_map/all_to_all | solution.py:457
  134.0 11.2 %all_to_all.74.half_ref = bf16[16,32,128]{2,1,0:T(8,128)(2,1)S(1)} all-to-all(bf16[16,32,128]{2,1,0:T(8,128)(2,1)S(1)} %shard_map.79), channel_id=1, replica_groups=mesh['chips'=8,'core'=2,'genes'=2] {'chips','genes'}, dimensions={0} | all-to-all | bytes 262144 | tf_op jit(solution)/shard_map/all_to_all | solution.py:457
  146.6 3.9 %shard_map.80 = (f32[64,1000]{1,0:T(8,128)S(1)}, bf16[32,1024]{1,0:T(8,128)(2,1)S(1)}, s32[1]{0:T(128)}) custom-call(s32[2]{0:T(128)S(1)} %pad_add_fusion.1.place_ref, bf16[16,32,128]{2,1,0:T(8,128)(2,1)S(1)} %all_to_all.74.half_ref, bf16[16,32,128]{2,1,0:T(8,128)(2,1)S(1)} %collective-permute-done.13.rest_ref, ...), custom_call_target="tpu_custom_call" | custom-call | tf_op jit(solution)/shard_map/pallas_call | solution.py:525
  151.1 166.3 %conditional.1 = (bf16[32,1024]{1,0:T(8,128)(2,1)S(1)}, f32[1000,64]{0,1:T(8,128)S(1)}) conditional(s32[]{:T(128)} %bitcast.15, (bf16[1024,1000]{0,1:T(8,128)(2,1)}, s32[4,8]{1,0:T(4,128)S(1)}, s32[4,8]{1,0:T(4,128)S(1)}, s32[4,8]{1,0:T(4,128)S(1)}, f32[1000,64]{0,1:T(8,128)S(1)}) %tuple.25, (f32[1000,64]{0,1:T(8,128)S(1)}, ...), branch_computations={%region_0.1_spmd, %region_1.2_spmd} | conditional | flops 195079 | bytes 18338188 | solution.py:541
  151.3 3.0 branch_0_fun.11
  154.3 2.7 all-to-all-start
  157.1 1.7 collective-permute-start
  158.9 19.2 %collective-permute-done = bf16[64,1024]{1,0:T(8,128)(2,1)S(1)} collective-permute-done((bf16[64,1024]{1,0:T(8,128)(2,1)S(1)}, bf16[64,1024]{1,0:T(8,128)(2,1)S(1)}, u32[]{:S(2)}, u32[]{:S(2)}) %collective-permute-start) | collective-permute-done | bytes 131104 | tf_op jit(solution)/shard_map/cond/branch_0_fun/ppermute | solution.py:466
  178.2 27.7 %all-to-all-done = bf16[32,32,1024]{2,1,0:T(8,128)(2,1)S(1)} async-done(((bf16[32,32,1024]{2,1,0:T(8,128)(2,1)}), bf16[32,32,1024]{2,1,0:T(8,128)(2,1)S(1)}, u32[]{:S(2)}, u32[]{:S(2)}) %all-to-all-start) | async-done | bytes 2097184 | tf_op jit(solution)/shard_map/cond/branch_0_fun/all_to_all | solution.py:483
  205.8 2.8 branch_0_fun.12
  210.2 14.5 %all_to_all.63.chunks_ref = f32[16,32,128]{2,1,0:T(8,128)S(1)} all-to-all(f32[16,32,128]{2,1,0:T(8,128)S(1)} %branch_0_fun.13), channel_id=1, replica_groups=mesh['chips'=8,'core'=2,'genes'=2] {'chips','genes'}, dimensions={0} | all-to-all | bytes 524288 | tf_op jit(solution)/shard_map/cond/branch_0_fun/all_to_all | solution.py:457
  224.8 12.8 %all_to_all.64.half_ref = f32[16,32,128]{2,1,0:T(8,128)S(1)} all-to-all(f32[16,32,128]{2,1,0:T(8,128)S(1)} %branch_0_fun.14), channel_id=1, replica_groups=mesh['chips'=8,'core'=2,'genes'=2] {'chips','genes'}, dimensions={0} | all-to-all | bytes 524288 | tf_op jit(solution)/shard_map/cond/branch_0_fun/all_to_all | solution.py:457
  239.1 5.9 %branch_0_fun.15 = (f32[16,32,128]{2,1,0:T(8,128)S(1)}, f32[16,32,128]{2,1,0:T(8,128)S(1)}, f32[64,128]{1,0:T(8,128)S(1)}) custom-call(s32[2]{0:T(128)S(1)} %pad_add_fusion.place_ref, f32[16,32,128]{2,1,0:T(8,128)S(1)} %all_to_all.64.half_ref, f32[16,32,128]{2,1,0:T(8,128)S(1)} %collective-permute-done.2.rest_ref, bf16[16,2,32,1024]{3,2,1,0:T(8,128)(2,1)S(1)} %bitcast.25, ...), custom_call_target="tpu_custom_call" | custom-call | tf_op jit(solution)/shard_map/cond/branch_0_fun/pallas_call | solution.py:516
  246.7 13.5 %all_to_all.65.chunks_ref = f32[16,32,128]{2,1,0:T(8,128)S(1)} all-to-all(f32[16,32,128]{2,1,0:T(8,128)S(1)} %branch_0_fun.16), channel_id=1, replica_groups=mesh['chips'=8,'core'=2,'genes'=2] {'chips','genes'}, dimensions={0} | all-to-all | bytes 524288 | tf_op jit(solution)/shard_map/cond/branch_0_fun/all_to_all | solution.py:457
  260.3 12.8 %all_to_all.66.half_ref = f32[16,32,128]{2,1,0:T(8,128)S(1)} all-to-all(f32[16,32,128]{2,1,0:T(8,128)S(1)} %branch_0_fun.17), channel_id=1, replica_groups=mesh['chips'=8,'core'=2,'genes'=2] {'chips','genes'}, dimensions={0} | all-to-all | bytes 524288 | tf_op jit(solution)/shard_map/cond/branch_0_fun/all_to_all | solution.py:457
  274.6 6.0 %branch_0_fun.18 = (f32[16,48,128]{2,1,0:T(8,128)S(1)}, f32[16,48,128]{2,1,0:T(8,128)S(1)}, f32[64,128]{1,0:T(8,128)S(1)}) custom-call(s32[2]{0:T(128)S(1)} %pad_add_fusion.place_ref, f32[16,32,128]{2,1,0:T(8,128)S(1)} %all_to_all.66.half_ref, f32[16,32,128]{2,1,0:T(8,128)S(1)} %collective-permute-done.4.rest_ref, bf16[16,2,32,1024]{3,2,1,0:T(8,128)(2,1)S(1)} %bitcast.26, ...), custom_call_target="tpu_custom_call" | custom-call | tf_op jit(solution)/shard_map/cond/branch_0_fun/pallas_call | solution.py:516
  280.7 1.6 collective-permute-done.5.arrived_ref
  282.4 16.2 %all_to_all.67.chunks_ref.arrived_ref = f32[16,48,128]{2,1,0:T(8,128)S(1)} all-to-all(f32[16,48,128]{2,1,0:T(8,128)S(1)} %branch_0_fun.19), channel_id=1, replica_groups=mesh['chips'=8,'core'=2,'genes'=2] {'chips','genes'}, dimensions={0} | all-to-all | bytes 786432 | tf_op jit(solution)/shard_map/cond/branch_0_fun/all_to_all | solution.py:457
  298.6 12.7 %all_to_all.68.half_ref = f32[16,32,128]{2,1,0:T(8,128)S(1)} all-to-all(f32[16,32,128]{2,1,0:T(8,128)S(1)} %branch_0_fun.20), channel_id=1, replica_groups=mesh['chips'=8,'core'=2,'genes'=2] {'chips','genes'}, dimensions={0} | all-to-all | bytes 524288 | tf_op jit(solution)/shard_map/cond/branch_0_fun/all_to_all | solution.py:457
  312.9 4.3 %branch_0_fun.21 = (f32[64,1000]{1,0:T(8,128)S(1)}, bf16[32,1024]{1,0:T(8,128)(2,1)S(1)}, s32[1]{0:T(128)}) custom-call(s32[2]{0:T(128)S(1)} %pad_add_fusion.place_ref, f32[16,32,128]{2,1,0:T(8,128)S(1)} %all_to_all.68.half_ref, f32[16,32,128]{2,1,0:T(8,128)S(1)} %collective-permute-done.6.rest_ref, f32[16,48,128]{2,1,0:T(8,128)S(1)} %all_to_all.67.chunks_ref.arrived_ref, ...), custom_call_target="tpu_custom_call" | custom-call | tf_op jit(solution)/shard_map/cond/branch_0_fun/pallas_call | solution.py:525
  (55 shorter events, 17.8 us)
Async XLA Ops:
  3.9 7.3 %copy-start = (f32[1000,64]{0,1:T(8,128)S(1)}, f32[1000,64]{0,1:T(8,128)}, u32[]{:S(2)}) copy-start(f32[1000,64]{0,1:T(8,128)} %param.8) | copy-start | bytes 768004
  3.9 56.1 %all-to-all-start.7 = ((bf16[32,32,1024]{2,1,0:T(8,128)(2,1)}), bf16[32,32,1024]{2,1,0:T(8,128)(2,1)S(1)}, u32[]{:S(2)}, u32[]{:S(2)}) async-start(bf16[32,32,1024]{2,1,0:T(8,128)(2,1)} %shard_map.70), calls=%async_computation.7 | async-start | bytes 4194304 | tf_op jit(solution)/shard_map/all_to_all | solution.py:483
  11.3 21.0 %collective-permute-start.7 = (bf16[64,1024]{1,0:T(8,128)(2,1)S(1)}, bf16[64,1024]{1,0:T(8,128)(2,1)S(1)}, u32[]{:S(2)}, u32[]{:S(2)}) collective-permute-start(bf16[64,1024]{1,0:T(8,128)(2,1)S(1)} %get-tuple-element.65), channel_id=1, source_target_pairs={{0,1},{1,0},{2,3},{3,2},{4,5},{5,4},{6,7},{7,6},{8,9},{9,8},{10,11... | collective-permute-start | bytes 393224 | tf_op jit(solution)/shard_map/ppermute | solution.py:466
  62.8 1.4 collective-permute-start.8
  87.2 1.3 collective-permute-start.9
  92.7 1.4 collective-permute-start.10
  115.5 35.6 %copy-start.1 = (s32[4,8]{1,0:T(4,128)S(1)}, s32[4,8]{1,0:T(4,128)}, u32[]{:S(2)}) copy-start(s32[4,8]{1,0:T(4,128)} %dev_any.1) | copy-start | bytes 388
  115.5 35.7 %copy-start.2 = (s32[4,8]{1,0:T(4,128)S(1)}, s32[4,8]{1,0:T(4,128)}, u32[]{:S(2)}) copy-start(s32[4,8]{1,0:T(4,128)} %slot_any.1) | copy-start | bytes 388
  115.5 35.7 %copy-start.3 = (s32[4,8]{1,0:T(4,128)S(1)}, s32[4,8]{1,0:T(4,128)}, u32[]{:S(2)}) copy-start(s32[4,8]{1,0:T(4,128)} %weight_any.1) | copy-start | bytes 388
  115.5 1.3 collective-permute-start.11
  120.9 1.5 collective-permute-start.12
  145.2 1.3 collective-permute-start.13
  154.3 51.5 %all-to-all-start = ((bf16[32,32,1024]{2,1,0:T(8,128)(2,1)}), bf16[32,32,1024]{2,1,0:T(8,128)(2,1)S(1)}, u32[]{:S(2)}, u32[]{:S(2)}) async-start(bf16[32,32,1024]{2,1,0:T(8,128)(2,1)} %branch_0_fun.11), calls=%async_computation | async-start | bytes 4194304 | tf_op jit(solution)/shard_map/cond/branch_0_fun/all_to_all | solution.py:483
  157.1 21.0 %collective-permute-start = (bf16[64,1024]{1,0:T(8,128)(2,1)S(1)}, bf16[64,1024]{1,0:T(8,128)(2,1)S(1)}, u32[]{:S(2)}, u32[]{:S(2)}) collective-permute-start(bf16[64,1024]{1,0:T(8,128)(2,1)S(1)} %get-tuple-element.63), channel_id=1, source_target_pairs={{0,1},{1,0},{2,3},{3,2},{4,5},{5,4},{6,7},{7,6},{8,9},{9,8},{10,11... | collective-permute-start | bytes 393224 | tf_op jit(solution)/shard_map/cond/branch_0_fun/ppermute | solution.py:466
  208.6 1.6 collective-permute-start.1
  237.6 1.5 collective-permute-start.2
  245.1 1.6 collective-permute-start.3
  273.0 1.5 collective-permute-start.4
  280.5 1.8 collective-permute-start.5
  311.4 1.5 collective-permute-start.6
  317.5 0.7 copy-start.4
  317.5 0.7 copy-start.5

commit v6 on v5

--- a/solution.py
+++ b/solution.py
@@ -47,25 +47,24 @@
         rest = {(at, j): column(strips[at], j) for at in below for j in range(8)}
         for j in range(0, 8, 2):
             a, b, c = core[j, j], core[j + 1, j], core[j + 1, j + 1]
-            inverse = 1.0 / (a * c - b * b)
-            step = b * (1.0 / a)
-            ia, ib, ic = c * inverse, b * inverse, a * inverse
-
-            def factors(first, second):
-                return first * ia - second * ib, second * ic - first * ib
-
+            area = a * c - b * b
+            over = 1.0 / a
+            step = b * over
+            later = a * (1.0 / area)
+            left = {i: core[i, j + 1] - step * core[i, j] for i in range(j + 2, 8)}
+            lines[j + 1] -= step * lines[j]
+            core[j + 1, j + 1] = area * over
             for i in range(j + 2, 8):
-                first, second = factors(core[i, j], core[i, j + 1])
+                first, second = core[i, j] * over, left[i] * later
                 for m in range(j + 2, i + 1):
-                    core[i, m] -= first * core[m, j] + second * core[m, j + 1]
+                    core[i, m] -= first * core[m, j] + second * left[m]
                 lines[i] -= first * lines[j] + second * lines[j + 1]
             for at in below:
-                first, second = factors(rest[at, j], rest[at, j + 1])
+                first = rest[at, j] * over
+                second = (rest[at, j + 1] - step * rest[at, j]) * later
                 for m in range(j + 2, 8):
-                    rest[at, m] -= first * core[m, j] + second * core[m, j + 1]
+                    rest[at, m] -= first * core[m, j] + second * left[m]
                 strips[at] -= first * lines[j] + second * lines[j + 1]
-            lines[j + 1] -= step * lines[j]
-            core[j + 1, j + 1] = c - step * b
         final = lines[0] * lax.rsqrt(core[0, 0])
         for j in range(1, 8):
             final = jnp.where(place == j, lines[j] * lax.rsqrt(core[j, j]), final)
@@ -120,20 +119,21 @@
     return part.reshape(part.shape[0] * part.shape[1], part.shape[2])
 
 
-def push_update(genes_here, data_ref, second, cut_ref):
+def push_update(core, genes_here, data_ref, second, mine_ref, other_ref):
     groups, padded = data_ref.shape[1], data_ref.shape[3]
-    cores = cut_ref.shape[0]
-    chunk = second.shape[0] // cores
+    chunk = second.shape[0] // 2
     blocks = padded // LANES
     for group in range(groups):
         update = jnp.dot(second, block(data_ref, group), preferred_element_type=jnp.float32)
         lane = lax.broadcasted_iota(jnp.int32, update.shape, 1)
-        update = jnp.where(lane < genes_here, update, 0.0).astype(cut_ref.dtype)
+        update = jnp.where(lane < genes_here, update, 0.0)
+        upper, lower = update[:chunk], update[chunk:]
+        mine = jnp.where(core == 0, upper, lower).astype(mine_ref.dtype)
+        other = jnp.where(core == 0, lower, upper).astype(mine_ref.dtype)
         for at in range(blocks):
-            for core in range(cores):
-                cut_ref[core, group * blocks + at, :chunk] = update[
-                    core * chunk : (core + 1) * chunk, at * LANES : (at + 1) * LANES
-                ]
+            lanes = slice(at * LANES, (at + 1) * LANES)
+            mine_ref[group * blocks + at, :chunk] = mine[:, lanes]
+            other_ref[group * blocks + at, :chunk] = other[:, lanes]
 
 
 def pull_update(core, mine_ref, other_ref, update_ref):
@@ -210,35 +210,38 @@
         pltpu.make_async_copy(data_any.at[:, at], data_ref.at[:, at], data_sem.at[tile])
         for tile, at in enumerate(tile_at)
     ]
-    for copy in link_copies + data_copies:
+    for copy in data_copies[:1] + link_copies + data_copies[1:]:
         copy.start()
 
-    spread = (
-        lax.broadcasted_iota(jnp.int32, (neighbours, cells), 0)
-        == lax.broadcasted_iota(jnp.int32, (neighbours, cells), 1) % rows_of
-    ).astype(jnp.float32)
-    tile = lax.broadcasted_iota(jnp.int32, (slots, cells), 0)
-    own_tile = tile == lax.broadcasted_iota(jnp.int32, (slots, cells), 1) // tile_cells
-    row = lax.broadcasted_iota(jnp.int32, (padded - genes_here, cells), 0)
-    links = jnp.zeros((padded - genes_here, cells), jnp.float32)
-    for at, copy in enumerate(link_copies):
-        copy.wait()
-        wide = jnp.dot(
-            link_ref[at].astype(jnp.float32), spread, preferred_element_type=jnp.float32
-        )
-        wide = jnp.sum(jnp.where(own_tile, wide, 0.0), axis=0, keepdims=True)
-        links = jnp.where(row == at, wide, links)
+    def wide_links():
+        spread = (
+            lax.broadcasted_iota(jnp.int32, (neighbours, cells), 0)
+            == lax.broadcasted_iota(jnp.int32, (neighbours, cells), 1) % rows_of
+        ).astype(jnp.float32)
+        tile = lax.broadcasted_iota(jnp.int32, (slots, cells), 0)
+        own_tile = tile == lax.broadcasted_iota(jnp.int32, (slots, cells), 1) // tile_cells
+        row = lax.broadcasted_iota(jnp.int32, (padded - genes_here, cells), 0)
+        links = jnp.zeros((padded - genes_here, cells), jnp.float32)
+        for at, copy in enumerate(link_copies):
+            copy.wait()
+            wide = jnp.dot(
+                link_ref[at].astype(jnp.float32), spread, preferred_element_type=jnp.float32
+            )
+            wide = jnp.sum(jnp.where(own_tile, wide, 0.0), axis=0, keepdims=True)
+            links = jnp.where(row == at, wide, links)
+        return links
 
     def turned(part):
         return part.T.astype(jnp.float32).reshape(parts, rows_of, part.shape[0])
 
-    out_copies = []
+    out_copies, links = [], None
     for first in range(0, slots, joined):
         main, rest = [], []
         for tile in range(first, first + joined):
             data_copies[tile].wait()
             at = slice(tile * tile_cells, (tile + 1) * tile_cells)
             main.append(turned(data_ref[:whole, at]))
+            links = wide_links() if links is None else links
             end = data_ref[whole:genes_here, at].astype(jnp.float32)
             end = jnp.concatenate([end, links[:, at]], axis=0)
             rest.append(turned(end.astype(jnp.bfloat16)))
@@ -256,15 +259,17 @@
         copy.wait()
 
 
-def share_second(core, second, cut_ref, chunk, groups):
+def share_second(core, second, mine_ref, other_ref, chunk, groups):
     width, cells = second.shape
-    cores, blocks, tall = cut_ref.shape[:3]
+    blocks, tall = mine_ref.shape[:2]
+    cores = 2
     rows = cells * groups // (cores * blocks)
     tall = tall - chunk
     slabs = width // groups // tall
     lane = lax.broadcasted_iota(jnp.int32, (tall, LANES), 1) // rows - core * slabs
     for at in range(cells // LANES):
         wide = second[:, at * LANES : (at + 1) * LANES].astype(jnp.float32)
+        shares = []
         for group in range(groups):
             for device in range(LANES // rows):
                 share = jnp.zeros((tall, LANES), jnp.float32)
@@ -277,8 +282,15 @@
                             1,
                         )
                         share = jnp.where((lane == slab) & (core == turn), turned, share)
-                chip, to = divmod(at * (LANES // rows) + device, cores)
-                cut_ref[to, chip * groups + group, chunk:] = share.astype(cut_ref.dtype)
+                shares.append(share.astype(mine_ref.dtype))
+        for device in range(0, LANES // rows, cores):
+            chip = (at * (LANES // rows) + device) // cores
+            for group in range(groups):
+                first = shares[group * (LANES // rows) + device]
+                second_core = shares[group * (LANES // rows) + device + 1]
+                to = chip * groups + group
+                mine_ref[to, chunk:] = jnp.where(core == 0, first, second_core)
+                other_ref[to, chunk:] = jnp.where(core == 0, second_core, first)
 
 
 def order_shares(arrived_ref, chunk, out_ref, groups, cores, slots):
@@ -318,7 +330,6 @@
     other_ref,
     links_ref,
     degree_ref,
-    cut_ref,
 ):
     devices, groups, rows, padded = data_ref.shape
     tiles = devices * slots
@@ -334,9 +345,7 @@
     scores = score(lambda shift: start_ref[shift], data_ref, order)
     scores = scores / math.sqrt(genes_here * groups)
     second = diffuse(scores, links, degree[:1])
-    push_update(genes_here, data_ref, second, cut_ref)
-    mine_ref[...] = cut_ref[core]
-    other_ref[...] = cut_ref[1 - core]
+    push_update(core, genes_here, data_ref, second, mine_ref, other_ref)
 
 
 def next_kernel(
@@ -351,7 +360,6 @@
     other_ref,
     worst_ref,
     update_ref,
-    cut_ref,
 ):
     core = place_ref[0]
     groups = data_ref.shape[1]
@@ -375,11 +383,9 @@
             score(lambda group: columns_of(update_ref, group), data_ref, range(groups))
         )
     second = diffuse(scores / math.sqrt(genes_total), links_ref[...], degree_ref[:1])
-    push_update(genes_here, data_ref, second, cut_ref)
-    if cut_ref.shape[2] > chunk:
-        share_second(core, second, cut_ref, chunk, groups)
-    mine_ref[...] = cut_ref[core]
-    other_ref[...] = cut_ref[1 - core]
+    push_update(core, genes_here, data_ref, second, mine_ref, other_ref)
+    if mine_ref.shape[1] > chunk:
+        share_second(core, second, mine_ref, other_ref, chunk, groups)
 
 
 def last_kernel(
@@ -484,10 +490,7 @@
     moved = moved.reshape(devices, groups, rows, padded)
 
     def cut(tall):
-        return (
-            jax.ShapeDtypeStruct((blocks, tall, LANES), kept),
-            pltpu.VMEM((cores, blocks, tall, LANES), kept),
-        )
+        return jax.ShapeDtypeStruct((blocks, tall, LANES), kept)
 
     update = pltpu.VMEM((groups, cores, chunk, padded), kept)
     worst = jax.ShapeDtypeStruct((width, LANES), jnp.float32)
@@ -499,24 +502,23 @@
         return exchange(call(add_kernel, like(mine), arrays=2)(mine, swap(other)))
 
     def gather(arrived):
-        half = exchange(call(sum_kernel, cut(chunk)[0], arrays=1)(arrived))
+        half = exchange(call(sum_kernel, cut(chunk), arrays=1)(arrived))
         return half, swap(half)
 
-    share, scratch = cut(chunk)
+    share = cut(chunk)
     mine, other, links, degree = call(
         functools.partial(first_kernel, genes_here, slots),
         (share, share, links, degree),
-        (scratch,),
         scalars=1,
         arrays=2,
     )(place, moved, starts)
     arrived = reduce(mine, other)
     for step in range(1, ITERS):
-        share, scratch = cut(chunk + 16 if step == ITERS - 1 else chunk)
+        share = cut(chunk + 16 if step == ITERS - 1 else chunk)
         mine, other, amplified = call(
             functools.partial(next_kernel, genes_here),
             (share, share, worst),
-            (update, scratch),
+            (update,),
             scalars=1,
             arrays=5,
         )(place, *gather(arrived), moved, links, degree)

time: 319 us -> 318 us (level)
  no operation moved by 1% of the time
where the time goes in v6:
time: 318 us
  blocking collectives  150 us (47%)
  waiting for transfers between devices  111 us (35%)
  Pallas kernels  39.9 us (13%)
  starting transfers between devices  14.6 us (5%)
    all_to_all x12, blocking collectives, exchange(): return lax.all_to_all(array, ('chips', 'genes'), 0, 0, tiled=True)  150 us
    all_to_all x2, waiting for transfers between devices, by_cell(): moved = lax.all_to_all(moved, ('chips', 'core', 'genes'), 0, 0, tiled=True)  55.3 us
    ppermute x2, waiting for transfers between devices, by_cell(): starts.append(lax.ppermute(narrow, 'genes', pairs))  38.4 us
    pallas_call x4, Pallas kernels, by_cell(): call(functools.partial(next_kernel, genes_here), (share, share, worst), (...  19.5 us
    ppermute x12, waiting for transfers between devices, swap(): return lax.ppermute(array, 'core', [(0, 1), (1, 0)])  17 us
    all_to_all x2, starting transfers between devices, by_cell(): moved = lax.all_to_all(moved, ('chips', 'core', 'genes'), 0, 0, tiled=True)  10 us
    pallas_call x2, Pallas kernels, by_cell(): call(functools.partial(last_kernel, genes_here, slots), (jax.ShapeDtypeSt...  7.69 us
    pallas_call x2, Pallas kernels, by_cell(): pl.pallas_call(functools.partial(regroup_kernel, rows_of), out_shape=jax....  6.77 us
  transfers between devices with their start and end apart: 16, of which 16 were waited for; matrix products, arithmetic and copies ran while one was open for 0% of the time, Pallas kernels for 0%

profile of v6, /device:TPU:0, one launch (start us, length us, event | category | flops | bytes accessed | tf_op | source)
XLA Modules:
  0.0 317.7 jit_solution(4513316625824096196)
XLA Ops:
  0.6 3.4 %shard_map.70 = bf16[32,32,1024]{2,1,0:T(8,128)(2,1)} custom-call(bf16[1000,1024]{1,0:T(8,128)(2,1)} %bitcast.10.data_any, s32[4,8]{1,0:T(4,128)} %dev_any.1, s32[4,8]{1,0:T(4,128)} %slot_any.1, s32[4,8]{1,0:T(4,128)} %weight_any.1), custom_call_target="tpu_custom_call" | custom-call | tf_op jit(solution)/shard_map/pallas_call | solution.py:474
  4.0 7.3 %all-to-all-start.7 = ((bf16[32,32,1024]{2,1,0:T(8,128)(2,1)}), bf16[32,32,1024]{2,1,0:T(8,128)(2,1)S(1)}, u32[]{:S(2)}, u32[]{:S(2)}) async-start(bf16[32,32,1024]{2,1,0:T(8,128)(2,1)} %shard_map.70), calls=%async_computation.7 | async-start | bytes 4194304 | tf_op jit(solution)/shard_map/all_to_all | solution.py:489
  11.4 1.8 collective-permute-start.7
  13.3 19.1 %collective-permute-done.7 = bf16[64,1024]{1,0:T(8,128)(2,1)S(1)} collective-permute-done((bf16[64,1024]{1,0:T(8,128)(2,1)S(1)}, bf16[64,1024]{1,0:T(8,128)(2,1)S(1)}, u32[]{:S(2)}, u32[]{:S(2)}) %collective-permute-start.7) | collective-permute-done | bytes 131104 | tf_op jit(solution)/shard_map/ppermute | solution.py:472
  32.5 27.6 %all-to-all-done.7 = bf16[32,32,1024]{2,1,0:T(8,128)(2,1)S(1)} async-done(((bf16[32,32,1024]{2,1,0:T(8,128)(2,1)}), bf16[32,32,1024]{2,1,0:T(8,128)(2,1)S(1)}, u32[]{:S(2)}, u32[]{:S(2)}) %all-to-all-start.7) | async-done | bytes 2097184 | tf_op jit(solution)/shard_map/all_to_all | solution.py:489
  60.1 2.8 shard_map.71
  64.4 12.2 %all_to_all.69.chunks_ref = bf16[16,32,128]{2,1,0:T(8,128)(2,1)S(1)} all-to-all(bf16[16,32,128]{2,1,0:T(8,128)(2,1)S(1)} %shard_map.72), channel_id=1, replica_groups=mesh['chips'=8,'core'=2,'genes'=2] {'chips','genes'}, dimensions={0} | all-to-all | bytes 262144 | tf_op jit(solution)/shard_map/all_to_all | solution.py:463
  76.6 10.7 %all_to_all.70.half_ref = bf16[16,32,128]{2,1,0:T(8,128)(2,1)S(1)} all-to-all(bf16[16,32,128]{2,1,0:T(8,128)(2,1)S(1)} %shard_map.73), channel_id=1, replica_groups=mesh['chips'=8,'core'=2,'genes'=2] {'chips','genes'}, dimensions={0} | all-to-all | bytes 262144 | tf_op jit(solution)/shard_map/all_to_all | solution.py:463
  88.7 3.9 %shard_map.74 = (bf16[16,32,128]{2,1,0:T(8,128)(2,1)S(1)}, bf16[16,32,128]{2,1,0:T(8,128)(2,1)S(1)}, f32[64,128]{1,0:T(8,128)S(1)}) custom-call(s32[2]{0:T(128)S(1)} %pad_add_fusion.1.place_ref, bf16[16,32,128]{2,1,0:T(8,128)(2,1)S(1)} %all_to_all.70.half_ref, bf16[16,32,128]{2,1,0:T(8,128)(2,1)S(1)} %collective-permute-done.9.rest_ref, ...), custom_call_target="tpu_custom_call" | custom-call | tf_op jit(solution)/shard_map/pallas_call | solution.py:518
  94.1 10.6 %all_to_all.71.chunks_ref = bf16[16,32,128]{2,1,0:T(8,128)(2,1)S(1)} all-to-all(bf16[16,32,128]{2,1,0:T(8,128)(2,1)S(1)} %shard_map.75), channel_id=1, replica_groups=mesh['chips'=8,'core'=2,'genes'=2] {'chips','genes'}, dimensions={0} | all-to-all | bytes 262144 | tf_op jit(solution)/shard_map/all_to_all | solution.py:463
  104.8 10.7 %all_to_all.72.half_ref = bf16[16,32,128]{2,1,0:T(8,128)(2,1)S(1)} all-to-all(bf16[16,32,128]{2,1,0:T(8,128)(2,1)S(1)} %shard_map.76), channel_id=1, replica_groups=mesh['chips'=8,'core'=2,'genes'=2] {'chips','genes'}, dimensions={0} | all-to-all | bytes 262144 | tf_op jit(solution)/shard_map/all_to_all | solution.py:463
  116.8 3.9 %shard_map.77 = (bf16[16,48,128]{2,1,0:T(8,128)(2,1)S(1)}, bf16[16,48,128]{2,1,0:T(8,128)(2,1)S(1)}, f32[64,128]{1,0:T(8,128)S(1)}) custom-call(s32[2]{0:T(128)S(1)} %pad_add_fusion.1.place_ref, bf16[16,32,128]{2,1,0:T(8,128)(2,1)S(1)} %all_to_all.72.half_ref, bf16[16,32,128]{2,1,0:T(8,128)(2,1)S(1)} %collective-permute-done.11.rest_ref, ...), custom_call_target="tpu_custom_call" | custom-call | tf_op jit(solution)/shard_map/pallas_call | solution.py:518
  122.3 11.5 %all_to_all.73.chunks_ref.arrived_ref = bf16[16,48,128]{2,1,0:T(8,128)(2,1)S(1)} all-to-all(bf16[16,48,128]{2,1,0:T(8,128)(2,1)S(1)} %shard_map.78), channel_id=1, replica_groups=mesh['chips'=8,'core'=2,'genes'=2] {'chips','genes'}, dimensions={0} | all-to-all | bytes 393216 | tf_op jit(solution)/shard_map/all_to_all | solution.py:463
  133.9 11.2 %all_to_all.74.half_ref = bf16[16,32,128]{2,1,0:T(8,128)(2,1)S(1)} all-to-all(bf16[16,32,128]{2,1,0:T(8,128)(2,1)S(1)} %shard_map.79), channel_id=1, replica_groups=mesh['chips'=8,'core'=2,'genes'=2] {'chips','genes'}, dimensions={0} | all-to-all | bytes 262144 | tf_op jit(solution)/shard_map/all_to_all | solution.py:463
  146.4 3.5 %shard_map.80 = (f32[64,1000]{1,0:T(8,128)S(1)}, bf16[32,1024]{1,0:T(8,128)(2,1)S(1)}, s32[1]{0:T(128)}) custom-call(s32[2]{0:T(128)S(1)} %pad_add_fusion.1.place_ref, bf16[16,32,128]{2,1,0:T(8,128)(2,1)S(1)} %all_to_all.74.half_ref, bf16[16,32,128]{2,1,0:T(8,128)(2,1)S(1)} %collective-permute-done.13.rest_ref, ...), custom_call_target="tpu_custom_call" | custom-call | tf_op jit(solution)/shard_map/pallas_call | solution.py:527
  150.6 166.3 %conditional.1 = (bf16[32,1024]{1,0:T(8,128)(2,1)S(1)}, f32[1000,64]{0,1:T(8,128)S(1)}) conditional(s32[]{:T(128)} %bitcast.15, (bf16[1024,1000]{0,1:T(8,128)(2,1)}, s32[4,8]{1,0:T(4,128)S(1)}, s32[4,8]{1,0:T(4,128)S(1)}, s32[4,8]{1,0:T(4,128)S(1)}, f32[1000,64]{0,1:T(8,128)S(1)}) %tuple.25, (f32[1000,64]{0,1:T(8,128)S(1)}, ...), branch_computations={%region_0.1_spmd, %region_1.2_spmd} | conditional | flops 195079 | bytes 18338188 | solution.py:543
  150.8 3.4 %branch_0_fun.11 = bf16[32,32,1024]{2,1,0:T(8,128)(2,1)} custom-call(bf16[1000,1024]{1,0:T(8,128)(2,1)} %bitcast.2.data_any, s32[4,8]{1,0:T(4,128)S(1)} %get-tuple-element.15.dev_any, s32[4,8]{1,0:T(4,128)S(1)} %get-tuple-element.16.slot_any, s32[4,8]{1,0:T(4,128)S(1)} %get-tuple-element.17.weight_any), custom_call_target="tpu_custom_call" | custom-call | tf_op jit(solution)/shard_map/cond/branch_0_fun/pallas_call | solution.py:474
  154.2 2.7 all-to-all-start
  157.0 1.7 collective-permute-start
  158.8 19.2 %collective-permute-done = bf16[64,1024]{1,0:T(8,128)(2,1)S(1)} collective-permute-done((bf16[64,1024]{1,0:T(8,128)(2,1)S(1)}, bf16[64,1024]{1,0:T(8,128)(2,1)S(1)}, u32[]{:S(2)}, u32[]{:S(2)}) %collective-permute-start) | collective-permute-done | bytes 131104 | tf_op jit(solution)/shard_map/cond/branch_0_fun/ppermute | solution.py:472
  178.0 27.7 %all-to-all-done = bf16[32,32,1024]{2,1,0:T(8,128)(2,1)S(1)} async-done(((bf16[32,32,1024]{2,1,0:T(8,128)(2,1)}), bf16[32,32,1024]{2,1,0:T(8,128)(2,1)S(1)}, u32[]{:S(2)}, u32[]{:S(2)}) %all-to-all-start) | async-done | bytes 2097184 | tf_op jit(solution)/shard_map/cond/branch_0_fun/all_to_all | solution.py:489
  205.7 2.8 branch_0_fun.12
  210.1 14.5 %all_to_all.63.chunks_ref = f32[16,32,128]{2,1,0:T(8,128)S(1)} all-to-all(f32[16,32,128]{2,1,0:T(8,128)S(1)} %branch_0_fun.13), channel_id=1, replica_groups=mesh['chips'=8,'core'=2,'genes'=2] {'chips','genes'}, dimensions={0} | all-to-all | bytes 524288 | tf_op jit(solution)/shard_map/cond/branch_0_fun/all_to_all | solution.py:463
  224.7 12.8 %all_to_all.64.half_ref = f32[16,32,128]{2,1,0:T(8,128)S(1)} all-to-all(f32[16,32,128]{2,1,0:T(8,128)S(1)} %branch_0_fun.14), channel_id=1, replica_groups=mesh['chips'=8,'core'=2,'genes'=2] {'chips','genes'}, dimensions={0} | all-to-all | bytes 524288 | tf_op jit(solution)/shard_map/cond/branch_0_fun/all_to_all | solution.py:463
  239.0 5.8 %branch_0_fun.15 = (f32[16,32,128]{2,1,0:T(8,128)S(1)}, f32[16,32,128]{2,1,0:T(8,128)S(1)}, f32[64,128]{1,0:T(8,128)S(1)}) custom-call(s32[2]{0:T(128)S(1)} %pad_add_fusion.place_ref, f32[16,32,128]{2,1,0:T(8,128)S(1)} %all_to_all.64.half_ref, f32[16,32,128]{2,1,0:T(8,128)S(1)} %collective-permute-done.2.rest_ref, bf16[16,2,32,1024]{3,2,1,0:T(8,128)(2,1)S(1)} %bitcast.25, ...), custom_call_target="tpu_custom_call" | custom-call | tf_op jit(solution)/shard_map/cond/branch_0_fun/pallas_call | solution.py:518
  246.4 13.5 %all_to_all.65.chunks_ref = f32[16,32,128]{2,1,0:T(8,128)S(1)} all-to-all(f32[16,32,128]{2,1,0:T(8,128)S(1)} %branch_0_fun.16), channel_id=1, replica_groups=mesh['chips'=8,'core'=2,'genes'=2] {'chips','genes'}, dimensions={0} | all-to-all | bytes 524288 | tf_op jit(solution)/shard_map/cond/branch_0_fun/all_to_all | solution.py:463
  260.0 12.8 %all_to_all.66.half_ref = f32[16,32,128]{2,1,0:T(8,128)S(1)} all-to-all(f32[16,32,128]{2,1,0:T(8,128)S(1)} %branch_0_fun.17), channel_id=1, replica_groups=mesh['chips'=8,'core'=2,'genes'=2] {'chips','genes'}, dimensions={0} | all-to-all | bytes 524288 | tf_op jit(solution)/shard_map/cond/branch_0_fun/all_to_all | solution.py:463
  274.3 5.8 %branch_0_fun.18 = (f32[16,48,128]{2,1,0:T(8,128)S(1)}, f32[16,48,128]{2,1,0:T(8,128)S(1)}, f32[64,128]{1,0:T(8,128)S(1)}) custom-call(s32[2]{0:T(128)S(1)} %pad_add_fusion.place_ref, f32[16,32,128]{2,1,0:T(8,128)S(1)} %all_to_all.66.half_ref, f32[16,32,128]{2,1,0:T(8,128)S(1)} %collective-permute-done.4.rest_ref, bf16[16,2,32,1024]{3,2,1,0:T(8,128)(2,1)S(1)} %bitcast.26, ...), custom_call_target="tpu_custom_call" | custom-call | tf_op jit(solution)/shard_map/cond/branch_0_fun/pallas_call | solution.py:518
  280.3 1.6 collective-permute-done.5.arrived_ref
  281.9 16.2 %all_to_all.67.chunks_ref.arrived_ref = f32[16,48,128]{2,1,0:T(8,128)S(1)} all-to-all(f32[16,48,128]{2,1,0:T(8,128)S(1)} %branch_0_fun.19), channel_id=1, replica_groups=mesh['chips'=8,'core'=2,'genes'=2] {'chips','genes'}, dimensions={0} | all-to-all | bytes 786432 | tf_op jit(solution)/shard_map/cond/branch_0_fun/all_to_all | solution.py:463
  298.2 12.7 %all_to_all.68.half_ref = f32[16,32,128]{2,1,0:T(8,128)S(1)} all-to-all(f32[16,32,128]{2,1,0:T(8,128)S(1)} %branch_0_fun.20), channel_id=1, replica_groups=mesh['chips'=8,'core'=2,'genes'=2] {'chips','genes'}, dimensions={0} | all-to-all | bytes 524288 | tf_op jit(solution)/shard_map/cond/branch_0_fun/all_to_all | solution.py:463
  312.5 4.2 %branch_0_fun.21 = (f32[64,1000]{1,0:T(8,128)S(1)}, bf16[32,1024]{1,0:T(8,128)(2,1)S(1)}, s32[1]{0:T(128)}) custom-call(s32[2]{0:T(128)S(1)} %pad_add_fusion.place_ref, f32[16,32,128]{2,1,0:T(8,128)S(1)} %all_to_all.68.half_ref, f32[16,32,128]{2,1,0:T(8,128)S(1)} %collective-permute-done.6.rest_ref, f32[16,48,128]{2,1,0:T(8,128)S(1)} %all_to_all.67.chunks_ref.arrived_ref, ...), custom_call_target="tpu_custom_call" | custom-call | tf_op jit(solution)/shard_map/cond/branch_0_fun/pallas_call | solution.py:527
  (55 shorter events, 17.7 us)
Async XLA Ops:
  4.0 7.3 %copy-start = (f32[1000,64]{0,1:T(8,128)S(1)}, f32[1000,64]{0,1:T(8,128)}, u32[]{:S(2)}) copy-start(f32[1000,64]{0,1:T(8,128)} %param.8) | copy-start | bytes 768004
  4.0 56.1 %all-to-all-start.7 = ((bf16[32,32,1024]{2,1,0:T(8,128)(2,1)}), bf16[32,32,1024]{2,1,0:T(8,128)(2,1)S(1)}, u32[]{:S(2)}, u32[]{:S(2)}) async-start(bf16[32,32,1024]{2,1,0:T(8,128)(2,1)} %shard_map.70), calls=%async_computation.7 | async-start | bytes 4194304 | tf_op jit(solution)/shard_map/all_to_all | solution.py:489
  11.4 21.0 %collective-permute-start.7 = (bf16[64,1024]{1,0:T(8,128)(2,1)S(1)}, bf16[64,1024]{1,0:T(8,128)(2,1)S(1)}, u32[]{:S(2)}, u32[]{:S(2)}) collective-permute-start(bf16[64,1024]{1,0:T(8,128)(2,1)S(1)} %get-tuple-element.65), channel_id=1, source_target_pairs={{0,1},{1,0},{2,3},{3,2},{4,5},{5,4},{6,7},{7,6},{8,9},{9,8},{10,11... | collective-permute-start | bytes 393224 | tf_op jit(solution)/shard_map/ppermute | solution.py:472
  62.9 1.4 collective-permute-start.8
  87.4 1.3 collective-permute-start.9
  92.6 1.4 collective-permute-start.10
  115.4 35.1 %copy-start.1 = (s32[4,8]{1,0:T(4,128)S(1)}, s32[4,8]{1,0:T(4,128)}, u32[]{:S(2)}) copy-start(s32[4,8]{1,0:T(4,128)} %dev_any.1) | copy-start | bytes 388
  115.5 35.1 %copy-start.2 = (s32[4,8]{1,0:T(4,128)S(1)}, s32[4,8]{1,0:T(4,128)}, u32[]{:S(2)}) copy-start(s32[4,8]{1,0:T(4,128)} %slot_any.1) | copy-start | bytes 388
  115.5 35.1 %copy-start.3 = (s32[4,8]{1,0:T(4,128)S(1)}, s32[4,8]{1,0:T(4,128)}, u32[]{:S(2)}) copy-start(s32[4,8]{1,0:T(4,128)} %weight_any.1) | copy-start | bytes 388
  115.5 1.3 collective-permute-start.11
  120.8 1.5 collective-permute-start.12
  145.1 1.3 collective-permute-start.13
  154.2 51.5 %all-to-all-start = ((bf16[32,32,1024]{2,1,0:T(8,128)(2,1)}), bf16[32,32,1024]{2,1,0:T(8,128)(2,1)S(1)}, u32[]{:S(2)}, u32[]{:S(2)}) async-start(bf16[32,32,1024]{2,1,0:T(8,128)(2,1)} %branch_0_fun.11), calls=%async_computation | async-start | bytes 4194304 | tf_op jit(solution)/shard_map/cond/branch_0_fun/all_to_all | solution.py:489
  157.0 21.0 %collective-permute-start = (bf16[64,1024]{1,0:T(8,128)(2,1)S(1)}, bf16[64,1024]{1,0:T(8,128)(2,1)S(1)}, u32[]{:S(2)}, u32[]{:S(2)}) collective-permute-start(bf16[64,1024]{1,0:T(8,128)(2,1)S(1)} %get-tuple-element.63), channel_id=1, source_target_pairs={{0,1},{1,0},{2,3},{3,2},{4,5},{5,4},{6,7},{7,6},{8,9},{9,8},{10,11... | collective-permute-start | bytes 393224 | tf_op jit(solution)/shard_map/cond/branch_0_fun/ppermute | solution.py:472
  208.5 1.6 collective-permute-start.1
  237.4 1.5 collective-permute-start.2
  244.8 1.6 collective-permute-start.3
  272.7 1.5 collective-permute-start.4
  280.1 1.8 collective-permute-start.5
  310.9 1.5 collective-permute-start.6
  316.9 0.7 copy-start.4
  317.0 0.7 copy-start.5

commit v7 on v6

--- a/solution.py
+++ b/solution.py
@@ -17,7 +17,7 @@
 HIGHEST = lax.Precision.HIGHEST
 
 
-def inverse_factor(gram):
+def inverse_factor(gram, spread_ref):
     width = gram.shape[0]
     rows = lax.broadcasted_iota(jnp.int32, (width, width), 0)
     cols = lax.broadcasted_iota(jnp.int32, (width, width), 1)
@@ -36,13 +36,16 @@
         def column(of, j):
             return jnp.broadcast_to(of[:, base + j : base + j + 1], shape)
 
-        columns = [column(strip, j) for j in range(8)]
-        core = {
-            (i, j): jnp.broadcast_to(columns[j][i : i + 1], shape)
-            for j in range(8)
-            for i in range(j, 8)
-        }
-        lines = [jnp.broadcast_to(strip[j : j + 1], shape) for j in range(8)]
+        slot = spread_ref.at[panel % 2]
+        for j in range(8):
+            slot[j] = column(strip, j)
+        slot[8] = strip
+
+        def row(of, i):
+            return slot[of, pl.ds(i, 8, stride=0)]
+
+        core = {(i, j): row(j, i) for j in range(8) for i in range(j, 8)}
+        lines = [row(8, j) for j in range(8)]
         below = range(panel + 1, len(strips))
         rest = {(at, j): column(strips[at], j) for at in below for j in range(8)}
         for j in range(0, 8, 2):
@@ -119,52 +122,53 @@
     return part.reshape(part.shape[0] * part.shape[1], part.shape[2])
 
 
-def push_update(core, genes_here, data_ref, second, mine_ref, other_ref):
-    groups, padded = data_ref.shape[1], data_ref.shape[3]
-    chunk = second.shape[0] // 2
-    blocks = padded // LANES
-    for group in range(groups):
-        update = jnp.dot(second, block(data_ref, group), preferred_element_type=jnp.float32)
-        lane = lax.broadcasted_iota(jnp.int32, update.shape, 1)
-        update = jnp.where(lane < genes_here, update, 0.0)
-        upper, lower = update[:chunk], update[chunk:]
-        mine = jnp.where(core == 0, upper, lower).astype(mine_ref.dtype)
-        other = jnp.where(core == 0, lower, upper).astype(mine_ref.dtype)
-        for at in range(blocks):
-            lanes = slice(at * LANES, (at + 1) * LANES)
-            mine_ref[group * blocks + at, :chunk] = mine[:, lanes]
-            other_ref[group * blocks + at, :chunk] = other[:, lanes]
-
-
-def pull_update(core, mine_ref, other_ref, update_ref):
-    groups, _, _, padded = update_ref.shape
-    blocks = padded // LANES
-    for group in range(groups):
-        for at in range(blocks):
-            lanes = slice(at * LANES, (at + 1) * LANES)
-            update_ref[group, core, :, lanes] = mine_ref[group * blocks + at]
-            update_ref[group, 1 - core, :, lanes] = other_ref[group * blocks + at]
-
-
-def columns_of(update_ref, group):
-    update = update_ref[group]
-    return update.reshape(update.shape[0] * update.shape[1], update.shape[2])
-
-
-def normaliser(update_ref, genes_total):
-    exact = update_ref.dtype == jnp.float32
-    gram = None
-    for group in range(update_ref.shape[0]):
-        update = columns_of(update_ref, group)
-        part = lax.dot_general(
-            update,
-            update,
-            (((1,), (1,)), ((), ())),
-            precision=HIGHEST if exact else None,
-            preferred_element_type=jnp.float32,
-        )
-        gram = part if gram is None else gram + part
-    return inverse_factor(gram / genes_total)
+def push_update(genes_here, data_ref, group, second, out_ref, chunk):
+    update = jnp.dot(second, block(data_ref, group), preferred_element_type=jnp.float32)
+    lane = lax.broadcasted_iota(jnp.int32, update.shape, 1)
+    update = jnp.where(lane < genes_here, update, 0.0).astype(out_ref.dtype)
+    halves = update.shape[0] // chunk
+    for at in range(update.shape[1] // LANES):
+        for half in range(halves):
+            out_ref[at * halves + half, :chunk] = update[
+                half * chunk : (half + 1) * chunk, at * LANES : (at + 1) * LANES
+            ]
+
+
+def pull_update(chunks_ref, update_ref):
+    width, padded = update_ref.shape
+    chunk = chunks_ref.shape[1]
+    halves = width // chunk
+    for at in range(padded // LANES):
+        for half in range(halves):
+            update_ref[
+                half * chunk : (half + 1) * chunk, at * LANES : (at + 1) * LANES
+            ] = chunks_ref[at * halves + half]
+
+
+def pull_both(core, half_ref, rest_ref, update_ref):
+    pull_update(half_ref, update_ref.at[core])
+    pull_update(rest_ref, update_ref.at[1 - core])
+
+
+def gram_of(update):
+    return lax.dot_general(
+        update,
+        update,
+        (((1,), (1,)), ((), ())),
+        precision=HIGHEST if update.dtype == jnp.float32 else None,
+        preferred_element_type=jnp.float32,
+    )
+
+
+def normaliser(update_ref, genes_total, spread_ref):
+    gram = gram_of(update_ref[0])
+    for group in range(1, update_ref.shape[0]):
+        gram = gram + gram_of(update_ref[group])
+    return inverse_factor(gram / genes_total, spread_ref)
+
+
+def apply(inverse, array):
+    return jnp.dot(inverse, array, precision=HIGHEST, preferred_element_type=jnp.float32)
 
 
 def score(left, data_ref, groups):
@@ -259,38 +263,33 @@
         copy.wait()
 
 
-def share_second(core, second, mine_ref, other_ref, chunk, groups):
+def share_second(core, to, second, out_ref, chunk, groups):
     width, cells = second.shape
-    blocks, tall = mine_ref.shape[:2]
+    blocks, tall = out_ref.shape[:2]
     cores = 2
     rows = cells * groups // (cores * blocks)
     tall = tall - chunk
     slabs = width // groups // tall
-    lane = lax.broadcasted_iota(jnp.int32, (tall, LANES), 1) // rows - core * slabs
+    lane = lax.broadcasted_iota(jnp.int32, (tall, LANES), 1) // rows
+    chips = LANES // rows // cores
     for at in range(cells // LANES):
         wide = second[:, at * LANES : (at + 1) * LANES].astype(jnp.float32)
-        shares = []
-        for group in range(groups):
-            for device in range(LANES // rows):
+        for chip in range(chips):
+            for group in range(groups):
                 share = jnp.zeros((tall, LANES), jnp.float32)
                 for slab in range(slabs):
                     first_row = (group * slabs + slab) * tall
-                    for turn in range(cores):
-                        turned = pltpu.roll(
-                            wide[first_row : first_row + tall],
-                            (turn * slabs + slab - device) * rows % LANES,
-                            1,
-                        )
-                        share = jnp.where((lane == slab) & (core == turn), turned, share)
-                shares.append(share.astype(mine_ref.dtype))
-        for device in range(0, LANES // rows, cores):
-            chip = (at * (LANES // rows) + device) // cores
-            for group in range(groups):
-                first = shares[group * (LANES // rows) + device]
-                second_core = shares[group * (LANES // rows) + device + 1]
-                to = chip * groups + group
-                mine_ref[to, chunk:] = jnp.where(core == 0, first, second_core)
-                other_ref[to, chunk:] = jnp.where(core == 0, second_core, first)
+                    place = core * slabs + slab
+                    shift = (place - chip * cores - to) * rows
+                    turned = pltpu.roll(
+                        wide[first_row : first_row + tall],
+                        lax.rem(shift + LANES, LANES),
+                        1,
+                    )
+                    share = jnp.where(lane == place, turned, share)
+                out_ref[(at * chips + chip) * groups + group, chunk:] = share.astype(
+                    out_ref.dtype
+                )
 
 
 def order_shares(arrived_ref, chunk, out_ref, groups, cores, slots):
@@ -326,8 +325,8 @@
     place_ref,
     data_ref,
     start_ref,
-    mine_ref,
     other_ref,
+    second_ref,
     links_ref,
     degree_ref,
 ):
@@ -345,72 +344,107 @@
     scores = score(lambda shift: start_ref[shift], data_ref, order)
     scores = scores / math.sqrt(genes_here * groups)
     second = diffuse(scores, links, degree[:1])
-    push_update(core, genes_here, data_ref, second, mine_ref, other_ref)
+    second_ref[...] = second
+    push_update(genes_here, data_ref, 1 - core, second, other_ref, other_ref.shape[1])
+
+
+def half_kernel(place_ref, half_ref, data_ref, scores_ref, gram_ref, update_ref):
+    pull_update(half_ref, update_ref)
+    gram_ref[...] = gram_of(update_ref[...])
+    scores_ref[...] = score(lambda _: update_ref[...], data_ref, [place_ref[0]])
 
 
 def next_kernel(
     genes_here,
+    chunk,
+    place_ref,
+    scores_ref,
+    gram_ref,
+    rest_ref,
+    data_ref,
+    links_ref,
+    degree_ref,
+    other_ref,
+    second_ref,
+    worst_ref,
+    update_ref,
+    spread_ref,
+):
+    core = place_ref[0]
+    groups = data_ref.shape[1]
+    genes_total = genes_here * groups
+    pull_update(rest_ref, update_ref)
+    gram = (gram_ref[...] + gram_of(update_ref[...])) / genes_total
+    inverse, amplified = inverse_factor(gram, spread_ref)
+    worst_ref[...] = jnp.broadcast_to(amplified, worst_ref.shape)
+    scores = scores_ref[...] + score(lambda _: update_ref[...], data_ref, [1 - core])
+    scores = apply(inverse, scores) / math.sqrt(genes_total)
+    second = diffuse(scores, links_ref[...], degree_ref[:1])
+    second_ref[...] = second
+    push_update(genes_here, data_ref, 1 - core, second, other_ref, chunk)
+    if other_ref.shape[1] > chunk:
+        share_second(core, 1 - core, second, other_ref, chunk, groups)
+
+
+def exact_kernel(
+    genes_here,
+    chunk,
     place_ref,
     half_ref,
     rest_ref,
     data_ref,
     links_ref,
     degree_ref,
-    mine_ref,
     other_ref,
+    second_ref,
     worst_ref,
     update_ref,
+    spread_ref,
 ):
     core = place_ref[0]
     groups = data_ref.shape[1]
-    chunk = half_ref.shape[1]
     genes_total = genes_here * groups
-    pull_update(core, half_ref, rest_ref, update_ref)
-    inverse, amplified = normaliser(update_ref, genes_total)
+    pull_both(core, half_ref, rest_ref, update_ref)
+    inverse, amplified = normaliser(update_ref, genes_total, spread_ref)
     worst_ref[...] = jnp.broadcast_to(amplified, worst_ref.shape)
-
-    def apply(array):
-        return jnp.dot(inverse, array, precision=HIGHEST, preferred_element_type=jnp.float32)
-
-    if update_ref.dtype == jnp.float32:
-        scores = score(
-            lambda group: apply(columns_of(update_ref, group)).astype(jnp.bfloat16),
-            data_ref,
-            range(groups),
-        )
-    else:
-        scores = apply(
-            score(lambda group: columns_of(update_ref, group), data_ref, range(groups))
-        )
-    second = diffuse(scores / math.sqrt(genes_total), links_ref[...], degree_ref[:1])
-    push_update(core, genes_here, data_ref, second, mine_ref, other_ref)
+    scores = score(
+        lambda group: apply(inverse, update_ref[group]).astype(jnp.bfloat16),
+        data_ref,
+        range(groups),
+    ) / math.sqrt(genes_total)
+    second = diffuse(scores, links_ref[...], degree_ref[:1])
+    second_ref[...] = second
+    push_update(genes_here, data_ref, 1 - core, second, other_ref, chunk)
+    if other_ref.shape[1] > chunk:
+        share_second(core, 1 - core, second, other_ref, chunk, groups)
+
+
+def mine_kernel(genes_here, chunk, place_ref, data_ref, second_ref, mine_ref):
+    core, second = place_ref[0], second_ref[...]
+    push_update(genes_here, data_ref, core, second, mine_ref, chunk)
     if mine_ref.shape[1] > chunk:
-        share_second(core, second, mine_ref, other_ref, chunk, groups)
-
-
-def last_kernel(
-    genes_here,
-    slots,
-    place_ref,
-    half_ref,
-    rest_ref,
-    arrived_ref,
-    *refs,
-):
-    *earlier, out_ref, smoothed_ref, good_ref, update_ref = refs
+        share_second(core, core, second, mine_ref, chunk, data_ref.shape[1])
+
+
+def own_kernel(slots, place_ref, half_ref, arrived_ref, smoothed_ref, gram_ref, update_ref):
+    pull_update(half_ref, update_ref)
+    gram_ref[...] = gram_of(update_ref[...])
+    order_shares(arrived_ref, half_ref.shape[1], smoothed_ref, 2, 2, slots)
+
+
+def last_kernel(genes_here, place_ref, half_ref, rest_ref, gram_ref, *refs):
+    *earlier, out_ref, good_ref, update_ref, spread_ref = refs
     core, own = place_ref[0], place_ref[1]
-    groups, cores = update_ref.shape[:2]
-    pull_update(core, half_ref, rest_ref, update_ref)
-    genes_total = genes_here * groups
-    inverse, amplified = normaliser(update_ref, genes_total)
+    groups = update_ref.shape[0]
+    pull_both(core, half_ref, rest_ref, update_ref)
+    gram = gram_ref[...] + gram_of(update_ref[1 - core])
+    inverse, amplified = inverse_factor(gram / (genes_here * groups), spread_ref)
     good = amplified <= AMPLIFIED
     for worst_ref in earlier:
         good = good & (worst_ref[:, :1] <= AMPLIFIED)
     good_ref[0] = jnp.min(good.astype(jnp.int32))
-    mine = columns_of(update_ref, own).astype(jnp.float32)
-    loadings = jnp.dot(inverse, mine, precision=HIGHEST, preferred_element_type=jnp.float32)
+    loadings = apply(inverse, update_ref[own].astype(jnp.float32))
     out_ref[...] = loadings[:, :genes_here]
-    order_shares(arrived_ref, half_ref.shape[1], smoothed_ref, groups, cores, slots)
 
 
 def add_kernel(mine_ref, arrived_ref, out_ref):
@@ -492,49 +526,75 @@
     def cut(tall):
         return jax.ShapeDtypeStruct((blocks, tall, LANES), kept)
 
-    update = pltpu.VMEM((groups, cores, chunk, padded), kept)
-    worst = jax.ShapeDtypeStruct((width, LANES), jnp.float32)
+    def shape(*sizes, dtype=jnp.float32):
+        return jax.ShapeDtypeStruct(sizes, dtype)
+
+    part = pltpu.VMEM((width, padded), kept)
+    update = pltpu.VMEM((groups, width, padded), kept)
+    spread = pltpu.VMEM((2, 9, 8, 2 * width), jnp.float32)
+    second_shape = shape(width, cells, dtype=jnp.bfloat16)
+    worst = shape(width, LANES)
     earlier = []
-    links = jax.ShapeDtypeStruct((cells, cells), jnp.bfloat16)
-    degree = jax.ShapeDtypeStruct((8, cells), jnp.float32)
-
-    def reduce(mine, other):
-        return exchange(call(add_kernel, like(mine), arrays=2)(mine, swap(other)))
+
+    def reduce(other, second):
+        swapped = swap(other)
+        mine = call(
+            functools.partial(mine_kernel, genes_here, chunk), like(other), scalars=1, arrays=2
+        )(place, moved, second)
+        return exchange(call(add_kernel, like(other), arrays=2)(mine, swapped))
 
     def gather(arrived):
         half = exchange(call(sum_kernel, cut(chunk), arrays=1)(arrived))
         return half, swap(half)
 
-    share = cut(chunk)
-    mine, other, links, degree = call(
+    other, second, links, degree = call(
         functools.partial(first_kernel, genes_here, slots),
-        (share, share, links, degree),
+        (cut(chunk), second_shape, shape(cells, cells, dtype=jnp.bfloat16), shape(8, cells)),
         scalars=1,
         arrays=2,
     )(place, moved, starts)
-    arrived = reduce(mine, other)
+    arrived = reduce(other, second)
     for step in range(1, ITERS):
         share = cut(chunk + 16 if step == ITERS - 1 else chunk)
-        mine, other, amplified = call(
-            functools.partial(next_kernel, genes_here),
-            (share, share, worst),
-            (update,),
+        half, rest = gather(arrived)
+        if kept == jnp.float32:
+            kernel, known, scratch = exact_kernel, (half, rest), update
+        else:
+            scores, gram = call(
+                half_kernel,
+                (shape(width, cells), shape(width, width)),
+                (part,),
+                scalars=1,
+                arrays=2,
+            )(place, half, moved)
+            kernel, known, scratch = next_kernel, (scores, gram, rest), part
+        other, second, amplified = call(
+            functools.partial(kernel, genes_here, chunk),
+            (share, second_shape, worst),
+            (scratch, spread),
             scalars=1,
-            arrays=5,
-        )(place, *gather(arrived), moved, links, degree)
+            arrays=3 + len(known),
+        )(place, *known, moved, links, degree)
         earlier.append(amplified)
-        arrived = reduce(mine, other)
-    loadings, smoothed, good = call(
-        functools.partial(last_kernel, genes_here, slots),
+        arrived = reduce(other, second)
+    half, rest = gather(arrived)
+    smoothed, gram = call(
+        functools.partial(own_kernel, slots),
         (
-            jax.ShapeDtypeStruct((width, genes_here), jnp.float32),
-            jax.ShapeDtypeStruct((width // groups, slots * tile_cells), jnp.bfloat16),
-            jax.ShapeDtypeStruct((1,), jnp.int32),
+            shape(width // groups, slots * tile_cells, dtype=jnp.bfloat16),
+            shape(width, width),
         ),
-        (update,),
+        (part,),
+        scalars=1,
+        arrays=2,
+    )(place, half, arrived)
+    loadings, good = call(
+        functools.partial(last_kernel, genes_here),
+        (shape(width, genes_here), shape(1, dtype=jnp.int32)),
+        (update, spread),
         scalars=1,
         arrays=3 + len(earlier),
-    )(place, *gather(arrived), arrived, *earlier)
+    )(place, half, rest, gram, *earlier)
     return loadings.T, smoothed, good[0] == 1
 
 
@@ -669,6 +729,7 @@
     rows = slots * rows_of
     return (
         mesh.shape["cells"] % 2 == 0
+        and groups == 2
         and tile_cells % (8 * parts) == 0
         and neighbours <= rows_of
         and rows % 16 == 0

time: 318 us -> 313 us (0.984)
  waiting for transfers between devices: 111 us -> 102 us
  Pallas kernels: 39.9 us -> 43.8 us
    ppermute x12, waiting for transfers between devices: 17 us -> 7.85 us  [swap(): return lax.ppermute(array, 'core', [(0, 1), (1, 0)])]
    pallas_call x14 -> x24, Pallas kernels: 32.9 us -> 36.9 us  [the longest x4 16.3 us: by_cell(): call(functools.partial(kernel, genes_here, chunk), (share, second_shape,...]
  transfers between devices with their start and end apart: 16 -> 16, of which waited for: 16 -> 16; matrix products, arithmetic and copies ran while one was open for 0% -> 0% of each run, Pallas kernels for 0% -> 3%
where the time goes in v7:
time: 313 us
  blocking collectives  150 us (48%)
  waiting for transfers between devices  102 us (33%)
  Pallas kernels  43.8 us (14%)
  starting transfers between devices  14.7 us (5%)
    all_to_all x12, blocking collectives, exchange(): return lax.all_to_all(array, ('chips', 'genes'), 0, 0, tiled=True)  150 us
    all_to_all x2, waiting for transfers between devices, by_cell(): moved = lax.all_to_all(moved, ('chips', 'core', 'genes'), 0, 0, tiled=True)  55.3 us
    ppermute x2, waiting for transfers between devices, by_cell(): starts.append(lax.ppermute(narrow, 'genes', pairs))  38.4 us
    pallas_call x4, Pallas kernels, by_cell(): call(functools.partial(kernel, genes_here, chunk), (share, second_shape,...  16.3 us
    all_to_all x2, starting transfers between devices, by_cell(): moved = lax.all_to_all(moved, ('chips', 'core', 'genes'), 0, 0, tiled=True)  10.2 us
    ppermute x12, waiting for transfers between devices, swap(): return lax.ppermute(array, 'core', [(0, 1), (1, 0)])  7.85 us
    pallas_call x2, Pallas kernels, by_cell(): pl.pallas_call(functools.partial(regroup_kernel, rows_of), out_shape=jax....  6.77 us
  transfers between devices with their start and end apart: 16, of which 16 were waited for; matrix products, arithmetic and copies ran while one was open for 0% of the time, Pallas kernels for 3%

profile of v7, /device:TPU:0, one launch (start us, length us, event | category | flops | bytes accessed | tf_op | source)
XLA Modules:
  0.0 312.6 jit_solution(10090991140127302075)
XLA Ops:
  0.6 3.4 %shard_map.70 = bf16[32,32,1024]{2,1,0:T(8,128)(2,1)} custom-call(bf16[1000,1024]{1,0:T(8,128)(2,1)} %bitcast.10.data_any, s32[4,8]{1,0:T(4,128)} %dev_any.1, s32[4,8]{1,0:T(4,128)} %slot_any.1, s32[4,8]{1,0:T(4,128)} %weight_any.1), custom_call_target="tpu_custom_call" | custom-call | tf_op jit(solution)/shard_map/pallas_call | solution.py:508
  4.0 7.3 %all-to-all-start.7 = ((bf16[32,32,1024]{2,1,0:T(8,128)(2,1)}), bf16[32,32,1024]{2,1,0:T(8,128)(2,1)S(1)}, u32[]{:S(2)}, u32[]{:S(2)}) async-start(bf16[32,32,1024]{2,1,0:T(8,128)(2,1)} %shard_map.70), calls=%async_computation.7 | async-start | bytes 4194304 | tf_op jit(solution)/shard_map/all_to_all | solution.py:523
  11.4 1.8 collective-permute-start.7
  13.3 19.1 %collective-permute-done.7 = bf16[64,1024]{1,0:T(8,128)(2,1)S(1)} collective-permute-done((bf16[64,1024]{1,0:T(8,128)(2,1)S(1)}, bf16[64,1024]{1,0:T(8,128)(2,1)S(1)}, u32[]{:S(2)}, u32[]{:S(2)}) %collective-permute-start.7) | collective-permute-done | bytes 131104 | tf_op jit(solution)/shard_map/ppermute | solution.py:506
  32.5 27.6 %all-to-all-done.7 = bf16[32,32,1024]{2,1,0:T(8,128)(2,1)S(1)} async-done(((bf16[32,32,1024]{2,1,0:T(8,128)(2,1)}), bf16[32,32,1024]{2,1,0:T(8,128)(2,1)S(1)}, u32[]{:S(2)}, u32[]{:S(2)}) %all-to-all-start.7) | async-done | bytes 2097184 | tf_op jit(solution)/shard_map/all_to_all | solution.py:523
  60.1 2.6 shard_map.71
  64.2 12.2 %all_to_all.69.chunks_ref = bf16[16,32,128]{2,1,0:T(8,128)(2,1)S(1)} all-to-all(bf16[16,32,128]{2,1,0:T(8,128)(2,1)S(1)} %shard_map.73), channel_id=1, replica_groups=mesh['chips'=8,'core'=2,'genes'=2] {'chips','genes'}, dimensions={0} | all-to-all | bytes 262144 | tf_op jit(solution)/shard_map/all_to_all | solution.py:497
  76.4 10.7 %all_to_all.70.half_ref = bf16[16,32,128]{2,1,0:T(8,128)(2,1)S(1)} all-to-all(bf16[16,32,128]{2,1,0:T(8,128)(2,1)S(1)} %shard_map.74), channel_id=1, replica_groups=mesh['chips'=8,'core'=2,'genes'=2] {'chips','genes'}, dimensions={0} | all-to-all | bytes 262144 | tf_op jit(solution)/shard_map/all_to_all | solution.py:497
  88.5 3.1 shard_map.76
  93.0 10.7 %all_to_all.71.chunks_ref = bf16[16,32,128]{2,1,0:T(8,128)(2,1)S(1)} all-to-all(bf16[16,32,128]{2,1,0:T(8,128)(2,1)S(1)} %shard_map.78), channel_id=1, replica_groups=mesh['chips'=8,'core'=2,'genes'=2] {'chips','genes'}, dimensions={0} | all-to-all | bytes 262144 | tf_op jit(solution)/shard_map/all_to_all | solution.py:497
  103.8 10.7 %all_to_all.72.half_ref = bf16[16,32,128]{2,1,0:T(8,128)(2,1)S(1)} all-to-all(bf16[16,32,128]{2,1,0:T(8,128)(2,1)S(1)} %shard_map.79), channel_id=1, replica_groups=mesh['chips'=8,'core'=2,'genes'=2] {'chips','genes'}, dimensions={0} | all-to-all | bytes 262144 | tf_op jit(solution)/shard_map/all_to_all | solution.py:497
  115.8 3.1 shard_map.81
  120.5 11.5 %all_to_all.73.chunks_ref.arrived_ref = bf16[16,48,128]{2,1,0:T(8,128)(2,1)S(1)} all-to-all(bf16[16,48,128]{2,1,0:T(8,128)(2,1)S(1)} %shard_map.83), channel_id=1, replica_groups=mesh['chips'=8,'core'=2,'genes'=2] {'chips','genes'}, dimensions={0} | all-to-all | bytes 393216 | tf_op jit(solution)/shard_map/all_to_all | solution.py:497
  132.0 11.3 %all_to_all.74.half_ref = bf16[16,32,128]{2,1,0:T(8,128)(2,1)S(1)} all-to-all(bf16[16,32,128]{2,1,0:T(8,128)(2,1)S(1)} %shard_map.84), channel_id=1, replica_groups=mesh['chips'=8,'core'=2,'genes'=2] {'chips','genes'}, dimensions={0} | all-to-all | bytes 262144 | tf_op jit(solution)/shard_map/all_to_all | solution.py:497
  144.6 3.0 shard_map.86
  148.4 163.5 %conditional.1 = (bf16[32,1024]{1,0:T(8,128)(2,1)S(1)}, f32[1000,64]{0,1:T(8,128)S(1)}) conditional(s32[]{:T(128)} %bitcast.15, (bf16[1024,1000]{0,1:T(8,128)(2,1)}, s32[4,8]{1,0:T(4,128)S(1)}, s32[4,8]{1,0:T(4,128)S(1)}, s32[4,8]{1,0:T(4,128)S(1)}, f32[1000,64]{0,1:T(8,128)S(1)}) %tuple.25, (f32[1000,64]{0,1:T(8,128)S(1)}, ...), branch_computations={%region_0.1_spmd, %region_1.2_spmd} | conditional | flops 195079 | bytes 18338188 | solution.py:603
  148.4 3.4 %branch_0_fun.15 = bf16[32,32,1024]{2,1,0:T(8,128)(2,1)} custom-call(bf16[1000,1024]{1,0:T(8,128)(2,1)} %bitcast.2.data_any, s32[4,8]{1,0:T(4,128)S(1)} %get-tuple-element.15.dev_any, s32[4,8]{1,0:T(4,128)S(1)} %get-tuple-element.16.slot_any, s32[4,8]{1,0:T(4,128)S(1)} %get-tuple-element.17.weight_any), custom_call_target="tpu_custom_call" | custom-call | tf_op jit(solution)/shard_map/cond/branch_0_fun/pallas_call | solution.py:508
  151.8 2.9 all-to-all-start
  156.4 19.2 %collective-permute-done = bf16[64,1024]{1,0:T(8,128)(2,1)S(1)} collective-permute-done((bf16[64,1024]{1,0:T(8,128)(2,1)S(1)}, bf16[64,1024]{1,0:T(8,128)(2,1)S(1)}, u32[]{:S(2)}, u32[]{:S(2)}) %collective-permute-start) | collective-permute-done | bytes 131104 | tf_op jit(solution)/shard_map/cond/branch_0_fun/ppermute | solution.py:506
  175.6 27.7 %all-to-all-done = bf16[32,32,1024]{2,1,0:T(8,128)(2,1)S(1)} async-done(((bf16[32,32,1024]{2,1,0:T(8,128)(2,1)}), bf16[32,32,1024]{2,1,0:T(8,128)(2,1)S(1)}, u32[]{:S(2)}, u32[]{:S(2)}) %all-to-all-start) | async-done | bytes 2097184 | tf_op jit(solution)/shard_map/cond/branch_0_fun/all_to_all | solution.py:523
  203.3 2.6 branch_0_fun.16
  207.5 14.5 %all_to_all.63.chunks_ref = f32[16,32,128]{2,1,0:T(8,128)S(1)} all-to-all(f32[16,32,128]{2,1,0:T(8,128)S(1)} %branch_0_fun.18), channel_id=1, replica_groups=mesh['chips'=8,'core'=2,'genes'=2] {'chips','genes'}, dimensions={0} | all-to-all | bytes 524288 | tf_op jit(solution)/shard_map/cond/branch_0_fun/all_to_all | solution.py:497
  222.1 12.8 %all_to_all.64.half_ref = f32[16,32,128]{2,1,0:T(8,128)S(1)} all-to-all(f32[16,32,128]{2,1,0:T(8,128)S(1)} %branch_0_fun.19), channel_id=1, replica_groups=mesh['chips'=8,'core'=2,'genes'=2] {'chips','genes'}, dimensions={0} | all-to-all | bytes 524288 | tf_op jit(solution)/shard_map/cond/branch_0_fun/all_to_all | solution.py:497
  234.9 1.5 collective-permute-done.2.rest_ref
  236.4 5.1 %branch_0_fun.20 = (f32[16,32,128]{2,1,0:T(8,128)S(1)}, bf16[64,512]{1,0:T(8,128)(2,1)S(1)}, f32[64,128]{1,0:T(8,128)S(1)}) custom-call(s32[2]{0:T(128)S(1)} %pad_add_fusion.place_ref, f32[16,32,128]{2,1,0:T(8,128)S(1)} %all_to_all.64.half_ref, f32[16,32,128]{2,1,0:T(8,128)S(1)} %collective-permute-done.2.rest_ref, bf16[16,2,32,1024]{3,2,1,0:T(8,128)(2,1)S(1)} %bitcast.31, ...), custom_call_target="tpu_custom_call" | custom-call | tf_op jit(solution)/shard_map/cond/branch_0_fun/pallas_call | solution.py:571
  243.1 13.5 %all_to_all.65.chunks_ref = f32[16,32,128]{2,1,0:T(8,128)S(1)} all-to-all(f32[16,32,128]{2,1,0:T(8,128)S(1)} %branch_0_fun.22), channel_id=1, replica_groups=mesh['chips'=8,'core'=2,'genes'=2] {'chips','genes'}, dimensions={0} | all-to-all | bytes 524288 | tf_op jit(solution)/shard_map/cond/branch_0_fun/all_to_all | solution.py:497
  256.7 12.8 %all_to_all.66.half_ref = f32[16,32,128]{2,1,0:T(8,128)S(1)} all-to-all(f32[16,32,128]{2,1,0:T(8,128)S(1)} %branch_0_fun.23), channel_id=1, replica_groups=mesh['chips'=8,'core'=2,'genes'=2] {'chips','genes'}, dimensions={0} | all-to-all | bytes 524288 | tf_op jit(solution)/shard_map/cond/branch_0_fun/all_to_all | solution.py:497
  269.4 1.5 collective-permute-done.4.rest_ref
  271.0 5.1 %branch_0_fun.24 = (f32[16,48,128]{2,1,0:T(8,128)S(1)}, bf16[64,512]{1,0:T(8,128)(2,1)S(1)}, f32[64,128]{1,0:T(8,128)S(1)}) custom-call(s32[2]{0:T(128)S(1)} %pad_add_fusion.place_ref, f32[16,32,128]{2,1,0:T(8,128)S(1)} %all_to_all.66.half_ref, f32[16,32,128]{2,1,0:T(8,128)S(1)} %collective-permute-done.4.rest_ref, bf16[16,2,32,1024]{3,2,1,0:T(8,128)(2,1)S(1)} %bitcast.33, ...), custom_call_target="tpu_custom_call" | custom-call | tf_op jit(solution)/shard_map/cond/branch_0_fun/pallas_call | solution.py:571
  277.9 16.2 %all_to_all.67.chunks_ref.arrived_ref = f32[16,48,128]{2,1,0:T(8,128)S(1)} all-to-all(f32[16,48,128]{2,1,0:T(8,128)S(1)} %branch_0_fun.26), channel_id=1, replica_groups=mesh['chips'=8,'core'=2,'genes'=2] {'chips','genes'}, dimensions={0} | all-to-all | bytes 786432 | tf_op jit(solution)/shard_map/cond/branch_0_fun/all_to_all | solution.py:497
  294.2 12.7 %all_to_all.68.half_ref = f32[16,32,128]{2,1,0:T(8,128)S(1)} all-to-all(f32[16,32,128]{2,1,0:T(8,128)S(1)} %branch_0_fun.27), channel_id=1, replica_groups=mesh['chips'=8,'core'=2,'genes'=2] {'chips','genes'}, dimensions={0} | all-to-all | bytes 524288 | tf_op jit(solution)/shard_map/cond/branch_0_fun/all_to_all | solution.py:497
  308.4 3.2 %branch_0_fun.29 = (f32[64,1000]{1,0:T(8,128)S(1)}, s32[1]{0:T(128)}) custom-call(s32[2]{0:T(128)S(1)} %pad_add_fusion.place_ref, f32[16,32,128]{2,1,0:T(8,128)S(1)} %all_to_all.68.half_ref, f32[16,32,128]{2,1,0:T(8,128)S(1)} %collective-permute-done.6.rest_ref, f32[64,64]{1,0:T(8,128)S(1)} %get-tuple-element.27.gram_ref, ...), custom_call_target="tpu_custom_call" | custom-call | tf_op jit(solution)/shard_map/cond/branch_0_fun/pallas_call | solution.py:591
  (65 shorter events, 17.7 us)
Async XLA Ops:
  4.0 7.3 %copy-start = (f32[1000,64]{0,1:T(8,128)S(1)}, f32[1000,64]{0,1:T(8,128)}, u32[]{:S(2)}) copy-start(f32[1000,64]{0,1:T(8,128)} %param.8) | copy-start | bytes 768004
  4.0 56.1 %all-to-all-start.7 = ((bf16[32,32,1024]{2,1,0:T(8,128)(2,1)}), bf16[32,32,1024]{2,1,0:T(8,128)(2,1)S(1)}, u32[]{:S(2)}, u32[]{:S(2)}) async-start(bf16[32,32,1024]{2,1,0:T(8,128)(2,1)} %shard_map.70), calls=%async_computation.7 | async-start | bytes 4194304 | tf_op jit(solution)/shard_map/all_to_all | solution.py:523
  11.4 21.0 %collective-permute-start.7 = (bf16[64,1024]{1,0:T(8,128)(2,1)S(1)}, bf16[64,1024]{1,0:T(8,128)(2,1)S(1)}, u32[]{:S(2)}, u32[]{:S(2)}) collective-permute-start(bf16[64,1024]{1,0:T(8,128)(2,1)S(1)} %get-tuple-element.76), channel_id=1, source_target_pairs={{0,1},{1,0},{2,3},{3,2},{4,5},{5,4},{6,7},{7,6},{8,9},{9,8},{10,11... | collective-permute-start | bytes 393224 | tf_op jit(solution)/shard_map/ppermute | solution.py:506
  62.7 1.4 collective-permute-start.8
  87.2 1.3 collective-permute-start.9
  91.6 1.4 collective-permute-start.10
  114.5 1.3 collective-permute-start.11
  118.9 1.5 collective-permute-start.12
  119.2 29.1 %copy-start.1 = (s32[4,8]{1,0:T(4,128)S(1)}, s32[4,8]{1,0:T(4,128)}, u32[]{:S(2)}) copy-start(s32[4,8]{1,0:T(4,128)} %dev_any.1) | copy-start | bytes 388
  119.2 29.2 %copy-start.2 = (s32[4,8]{1,0:T(4,128)S(1)}, s32[4,8]{1,0:T(4,128)}, u32[]{:S(2)}) copy-start(s32[4,8]{1,0:T(4,128)} %slot_any.1) | copy-start | bytes 388
  119.2 29.2 %copy-start.3 = (s32[4,8]{1,0:T(4,128)S(1)}, s32[4,8]{1,0:T(4,128)}, u32[]{:S(2)}) copy-start(s32[4,8]{1,0:T(4,128)} %weight_any.1) | copy-start | bytes 388
  143.3 1.3 collective-permute-start.13
  151.8 51.5 %all-to-all-start = ((bf16[32,32,1024]{2,1,0:T(8,128)(2,1)}), bf16[32,32,1024]{2,1,0:T(8,128)(2,1)S(1)}, u32[]{:S(2)}, u32[]{:S(2)}) async-start(bf16[32,32,1024]{2,1,0:T(8,128)(2,1)} %branch_0_fun.15), calls=%async_computation | async-start | bytes 4194304 | tf_op jit(solution)/shard_map/cond/branch_0_fun/all_to_all | solution.py:523
  154.8 20.8 %collective-permute-start = (bf16[64,1024]{1,0:T(8,128)(2,1)S(1)}, bf16[64,1024]{1,0:T(8,128)(2,1)S(1)}, u32[]{:S(2)}, u32[]{:S(2)}) collective-permute-start(bf16[64,1024]{1,0:T(8,128)(2,1)S(1)} %get-tuple-element.74), channel_id=1, source_target_pairs={{0,1},{1,0},{2,3},{3,2},{4,5},{5,4},{6,7},{7,6},{8,9},{9,8},{10,11... | collective-permute-start | bytes 393224 | tf_op jit(solution)/shard_map/cond/branch_0_fun/ppermute | solution.py:506
  205.9 1.6 collective-permute-start.1
  234.8 1.5 collective-permute-start.2
  241.5 1.6 collective-permute-start.3
  269.4 1.5 collective-permute-start.4
  276.0 1.8 collective-permute-start.5
  306.9 1.5 collective-permute-start.6
  311.9 0.7 copy-start.4
  311.9 0.7 copy-start.5

commit v8 on v7

--- a/solution.py
+++ b/solution.py
@@ -81,14 +81,13 @@
     target = own_dev * slots + own_slot
     lane = lax.broadcasted_iota(jnp.int32, (tiles * neighbours, tiles), 1).astype(jnp.float32)
     hits = jnp.where(lane == target, own_weight, 0.0)
-    weights = jnp.sum(hits.reshape(tiles, neighbours, tiles), axis=1)
-    tile_row = lax.broadcasted_iota(jnp.int32, (tiles, tiles), 0)
-    tile_col = lax.broadcasted_iota(jnp.int32, (tiles, tiles), 1)
-    weights = weights + jnp.where(tile_row == tile_col, self_weight, 0.0)
+    weights = jnp.sum(hits.reshape(tiles, neighbours, tiles), axis=1, keepdims=True)
     cells = tiles * rows_of
+    tall = jnp.broadcast_to(weights, (tiles, rows_of, tiles)).reshape(cells, tiles)
     tile_of = lax.broadcasted_iota(jnp.int32, (cells, tiles), 0) // rows_of
-    expand = (tile_of == lax.broadcasted_iota(jnp.int32, (cells, tiles), 1)).astype(jnp.bfloat16)
-    tall = jnp.dot(expand, weights.astype(jnp.bfloat16), preferred_element_type=jnp.float32)
+    own = tile_of == lax.broadcasted_iota(jnp.int32, (cells, tiles), 1)
+    tall = tall + jnp.where(own, self_weight, 0.0)
+    expand = own.astype(jnp.bfloat16)
     full = lax.dot_general(
         tall.astype(jnp.bfloat16),
         expand,
@@ -600,12 +599,11 @@
 
 def by_condition(*arguments):
     loadings, smoothed, good = by_cell(jnp.bfloat16, *arguments)
-    return lax.cond(
-        good,
-        lambda *_: (loadings, smoothed),
-        lambda *again: by_cell(jnp.float32, *again)[:2],
-        *arguments,
-    )
+    return lax.while_loop(
+        lambda state: jnp.logical_not(state[2]),
+        lambda _: by_cell(jnp.float32, *arguments)[:2] + (jnp.array(True),),
+        (loadings, smoothed, good),
+    )[:2]
 
 
 def by_tile(data, start, link_dev, link_slot, link_weight):

time: 313 us -> 313 us (level)
  transfers between devices with their start and end apart: 16 -> 16, of which waited for: 16 -> 14; matrix products, arithmetic and copies ran while one was open for 0% -> 0% of each run, Pallas kernels for 3% -> 3%
where the time goes in v8:
time: 313 us; the launch traced here: 312 us
  blocking collectives  150 us (48%)
  waiting for transfers between devices  100 us (32%)
  Pallas kernels  45.1 us (14%)
  starting transfers between devices  14.7 us (5%)
    all_to_all x12, blocking collectives, exchange(): return lax.all_to_all(array, ('chips', 'genes'), 0, 0, tiled=True)  150 us
    all_to_all x2, waiting for transfers between devices, by_cell(): moved = lax.all_to_all(moved, ('chips', 'core', 'genes'), 0, 0, tiled=True)  55.3 us
    ppermute x2, waiting for transfers between devices, by_cell(): starts.append(lax.ppermute(narrow, 'genes', pairs))  38.4 us
    pallas_call x4, Pallas kernels, by_cell(): call(functools.partial(kernel, genes_here, chunk), (share, second_shape,...  16.3 us
    all_to_all x2, starting transfers between devices, by_cell(): moved = lax.all_to_all(moved, ('chips', 'core', 'genes'), 0, 0, tiled=True)  10 us
    ppermute x12, waiting for transfers between devices, swap(): return lax.ppermute(array, 'core', [(0, 1), (1, 0)])  6.77 us
    pallas_call x2, Pallas kernels, by_cell(): pl.pallas_call(functools.partial(regroup_kernel, rows_of), out_shape=jax....  6.73 us
    pallas_call x2, Pallas kernels, by_cell(): call(functools.partial(last_kernel, genes_here), (shape(width, genes_here...  6.72 us
  transfers between devices with their start and end apart: 16, of which 14 were waited for; matrix products, arithmetic and copies ran while one was open for 0% of the time, Pallas kernels for 3%

profile of v8, /device:TPU:0, one launch (start us, length us, event | category | flops | bytes accessed | tf_op | source)
XLA Modules:
  0.0 312.5 jit_solution(15758194856866435960)
XLA Ops:
  0.6 3.4 %shard_map.68 = bf16[32,32,1024]{2,1,0:T(8,128)(2,1)} custom-call(bf16[1000,1024]{1,0:T(8,128)(2,1)} %bitcast.10.data_any, s32[4,8]{1,0:T(4,128)} %dev_any.1, s32[4,8]{1,0:T(4,128)} %slot_any.1, s32[4,8]{1,0:T(4,128)} %weight_any.1), custom_call_target="tpu_custom_call" | custom-call | tf_op jit(solution)/shard_map/pallas_call | solution.py:507
  4.0 7.3 %all-to-all-start.7 = ((bf16[32,32,1024]{2,1,0:T(8,128)(2,1)}), bf16[32,32,1024]{2,1,0:T(8,128)(2,1)S(1)}, u32[]{:S(2)}, u32[]{:S(2)}) async-start(bf16[32,32,1024]{2,1,0:T(8,128)(2,1)} %shard_map.68), calls=%async_computation.7 | async-start | bytes 4194304 | tf_op jit(solution)/shard_map/all_to_all | solution.py:522
  11.4 1.8 collective-permute-start.7
  13.3 19.1 %collective-permute-done.7 = bf16[64,1024]{1,0:T(8,128)(2,1)S(1)} collective-permute-done((bf16[64,1024]{1,0:T(8,128)(2,1)S(1)}, bf16[64,1024]{1,0:T(8,128)(2,1)S(1)}, u32[]{:S(2)}, u32[]{:S(2)}) %collective-permute-start.7) | collective-permute-done | bytes 131104 | tf_op jit(solution)/shard_map/ppermute | solution.py:505
  32.5 27.6 %all-to-all-done.7 = bf16[32,32,1024]{2,1,0:T(8,128)(2,1)S(1)} async-done(((bf16[32,32,1024]{2,1,0:T(8,128)(2,1)}), bf16[32,32,1024]{2,1,0:T(8,128)(2,1)S(1)}, u32[]{:S(2)}, u32[]{:S(2)}) %all-to-all-start.7) | async-done | bytes 2097184 | tf_op jit(solution)/shard_map/all_to_all | solution.py:522
  60.1 2.4 shard_map.69
  64.0 12.3 %all_to_all.69.chunks_ref = bf16[16,32,128]{2,1,0:T(8,128)(2,1)S(1)} all-to-all(bf16[16,32,128]{2,1,0:T(8,128)(2,1)S(1)} %shard_map.71), channel_id=1, replica_groups=mesh['chips'=8,'core'=2,'genes'=2] {'chips','genes'}, dimensions={0} | all-to-all | bytes 262144 | tf_op jit(solution)/shard_map/all_to_all | solution.py:496
  76.2 10.7 %all_to_all.70.half_ref = bf16[16,32,128]{2,1,0:T(8,128)(2,1)S(1)} all-to-all(bf16[16,32,128]{2,1,0:T(8,128)(2,1)S(1)} %shard_map.72), channel_id=1, replica_groups=mesh['chips'=8,'core'=2,'genes'=2] {'chips','genes'}, dimensions={0} | all-to-all | bytes 262144 | tf_op jit(solution)/shard_map/all_to_all | solution.py:496
  88.3 3.1 shard_map.74
  92.8 10.7 %all_to_all.71.chunks_ref = bf16[16,32,128]{2,1,0:T(8,128)(2,1)S(1)} all-to-all(bf16[16,32,128]{2,1,0:T(8,128)(2,1)S(1)} %shard_map.76), channel_id=1, replica_groups=mesh['chips'=8,'core'=2,'genes'=2] {'chips','genes'}, dimensions={0} | all-to-all | bytes 262144 | tf_op jit(solution)/shard_map/all_to_all | solution.py:496
  103.6 10.7 %all_to_all.72.half_ref = bf16[16,32,128]{2,1,0:T(8,128)(2,1)S(1)} all-to-all(bf16[16,32,128]{2,1,0:T(8,128)(2,1)S(1)} %shard_map.77), channel_id=1, replica_groups=mesh['chips'=8,'core'=2,'genes'=2] {'chips','genes'}, dimensions={0} | all-to-all | bytes 262144 | tf_op jit(solution)/shard_map/all_to_all | solution.py:496
  115.6 3.1 shard_map.79
  120.3 11.5 %all_to_all.73.chunks_ref.arrived_ref = bf16[16,48,128]{2,1,0:T(8,128)(2,1)S(1)} all-to-all(bf16[16,48,128]{2,1,0:T(8,128)(2,1)S(1)} %shard_map.81), channel_id=1, replica_groups=mesh['chips'=8,'core'=2,'genes'=2] {'chips','genes'}, dimensions={0} | all-to-all | bytes 393216 | tf_op jit(solution)/shard_map/all_to_all | solution.py:496
  131.8 11.3 %all_to_all.74.half_ref = bf16[16,32,128]{2,1,0:T(8,128)(2,1)S(1)} all-to-all(bf16[16,32,128]{2,1,0:T(8,128)(2,1)S(1)} %shard_map.82), channel_id=1, replica_groups=mesh['chips'=8,'core'=2,'genes'=2] {'chips','genes'}, dimensions={0} | all-to-all | bytes 262144 | tf_op jit(solution)/shard_map/all_to_all | solution.py:496
  144.6 3.3 %shard_map.84 = (f32[64,1000]{1,0:T(8,128)}, s32[1]{0:T(128)}) custom-call(s32[2]{0:T(128)S(1)} %pad_add_fusion.1.place_ref, bf16[16,32,128]{2,1,0:T(8,128)(2,1)S(1)} %all_to_all.74.half_ref, bf16[16,32,128]{2,1,0:T(8,128)(2,1)S(1)} %collective-permute-done.13.rest_ref, f32[64,64]{1,0:T(8,128)S(1)} %get-tuple-element.85.gram_ref, ...), custom_call_target="tpu_custom_call" | custom-call | tf_op jit(solution)/shard_map/pallas_call | solution.py:590
  148.6 163.7 %while.11 = (f32[1000,64]{0,1:T(8,128)}, bf16[32,1024]{1,0:T(8,128)(2,1)}, pred[]{:T(512)}, bf16[1024,1000]{0,1:T(8,128)(2,1)}, s32[4,8]{1,0:T(4,128)S(1)}, /*in...) while((f32[1000,64]{0,1:T(8,128)}, bf16[32,1024]{1,0:T(8,128)(2,1)}, pred[]{:T(512)}, ...), condition=%region_1.2_spmd, body=%region_0.1_spmd | while | flops 131080 | bytes 17954240 | solution.py:602
  148.8 3.4 %body.15 = bf16[32,32,1024]{2,1,0:T(8,128)(2,1)} custom-call(bf16[1000,1024]{1,0:T(8,128)(2,1)} %bitcast.2.data_any, s32[4,8]{1,0:T(4,128)S(1)} %get-tuple-element.143.dev_any, s32[4,8]{1,0:T(4,128)S(1)} %get-tuple-element.144.slot_any, s32[4,8]{1,0:T(4,128)S(1)} %get-tuple-element.145.weight_any), custom_call_target="tpu_custom_call" | custom-call | tf_op jit(solution)/shard_map/while/body/pallas_call | solution.py:507
  152.2 2.7 all-to-all-start
  154.9 1.7 collective-permute-start
  156.7 19.3 %collective-permute-done = bf16[64,1024]{1,0:T(8,128)(2,1)S(1)} collective-permute-done((bf16[64,1024]{1,0:T(8,128)(2,1)S(1)}, bf16[64,1024]{1,0:T(8,128)(2,1)S(1)}, u32[]{:S(2)}, u32[]{:S(2)}) %collective-permute-start) | collective-permute-done | bytes 131104 | tf_op jit(solution)/shard_map/while/body/ppermute | solution.py:505
  176.0 27.7 %all-to-all-done = bf16[32,32,1024]{2,1,0:T(8,128)(2,1)S(1)} async-done(((bf16[32,32,1024]{2,1,0:T(8,128)(2,1)}), bf16[32,32,1024]{2,1,0:T(8,128)(2,1)S(1)}, u32[]{:S(2)}, u32[]{:S(2)}) %all-to-all-start) | async-done | bytes 2097184 | tf_op jit(solution)/shard_map/while/body/all_to_all | solution.py:522
  203.7 2.4 body.16
  207.7 14.5 %all_to_all.63.chunks_ref = f32[16,32,128]{2,1,0:T(8,128)S(1)} all-to-all(f32[16,32,128]{2,1,0:T(8,128)S(1)} %body.18), channel_id=1, replica_groups=mesh['chips'=8,'core'=2,'genes'=2] {'chips','genes'}, dimensions={0} | all-to-all | bytes 524288 | tf_op jit(solution)/shard_map/while/body/all_to_all | solution.py:496
  222.3 12.8 %all_to_all.64.half_ref = f32[16,32,128]{2,1,0:T(8,128)S(1)} all-to-all(f32[16,32,128]{2,1,0:T(8,128)S(1)} %body.19), channel_id=1, replica_groups=mesh['chips'=8,'core'=2,'genes'=2] {'chips','genes'}, dimensions={0} | all-to-all | bytes 524288 | tf_op jit(solution)/shard_map/while/body/all_to_all | solution.py:496
  236.6 5.1 %body.20 = (f32[16,32,128]{2,1,0:T(8,128)S(1)}, bf16[64,512]{1,0:T(8,128)(2,1)S(1)}, f32[64,128]{1,0:T(8,128)S(1)}) custom-call(s32[2]{0:T(128)S(1)} %pad_add_fusion.place_ref, f32[16,32,128]{2,1,0:T(8,128)S(1)} %all_to_all.64.half_ref, f32[16,32,128]{2,1,0:T(8,128)S(1)} %collective-permute-done.2.rest_ref, bf16[16,2,32,1024]{3,2,1,0:T(8,128)(2,1)S(1)} %bitcast.24, ...), custom_call_target="tpu_custom_call" | custom-call | tf_op jit(solution)/shard_map/while/body/pallas_call | solution.py:570
  243.3 13.5 %all_to_all.65.chunks_ref = f32[16,32,128]{2,1,0:T(8,128)S(1)} all-to-all(f32[16,32,128]{2,1,0:T(8,128)S(1)} %body.22), channel_id=1, replica_groups=mesh['chips'=8,'core'=2,'genes'=2] {'chips','genes'}, dimensions={0} | all-to-all | bytes 524288 | tf_op jit(solution)/shard_map/while/body/all_to_all | solution.py:496
  256.9 12.8 %all_to_all.66.half_ref = f32[16,32,128]{2,1,0:T(8,128)S(1)} all-to-all(f32[16,32,128]{2,1,0:T(8,128)S(1)} %body.23), channel_id=1, replica_groups=mesh['chips'=8,'core'=2,'genes'=2] {'chips','genes'}, dimensions={0} | all-to-all | bytes 524288 | tf_op jit(solution)/shard_map/while/body/all_to_all | solution.py:496
  271.2 5.1 %body.24 = (f32[16,48,128]{2,1,0:T(8,128)S(1)}, bf16[64,512]{1,0:T(8,128)(2,1)S(1)}, f32[64,128]{1,0:T(8,128)S(1)}) custom-call(s32[2]{0:T(128)S(1)} %pad_add_fusion.place_ref, f32[16,32,128]{2,1,0:T(8,128)S(1)} %all_to_all.66.half_ref, f32[16,32,128]{2,1,0:T(8,128)S(1)} %collective-permute-done.4.rest_ref, bf16[16,2,32,1024]{3,2,1,0:T(8,128)(2,1)S(1)} %bitcast.26, ...), custom_call_target="tpu_custom_call" | custom-call | tf_op jit(solution)/shard_map/while/body/pallas_call | solution.py:570
  278.1 16.2 %all_to_all.67.chunks_ref.arrived_ref = f32[16,48,128]{2,1,0:T(8,128)S(1)} all-to-all(f32[16,48,128]{2,1,0:T(8,128)S(1)} %body.26), channel_id=1, replica_groups=mesh['chips'=8,'core'=2,'genes'=2] {'chips','genes'}, dimensions={0} | all-to-all | bytes 786432 | tf_op jit(solution)/shard_map/while/body/all_to_all | solution.py:496
  294.4 12.7 %all_to_all.68.half_ref = f32[16,32,128]{2,1,0:T(8,128)S(1)} all-to-all(f32[16,32,128]{2,1,0:T(8,128)S(1)} %body.27), channel_id=1, replica_groups=mesh['chips'=8,'core'=2,'genes'=2] {'chips','genes'}, dimensions={0} | all-to-all | bytes 524288 | tf_op jit(solution)/shard_map/while/body/all_to_all | solution.py:496
  307.1 1.5 body.28
  308.6 3.5 %body.29 = (f32[64,1000]{1,0:T(8,128)}, s32[1]{0:T(128)}) custom-call(s32[2]{0:T(128)S(1)} %pad_add_fusion.place_ref, f32[16,32,128]{2,1,0:T(8,128)S(1)} %all_to_all.68.half_ref, f32[16,32,128]{2,1,0:T(8,128)S(1)} %collective-permute-done.6.rest_ref, f32[64,64]{1,0:T(8,128)S(1)} %get-tuple-element.45.gram_ref, f32[64,128]{1,0:T(8,128)S(1)} %get-tuple-element.46.refs_0_, ...), custom_call_target="tpu_custom_call" | custom-call | tf_op jit(solution)/shard_map/while/body/pallas_call | solution.py:590
  (60 shorter events, 17.2 us)
Async XLA Ops:
  4.0 7.3 %copy-start = (f32[1000,64]{0,1:T(8,128)S(1)}, f32[1000,64]{0,1:T(8,128)}, u32[]{:S(2)}) copy-start(f32[1000,64]{0,1:T(8,128)} %param.8) | copy-start | bytes 768004
  4.0 56.1 %all-to-all-start.7 = ((bf16[32,32,1024]{2,1,0:T(8,128)(2,1)}), bf16[32,32,1024]{2,1,0:T(8,128)(2,1)S(1)}, u32[]{:S(2)}, u32[]{:S(2)}) async-start(bf16[32,32,1024]{2,1,0:T(8,128)(2,1)} %shard_map.68), calls=%async_computation.7 | async-start | bytes 4194304 | tf_op jit(solution)/shard_map/all_to_all | solution.py:522
  11.4 21.0 %collective-permute-start.7 = (bf16[64,1024]{1,0:T(8,128)(2,1)S(1)}, bf16[64,1024]{1,0:T(8,128)(2,1)S(1)}, u32[]{:S(2)}, u32[]{:S(2)}) collective-permute-start(bf16[64,1024]{1,0:T(8,128)(2,1)S(1)} %get-tuple-element.114), channel_id=1, source_target_pairs={{0,1},{1,0},{2,3},{3,2},{4,5},{5,4},{6,7},{7,6},{8,9},{9,8},{10,11... | collective-permute-start | bytes 393224 | tf_op jit(solution)/shard_map/ppermute | solution.py:505
  62.5 1.4 collective-permute-start.8
  87.0 1.3 collective-permute-start.9
  91.4 1.4 collective-permute-start.10
  114.3 1.3 collective-permute-start.11
  118.7 1.5 collective-permute-start.12
  119.0 29.6 %copy-start.1 = (s32[4,8]{1,0:T(4,128)S(1)}, s32[4,8]{1,0:T(4,128)}, u32[]{:S(2)}) copy-start(s32[4,8]{1,0:T(4,128)} %dev_any.1) | copy-start | bytes 388
  119.0 29.6 %copy-start.2 = (s32[4,8]{1,0:T(4,128)S(1)}, s32[4,8]{1,0:T(4,128)}, u32[]{:S(2)}) copy-start(s32[4,8]{1,0:T(4,128)} %slot_any.1) | copy-start | bytes 388
  119.0 29.6 %copy-start.3 = (s32[4,8]{1,0:T(4,128)S(1)}, s32[4,8]{1,0:T(4,128)}, u32[]{:S(2)}) copy-start(s32[4,8]{1,0:T(4,128)} %weight_any.1) | copy-start | bytes 388
  143.1 1.5 collective-permute-start.13
  152.2 51.5 %all-to-all-start = ((bf16[32,32,1024]{2,1,0:T(8,128)(2,1)}), bf16[32,32,1024]{2,1,0:T(8,128)(2,1)S(1)}, u32[]{:S(2)}, u32[]{:S(2)}) async-start(bf16[32,32,1024]{2,1,0:T(8,128)(2,1)} %body.15), calls=%async_computation | async-start | bytes 4194304 | tf_op jit(solution)/shard_map/while/body/all_to_all | solution.py:522
  154.9 21.0 %collective-permute-start = (bf16[64,1024]{1,0:T(8,128)(2,1)S(1)}, bf16[64,1024]{1,0:T(8,128)(2,1)S(1)}, u32[]{:S(2)}, u32[]{:S(2)}) collective-permute-start(bf16[64,1024]{1,0:T(8,128)(2,1)S(1)} %get-tuple-element.110), channel_id=1, source_target_pairs={{0,1},{1,0},{2,3},{3,2},{4,5},{5,4},{6,7},{7,6},{8,9},{9,8},{10,11... | collective-permute-start | bytes 393224 | tf_op jit(solution)/shard_map/while/body/ppermute | solution.py:505
  206.1 1.6 collective-permute-start.1
  235.1 1.5 collective-permute-start.2
  241.7 1.6 collective-permute-start.3
  269.6 1.5 collective-permute-start.4
  276.2 1.8 collective-permute-start.5
  307.1 1.5 collective-permute-start.6

commit v9 on v8

--- a/solution.py
+++ b/solution.py
@@ -30,24 +30,27 @@
     shape = strips[0].shape
     place = lax.broadcasted_iota(jnp.int32, shape, 0)
     done = []
-    for panel, strip in enumerate(strips):
+
+    def column(of, lane):
+        return jnp.broadcast_to(of[:, lane : lane + 1], shape)
+
+    ahead = [column(strips[0], width + j) for j in range(8)]
+    for panel in range(len(strips)):
         base = width + 8 * panel
-
-        def column(of, j):
-            return jnp.broadcast_to(of[:, base + j : base + j + 1], shape)
-
         slot = spread_ref.at[panel % 2]
         for j in range(8):
-            slot[j] = column(strip, j)
-        slot[8] = strip
+            slot[j] = ahead[j]
+        slot[16] = strips[panel]
 
         def row(of, i):
             return slot[of, pl.ds(i, 8, stride=0)]
 
         core = {(i, j): row(j, i) for j in range(8) for i in range(j, 8)}
-        lines = [row(8, j) for j in range(8)]
+        lines = [row(16, j) for j in range(8)]
         below = range(panel + 1, len(strips))
-        rest = {(at, j): column(strips[at], j) for at in below for j in range(8)}
+        rest = {(at, j): column(strips[at], base + j) for at in below for j in range(8)}
+        if below:
+            ahead = [column(strips[panel + 1], base + 8 + j) for j in range(8)]
         for j in range(0, 8, 2):
             a, b, c = core[j, j], core[j + 1, j], core[j + 1, j + 1]
             area = a * c - b * b
@@ -63,10 +66,14 @@
                     core[i, m] -= first * core[m, j] + second * left[m]
                 lines[i] -= first * lines[j] + second * lines[j + 1]
             for at in below:
-                first = rest[at, j] * over
-                second = (rest[at, j + 1] - step * rest[at, j]) * later
+                rest[at, j + 1] -= step * rest[at, j]
+                first, second = rest[at, j] * over, rest[at, j + 1] * later
                 for m in range(j + 2, 8):
                     rest[at, m] -= first * core[m, j] + second * left[m]
+                if at == panel + 1:
+                    slot[8 + j], slot[9 + j] = rest[at, j], rest[at, j + 1]
+                    for i in range(8):
+                        ahead[i] -= first * row(8 + j, i) + second * row(9 + j, i)
                 strips[at] -= first * lines[j] + second * lines[j + 1]
         final = lines[0] * lax.rsqrt(core[0, 0])
         for j in range(1, 8):
@@ -530,7 +537,7 @@
 
     part = pltpu.VMEM((width, padded), kept)
     update = pltpu.VMEM((groups, width, padded), kept)
-    spread = pltpu.VMEM((2, 9, 8, 2 * width), jnp.float32)
+    spread = pltpu.VMEM((2, 17, 8, 2 * width), jnp.float32)
     second_shape = shape(width, cells, dtype=jnp.bfloat16)
     worst = shape(width, LANES)
     earlier = []

time: 313 us -> 312 us (level)
  no operation moved by 1% of the time
where the time goes in v9:
time: 312 us; the launch traced here: 311 us
  blocking collectives  150 us (48%)
  waiting for transfers between devices  100 us (32%)
  Pallas kernels  43.8 us (14%)
  starting transfers between devices  14.7 us (5%)
    all_to_all x12, blocking collectives, exchange(): return lax.all_to_all(array, ('chips', 'genes'), 0, 0, tiled=True)  150 us
    all_to_all x2, waiting for transfers between devices, by_cell(): moved = lax.all_to_all(moved, ('chips', 'core', 'genes'), 0, 0, tiled=True)  55.3 us
    ppermute x2, waiting for transfers between devices, by_cell(): starts.append(lax.ppermute(narrow, 'genes', pairs))  38.4 us
    pallas_call x4, Pallas kernels, by_cell(): call(functools.partial(kernel, genes_here, chunk), (share, second_shape,...  15.4 us
    all_to_all x2, starting transfers between devices, by_cell(): moved = lax.all_to_all(moved, ('chips', 'core', 'genes'), 0, 0, tiled=True)  10 us
    ppermute x12, waiting for transfers between devices, swap(): return lax.ppermute(array, 'core', [(0, 1), (1, 0)])  6.79 us
    pallas_call x2, Pallas kernels, by_cell(): pl.pallas_call(functools.partial(regroup_kernel, rows_of), out_shape=jax....  6.73 us
    pallas_call x2, Pallas kernels, by_cell(): call(functools.partial(last_kernel, genes_here), (shape(width, genes_here...  6.29 us
  transfers between devices with their start and end apart: 16, of which 14 were waited for; matrix products, arithmetic and copies ran while one was open for 0% of the time, Pallas kernels for 3%

profile of v9, /device:TPU:0, one launch (start us, length us, event | category | flops | bytes accessed | tf_op | source)
XLA Modules:
  0.0 311.1 jit_solution(15310364882321098597)
XLA Ops:
  0.6 3.4 %shard_map.68 = bf16[32,32,1024]{2,1,0:T(8,128)(2,1)} custom-call(bf16[1000,1024]{1,0:T(8,128)(2,1)} %bitcast.10.data_any, s32[4,8]{1,0:T(4,128)} %dev_any.1, s32[4,8]{1,0:T(4,128)} %slot_any.1, s32[4,8]{1,0:T(4,128)} %weight_any.1), custom_call_target="tpu_custom_call" | custom-call | tf_op jit(solution)/shard_map/pallas_call | solution.py:514
  4.0 7.3 %all-to-all-start.7 = ((bf16[32,32,1024]{2,1,0:T(8,128)(2,1)}), bf16[32,32,1024]{2,1,0:T(8,128)(2,1)S(1)}, u32[]{:S(2)}, u32[]{:S(2)}) async-start(bf16[32,32,1024]{2,1,0:T(8,128)(2,1)} %shard_map.68), calls=%async_computation.7 | async-start | bytes 4194304 | tf_op jit(solution)/shard_map/all_to_all | solution.py:529
  11.4 1.8 collective-permute-start.7
  13.3 19.1 %collective-permute-done.7 = bf16[64,1024]{1,0:T(8,128)(2,1)S(1)} collective-permute-done((bf16[64,1024]{1,0:T(8,128)(2,1)S(1)}, bf16[64,1024]{1,0:T(8,128)(2,1)S(1)}, u32[]{:S(2)}, u32[]{:S(2)}) %collective-permute-start.7) | collective-permute-done | bytes 131104 | tf_op jit(solution)/shard_map/ppermute | solution.py:512
  32.5 27.6 %all-to-all-done.7 = bf16[32,32,1024]{2,1,0:T(8,128)(2,1)S(1)} async-done(((bf16[32,32,1024]{2,1,0:T(8,128)(2,1)}), bf16[32,32,1024]{2,1,0:T(8,128)(2,1)S(1)}, u32[]{:S(2)}, u32[]{:S(2)}) %all-to-all-start.7) | async-done | bytes 2097184 | tf_op jit(solution)/shard_map/all_to_all | solution.py:529
  60.1 2.4 shard_map.69
  64.0 12.3 %all_to_all.69.chunks_ref = bf16[16,32,128]{2,1,0:T(8,128)(2,1)S(1)} all-to-all(bf16[16,32,128]{2,1,0:T(8,128)(2,1)S(1)} %shard_map.71), channel_id=1, replica_groups=mesh['chips'=8,'core'=2,'genes'=2] {'chips','genes'}, dimensions={0} | all-to-all | bytes 262144 | tf_op jit(solution)/shard_map/all_to_all | solution.py:503
  76.2 10.7 %all_to_all.70.half_ref = bf16[16,32,128]{2,1,0:T(8,128)(2,1)S(1)} all-to-all(bf16[16,32,128]{2,1,0:T(8,128)(2,1)S(1)} %shard_map.72), channel_id=1, replica_groups=mesh['chips'=8,'core'=2,'genes'=2] {'chips','genes'}, dimensions={0} | all-to-all | bytes 262144 | tf_op jit(solution)/shard_map/all_to_all | solution.py:503
  88.3 2.8 shard_map.74
  92.6 10.7 %all_to_all.71.chunks_ref = bf16[16,32,128]{2,1,0:T(8,128)(2,1)S(1)} all-to-all(bf16[16,32,128]{2,1,0:T(8,128)(2,1)S(1)} %shard_map.76), channel_id=1, replica_groups=mesh['chips'=8,'core'=2,'genes'=2] {'chips','genes'}, dimensions={0} | all-to-all | bytes 262144 | tf_op jit(solution)/shard_map/all_to_all | solution.py:503
  103.3 10.7 %all_to_all.72.half_ref = bf16[16,32,128]{2,1,0:T(8,128)(2,1)S(1)} all-to-all(bf16[16,32,128]{2,1,0:T(8,128)(2,1)S(1)} %shard_map.77), channel_id=1, replica_groups=mesh['chips'=8,'core'=2,'genes'=2] {'chips','genes'}, dimensions={0} | all-to-all | bytes 262144 | tf_op jit(solution)/shard_map/all_to_all | solution.py:503
  115.4 2.8 shard_map.79
  119.8 11.5 %all_to_all.73.chunks_ref.arrived_ref = bf16[16,48,128]{2,1,0:T(8,128)(2,1)S(1)} all-to-all(bf16[16,48,128]{2,1,0:T(8,128)(2,1)S(1)} %shard_map.81), channel_id=1, replica_groups=mesh['chips'=8,'core'=2,'genes'=2] {'chips','genes'}, dimensions={0} | all-to-all | bytes 393216 | tf_op jit(solution)/shard_map/all_to_all | solution.py:503
  131.3 11.3 %all_to_all.74.half_ref = bf16[16,32,128]{2,1,0:T(8,128)(2,1)S(1)} all-to-all(bf16[16,32,128]{2,1,0:T(8,128)(2,1)S(1)} %shard_map.82), channel_id=1, replica_groups=mesh['chips'=8,'core'=2,'genes'=2] {'chips','genes'}, dimensions={0} | all-to-all | bytes 262144 | tf_op jit(solution)/shard_map/all_to_all | solution.py:503
  144.1 3.1 shard_map.84
  147.9 163.0 %while.11 = (f32[1000,64]{0,1:T(8,128)}, bf16[32,1024]{1,0:T(8,128)(2,1)}, pred[]{:T(512)}, bf16[1024,1000]{0,1:T(8,128)(2,1)}, s32[4,8]{1,0:T(4,128)S(1)}, /*in...) while((f32[1000,64]{0,1:T(8,128)}, bf16[32,1024]{1,0:T(8,128)(2,1)}, pred[]{:T(512)}, ...), condition=%region_1.2_spmd, body=%region_0.1_spmd | while | flops 131080 | bytes 17954240 | solution.py:609
  148.1 3.4 %body.15 = bf16[32,32,1024]{2,1,0:T(8,128)(2,1)} custom-call(bf16[1000,1024]{1,0:T(8,128)(2,1)} %bitcast.2.data_any, s32[4,8]{1,0:T(4,128)S(1)} %get-tuple-element.143.dev_any, s32[4,8]{1,0:T(4,128)S(1)} %get-tuple-element.144.slot_any, s32[4,8]{1,0:T(4,128)S(1)} %get-tuple-element.145.weight_any), custom_call_target="tpu_custom_call" | custom-call | tf_op jit(solution)/shard_map/while/body/pallas_call | solution.py:514
  151.5 2.7 all-to-all-start
  154.2 1.7 collective-permute-start
  156.0 19.3 %collective-permute-done = bf16[64,1024]{1,0:T(8,128)(2,1)S(1)} collective-permute-done((bf16[64,1024]{1,0:T(8,128)(2,1)S(1)}, bf16[64,1024]{1,0:T(8,128)(2,1)S(1)}, u32[]{:S(2)}, u32[]{:S(2)}) %collective-permute-start) | collective-permute-done | bytes 131104 | tf_op jit(solution)/shard_map/while/body/ppermute | solution.py:512
  175.3 27.7 %all-to-all-done = bf16[32,32,1024]{2,1,0:T(8,128)(2,1)S(1)} async-done(((bf16[32,32,1024]{2,1,0:T(8,128)(2,1)}), bf16[32,32,1024]{2,1,0:T(8,128)(2,1)S(1)}, u32[]{:S(2)}, u32[]{:S(2)}) %all-to-all-start) | async-done | bytes 2097184 | tf_op jit(solution)/shard_map/while/body/all_to_all | solution.py:529
  203.0 2.4 body.16
  207.0 14.5 %all_to_all.63.chunks_ref = f32[16,32,128]{2,1,0:T(8,128)S(1)} all-to-all(f32[16,32,128]{2,1,0:T(8,128)S(1)} %body.18), channel_id=1, replica_groups=mesh['chips'=8,'core'=2,'genes'=2] {'chips','genes'}, dimensions={0} | all-to-all | bytes 524288 | tf_op jit(solution)/shard_map/while/body/all_to_all | solution.py:503
  221.6 12.8 %all_to_all.64.half_ref = f32[16,32,128]{2,1,0:T(8,128)S(1)} all-to-all(f32[16,32,128]{2,1,0:T(8,128)S(1)} %body.19), channel_id=1, replica_groups=mesh['chips'=8,'core'=2,'genes'=2] {'chips','genes'}, dimensions={0} | all-to-all | bytes 524288 | tf_op jit(solution)/shard_map/while/body/all_to_all | solution.py:503
  235.9 4.9 %body.20 = (f32[16,32,128]{2,1,0:T(8,128)S(1)}, bf16[64,512]{1,0:T(8,128)(2,1)S(1)}, f32[64,128]{1,0:T(8,128)S(1)}) custom-call(s32[2]{0:T(128)S(1)} %pad_add_fusion.place_ref, f32[16,32,128]{2,1,0:T(8,128)S(1)} %all_to_all.64.half_ref, f32[16,32,128]{2,1,0:T(8,128)S(1)} %collective-permute-done.2.rest_ref, bf16[16,2,32,1024]{3,2,1,0:T(8,128)(2,1)S(1)} %bitcast.24, ...), custom_call_target="tpu_custom_call" | custom-call | tf_op jit(solution)/shard_map/while/body/pallas_call | solution.py:577
  242.4 13.5 %all_to_all.65.chunks_ref = f32[16,32,128]{2,1,0:T(8,128)S(1)} all-to-all(f32[16,32,128]{2,1,0:T(8,128)S(1)} %body.22), channel_id=1, replica_groups=mesh['chips'=8,'core'=2,'genes'=2] {'chips','genes'}, dimensions={0} | all-to-all | bytes 524288 | tf_op jit(solution)/shard_map/while/body/all_to_all | solution.py:503
  255.9 12.8 %all_to_all.66.half_ref = f32[16,32,128]{2,1,0:T(8,128)S(1)} all-to-all(f32[16,32,128]{2,1,0:T(8,128)S(1)} %body.23), channel_id=1, replica_groups=mesh['chips'=8,'core'=2,'genes'=2] {'chips','genes'}, dimensions={0} | all-to-all | bytes 524288 | tf_op jit(solution)/shard_map/while/body/all_to_all | solution.py:503
  270.2 4.9 %body.24 = (f32[16,48,128]{2,1,0:T(8,128)S(1)}, bf16[64,512]{1,0:T(8,128)(2,1)S(1)}, f32[64,128]{1,0:T(8,128)S(1)}) custom-call(s32[2]{0:T(128)S(1)} %pad_add_fusion.place_ref, f32[16,32,128]{2,1,0:T(8,128)S(1)} %all_to_all.66.half_ref, f32[16,32,128]{2,1,0:T(8,128)S(1)} %collective-permute-done.4.rest_ref, bf16[16,2,32,1024]{3,2,1,0:T(8,128)(2,1)S(1)} %bitcast.26, ...), custom_call_target="tpu_custom_call" | custom-call | tf_op jit(solution)/shard_map/while/body/pallas_call | solution.py:577
  276.9 16.2 %all_to_all.67.chunks_ref.arrived_ref = f32[16,48,128]{2,1,0:T(8,128)S(1)} all-to-all(f32[16,48,128]{2,1,0:T(8,128)S(1)} %body.26), channel_id=1, replica_groups=mesh['chips'=8,'core'=2,'genes'=2] {'chips','genes'}, dimensions={0} | all-to-all | bytes 786432 | tf_op jit(solution)/shard_map/while/body/all_to_all | solution.py:503
  293.2 12.7 %all_to_all.68.half_ref = f32[16,32,128]{2,1,0:T(8,128)S(1)} all-to-all(f32[16,32,128]{2,1,0:T(8,128)S(1)} %body.27), channel_id=1, replica_groups=mesh['chips'=8,'core'=2,'genes'=2] {'chips','genes'}, dimensions={0} | all-to-all | bytes 524288 | tf_op jit(solution)/shard_map/while/body/all_to_all | solution.py:503
  305.9 1.5 body.28
  307.5 3.2 %body.29 = (f32[64,1000]{1,0:T(8,128)}, s32[1]{0:T(128)}) custom-call(s32[2]{0:T(128)S(1)} %pad_add_fusion.place_ref, f32[16,32,128]{2,1,0:T(8,128)S(1)} %all_to_all.68.half_ref, f32[16,32,128]{2,1,0:T(8,128)S(1)} %collective-permute-done.6.rest_ref, f32[64,64]{1,0:T(8,128)S(1)} %get-tuple-element.45.gram_ref, f32[64,128]{1,0:T(8,128)S(1)} %get-tuple-element.46.refs_0_, ...), custom_call_target="tpu_custom_call" | custom-call | tf_op jit(solution)/shard_map/while/body/pallas_call | solution.py:597
  (60 shorter events, 17.2 us)
Async XLA Ops:
  4.0 7.3 %copy-start = (f32[1000,64]{0,1:T(8,128)S(1)}, f32[1000,64]{0,1:T(8,128)}, u32[]{:S(2)}) copy-start(f32[1000,64]{0,1:T(8,128)} %param.8) | copy-start | bytes 768004
  4.0 56.1 %all-to-all-start.7 = ((bf16[32,32,1024]{2,1,0:T(8,128)(2,1)}), bf16[32,32,1024]{2,1,0:T(8,128)(2,1)S(1)}, u32[]{:S(2)}, u32[]{:S(2)}) async-start(bf16[32,32,1024]{2,1,0:T(8,128)(2,1)} %shard_map.68), calls=%async_computation.7 | async-start | bytes 4194304 | tf_op jit(solution)/shard_map/all_to_all | solution.py:529
  11.4 21.0 %collective-permute-start.7 = (bf16[64,1024]{1,0:T(8,128)(2,1)S(1)}, bf16[64,1024]{1,0:T(8,128)(2,1)S(1)}, u32[]{:S(2)}, u32[]{:S(2)}) collective-permute-start(bf16[64,1024]{1,0:T(8,128)(2,1)S(1)} %get-tuple-element.114), channel_id=1, source_target_pairs={{0,1},{1,0},{2,3},{3,2},{4,5},{5,4},{6,7},{7,6},{8,9},{9,8},{10,11... | collective-permute-start | bytes 393224 | tf_op jit(solution)/shard_map/ppermute | solution.py:512
  62.5 1.4 collective-permute-start.8
  87.0 1.3 collective-permute-start.9
  91.1 1.4 collective-permute-start.10
  114.0 1.3 collective-permute-start.11
  118.2 1.5 collective-permute-start.12
  118.5 29.4 %copy-start.1 = (s32[4,8]{1,0:T(4,128)S(1)}, s32[4,8]{1,0:T(4,128)}, u32[]{:S(2)}) copy-start(s32[4,8]{1,0:T(4,128)} %dev_any.1) | copy-start | bytes 388
  118.5 29.4 %copy-start.2 = (s32[4,8]{1,0:T(4,128)S(1)}, s32[4,8]{1,0:T(4,128)}, u32[]{:S(2)}) copy-start(s32[4,8]{1,0:T(4,128)} %slot_any.1) | copy-start | bytes 388
  118.5 29.4 %copy-start.3 = (s32[4,8]{1,0:T(4,128)S(1)}, s32[4,8]{1,0:T(4,128)}, u32[]{:S(2)}) copy-start(s32[4,8]{1,0:T(4,128)} %weight_any.1) | copy-start | bytes 388
  142.6 1.5 collective-permute-start.13
  151.5 51.5 %all-to-all-start = ((bf16[32,32,1024]{2,1,0:T(8,128)(2,1)}), bf16[32,32,1024]{2,1,0:T(8,128)(2,1)S(1)}, u32[]{:S(2)}, u32[]{:S(2)}) async-start(bf16[32,32,1024]{2,1,0:T(8,128)(2,1)} %body.15), calls=%async_computation | async-start | bytes 4194304 | tf_op jit(solution)/shard_map/while/body/all_to_all | solution.py:529
  154.2 21.0 %collective-permute-start = (bf16[64,1024]{1,0:T(8,128)(2,1)S(1)}, bf16[64,1024]{1,0:T(8,128)(2,1)S(1)}, u32[]{:S(2)}, u32[]{:S(2)}) collective-permute-start(bf16[64,1024]{1,0:T(8,128)(2,1)S(1)} %get-tuple-element.110), channel_id=1, source_target_pairs={{0,1},{1,0},{2,3},{3,2},{4,5},{5,4},{6,7},{7,6},{8,9},{9,8},{10,11... | collective-permute-start | bytes 393224 | tf_op jit(solution)/shard_map/while/body/ppermute | solution.py:512
  205.4 1.6 collective-permute-start.1
  234.3 1.5 collective-permute-start.2
  240.7 1.6 collective-permute-start.3
  268.7 1.5 collective-permute-start.4
  275.1 1.8 collective-permute-start.5
  305.9 1.5 collective-permute-start.6

commit v10 on v9

--- a/solution.py
+++ b/solution.py
@@ -232,13 +232,13 @@
         own_tile = tile == lax.broadcasted_iota(jnp.int32, (slots, cells), 1) // tile_cells
         row = lax.broadcasted_iota(jnp.int32, (padded - genes_here, cells), 0)
         links = jnp.zeros((padded - genes_here, cells), jnp.float32)
-        for at, copy in enumerate(link_copies):
+        for copy in link_copies:
             copy.wait()
-            wide = jnp.dot(
-                link_ref[at].astype(jnp.float32), spread, preferred_element_type=jnp.float32
-            )
-            wide = jnp.sum(jnp.where(own_tile, wide, 0.0), axis=0, keepdims=True)
-            links = jnp.where(row == at, wide, links)
+        known = jnp.concatenate([link_ref[at] for at in range(3)], axis=0).astype(jnp.float32)
+        wide = jnp.dot(known, spread, preferred_element_type=jnp.float32)
+        for at in range(3):
+            one = jnp.where(own_tile, wide[at * slots : (at + 1) * slots], 0.0)
+            links = jnp.where(row == at, jnp.sum(one, axis=0, keepdims=True), links)
         return links
 
     def turned(part):
@@ -449,7 +449,16 @@
     for worst_ref in earlier:
         good = good & (worst_ref[:, :1] <= AMPLIFIED)
     good_ref[0] = jnp.min(good.astype(jnp.int32))
-    loadings = apply(inverse, update_ref[own].astype(jnp.float32))
+    mine = update_ref[own]
+    if mine.dtype == jnp.float32:
+        loadings = apply(inverse, mine)
+    else:
+        loadings = None
+        for _ in range(3):
+            piece = inverse.astype(jnp.bfloat16)
+            inverse = inverse - piece.astype(jnp.float32)
+            part = jnp.dot(piece, mine, preferred_element_type=jnp.float32)
+            loadings = part if loadings is None else loadings + part
     out_ref[...] = loadings[:, :genes_here]
 
 

time: 312 us -> 311 us (level)
  no operation moved by 1% of the time
where the time goes in v10:
time: 311 us; the launch traced here: 310 us
  blocking collectives  150 us (48%)
  waiting for transfers between devices  100 us (32%)
  Pallas kernels  43.1 us (14%)
  starting transfers between devices  14.7 us (5%)
    all_to_all x12, blocking collectives, exchange(): return lax.all_to_all(array, ('chips', 'genes'), 0, 0, tiled=True)  150 us
    all_to_all x2, waiting for transfers between devices, by_cell(): moved = lax.all_to_all(moved, ('chips', 'core', 'genes'), 0, 0, tiled=True)  55.3 us
    ppermute x2, waiting for transfers between devices, by_cell(): starts.append(lax.ppermute(narrow, 'genes', pairs))  38.4 us
    pallas_call x4, Pallas kernels, by_cell(): call(functools.partial(kernel, genes_here, chunk), (share, second_shape,...  15.4 us
    all_to_all x2, starting transfers between devices, by_cell(): moved = lax.all_to_all(moved, ('chips', 'core', 'genes'), 0, 0, tiled=True)  10 us
    ppermute x12, waiting for transfers between devices, swap(): return lax.ppermute(array, 'core', [(0, 1), (1, 0)])  6.79 us
    pallas_call x2, Pallas kernels, by_cell(): pl.pallas_call(functools.partial(regroup_kernel, rows_of), out_shape=jax....  6.23 us
  transfers between devices with their start and end apart: 16, of which 14 were waited for; matrix products, arithmetic and copies ran while one was open for 0% of the time, Pallas kernels for 3%

profile of v10, /device:TPU:0, one launch (start us, length us, event | category | flops | bytes accessed | tf_op | source)
XLA Modules:
  0.0 310.5 jit_solution(5231011058057282510)
XLA Ops:
  0.6 3.1 %shard_map.68 = bf16[32,32,1024]{2,1,0:T(8,128)(2,1)} custom-call(bf16[1000,1024]{1,0:T(8,128)(2,1)} %bitcast.10.data_any, s32[4,8]{1,0:T(4,128)} %dev_any.1, s32[4,8]{1,0:T(4,128)} %slot_any.1, s32[4,8]{1,0:T(4,128)} %weight_any.1), custom_call_target="tpu_custom_call" | custom-call | tf_op jit(solution)/shard_map/pallas_call | solution.py:523
  3.8 7.3 %all-to-all-start.7 = ((bf16[32,32,1024]{2,1,0:T(8,128)(2,1)}), bf16[32,32,1024]{2,1,0:T(8,128)(2,1)S(1)}, u32[]{:S(2)}, u32[]{:S(2)}) async-start(bf16[32,32,1024]{2,1,0:T(8,128)(2,1)} %shard_map.68), calls=%async_computation.7 | async-start | bytes 4194304 | tf_op jit(solution)/shard_map/all_to_all | solution.py:538
  11.1 1.8 collective-permute-start.7
  13.0 19.1 %collective-permute-done.7 = bf16[64,1024]{1,0:T(8,128)(2,1)S(1)} collective-permute-done((bf16[64,1024]{1,0:T(8,128)(2,1)S(1)}, bf16[64,1024]{1,0:T(8,128)(2,1)S(1)}, u32[]{:S(2)}, u32[]{:S(2)}) %collective-permute-start.7) | collective-permute-done | bytes 131104 | tf_op jit(solution)/shard_map/ppermute | solution.py:521
  32.2 27.6 %all-to-all-done.7 = bf16[32,32,1024]{2,1,0:T(8,128)(2,1)S(1)} async-done(((bf16[32,32,1024]{2,1,0:T(8,128)(2,1)}), bf16[32,32,1024]{2,1,0:T(8,128)(2,1)S(1)}, u32[]{:S(2)}, u32[]{:S(2)}) %all-to-all-start.7) | async-done | bytes 2097184 | tf_op jit(solution)/shard_map/all_to_all | solution.py:538
  59.8 2.4 shard_map.69
  63.7 12.2 %all_to_all.69.chunks_ref = bf16[16,32,128]{2,1,0:T(8,128)(2,1)S(1)} all-to-all(bf16[16,32,128]{2,1,0:T(8,128)(2,1)S(1)} %shard_map.71), channel_id=1, replica_groups=mesh['chips'=8,'core'=2,'genes'=2] {'chips','genes'}, dimensions={0} | all-to-all | bytes 262144 | tf_op jit(solution)/shard_map/all_to_all | solution.py:512
  76.0 10.7 %all_to_all.70.half_ref = bf16[16,32,128]{2,1,0:T(8,128)(2,1)S(1)} all-to-all(bf16[16,32,128]{2,1,0:T(8,128)(2,1)S(1)} %shard_map.72), channel_id=1, replica_groups=mesh['chips'=8,'core'=2,'genes'=2] {'chips','genes'}, dimensions={0} | all-to-all | bytes 262144 | tf_op jit(solution)/shard_map/all_to_all | solution.py:512
  88.1 2.8 shard_map.74
  92.4 10.7 %all_to_all.71.chunks_ref = bf16[16,32,128]{2,1,0:T(8,128)(2,1)S(1)} all-to-all(bf16[16,32,128]{2,1,0:T(8,128)(2,1)S(1)} %shard_map.76), channel_id=1, replica_groups=mesh['chips'=8,'core'=2,'genes'=2] {'chips','genes'}, dimensions={0} | all-to-all | bytes 262144 | tf_op jit(solution)/shard_map/all_to_all | solution.py:512
  103.1 10.7 %all_to_all.72.half_ref = bf16[16,32,128]{2,1,0:T(8,128)(2,1)S(1)} all-to-all(bf16[16,32,128]{2,1,0:T(8,128)(2,1)S(1)} %shard_map.77), channel_id=1, replica_groups=mesh['chips'=8,'core'=2,'genes'=2] {'chips','genes'}, dimensions={0} | all-to-all | bytes 262144 | tf_op jit(solution)/shard_map/all_to_all | solution.py:512
  115.1 2.8 shard_map.79
  119.5 11.5 %all_to_all.73.chunks_ref.arrived_ref = bf16[16,48,128]{2,1,0:T(8,128)(2,1)S(1)} all-to-all(bf16[16,48,128]{2,1,0:T(8,128)(2,1)S(1)} %shard_map.81), channel_id=1, replica_groups=mesh['chips'=8,'core'=2,'genes'=2] {'chips','genes'}, dimensions={0} | all-to-all | bytes 393216 | tf_op jit(solution)/shard_map/all_to_all | solution.py:512
  131.0 11.3 %all_to_all.74.half_ref = bf16[16,32,128]{2,1,0:T(8,128)(2,1)S(1)} all-to-all(bf16[16,32,128]{2,1,0:T(8,128)(2,1)S(1)} %shard_map.82), channel_id=1, replica_groups=mesh['chips'=8,'core'=2,'genes'=2] {'chips','genes'}, dimensions={0} | all-to-all | bytes 262144 | tf_op jit(solution)/shard_map/all_to_all | solution.py:512
  143.9 2.9 shard_map.84
  147.5 162.8 %while.11 = (f32[1000,64]{0,1:T(8,128)}, bf16[32,1024]{1,0:T(8,128)(2,1)}, pred[]{:T(512)}, bf16[1024,1000]{0,1:T(8,128)(2,1)}, s32[4,8]{1,0:T(4,128)S(1)}, /*in...) while((f32[1000,64]{0,1:T(8,128)}, bf16[32,1024]{1,0:T(8,128)(2,1)}, pred[]{:T(512)}, ...), condition=%region_1.2_spmd, body=%region_0.1_spmd | while | flops 131080 | bytes 17954240 | solution.py:618
  147.7 3.1 %body.15 = bf16[32,32,1024]{2,1,0:T(8,128)(2,1)} custom-call(bf16[1000,1024]{1,0:T(8,128)(2,1)} %bitcast.2.data_any, s32[4,8]{1,0:T(4,128)S(1)} %get-tuple-element.143.dev_any, s32[4,8]{1,0:T(4,128)S(1)} %get-tuple-element.144.slot_any, s32[4,8]{1,0:T(4,128)S(1)} %get-tuple-element.145.weight_any), custom_call_target="tpu_custom_call" | custom-call | tf_op jit(solution)/shard_map/while/body/pallas_call | solution.py:523
  150.8 2.7 all-to-all-start
  153.6 1.7 collective-permute-start
  155.4 19.3 %collective-permute-done = bf16[64,1024]{1,0:T(8,128)(2,1)S(1)} collective-permute-done((bf16[64,1024]{1,0:T(8,128)(2,1)S(1)}, bf16[64,1024]{1,0:T(8,128)(2,1)S(1)}, u32[]{:S(2)}, u32[]{:S(2)}) %collective-permute-start) | collective-permute-done | bytes 131104 | tf_op jit(solution)/shard_map/while/body/ppermute | solution.py:521
  174.7 27.7 %all-to-all-done = bf16[32,32,1024]{2,1,0:T(8,128)(2,1)S(1)} async-done(((bf16[32,32,1024]{2,1,0:T(8,128)(2,1)}), bf16[32,32,1024]{2,1,0:T(8,128)(2,1)S(1)}, u32[]{:S(2)}, u32[]{:S(2)}) %all-to-all-start) | async-done | bytes 2097184 | tf_op jit(solution)/shard_map/while/body/all_to_all | solution.py:538
  202.3 2.4 body.16
  206.4 14.5 %all_to_all.63.chunks_ref = f32[16,32,128]{2,1,0:T(8,128)S(1)} all-to-all(f32[16,32,128]{2,1,0:T(8,128)S(1)} %body.18), channel_id=1, replica_groups=mesh['chips'=8,'core'=2,'genes'=2] {'chips','genes'}, dimensions={0} | all-to-all | bytes 524288 | tf_op jit(solution)/shard_map/while/body/all_to_all | solution.py:512
  220.9 12.8 %all_to_all.64.half_ref = f32[16,32,128]{2,1,0:T(8,128)S(1)} all-to-all(f32[16,32,128]{2,1,0:T(8,128)S(1)} %body.19), channel_id=1, replica_groups=mesh['chips'=8,'core'=2,'genes'=2] {'chips','genes'}, dimensions={0} | all-to-all | bytes 524288 | tf_op jit(solution)/shard_map/while/body/all_to_all | solution.py:512
  235.2 4.9 %body.20 = (f32[16,32,128]{2,1,0:T(8,128)S(1)}, bf16[64,512]{1,0:T(8,128)(2,1)S(1)}, f32[64,128]{1,0:T(8,128)S(1)}) custom-call(s32[2]{0:T(128)S(1)} %pad_add_fusion.place_ref, f32[16,32,128]{2,1,0:T(8,128)S(1)} %all_to_all.64.half_ref, f32[16,32,128]{2,1,0:T(8,128)S(1)} %collective-permute-done.2.rest_ref, bf16[16,2,32,1024]{3,2,1,0:T(8,128)(2,1)S(1)} %bitcast.24, ...), custom_call_target="tpu_custom_call" | custom-call | tf_op jit(solution)/shard_map/while/body/pallas_call | solution.py:586
  241.7 13.5 %all_to_all.65.chunks_ref = f32[16,32,128]{2,1,0:T(8,128)S(1)} all-to-all(f32[16,32,128]{2,1,0:T(8,128)S(1)} %body.22), channel_id=1, replica_groups=mesh['chips'=8,'core'=2,'genes'=2] {'chips','genes'}, dimensions={0} | all-to-all | bytes 524288 | tf_op jit(solution)/shard_map/while/body/all_to_all | solution.py:512
  255.3 12.8 %all_to_all.66.half_ref = f32[16,32,128]{2,1,0:T(8,128)S(1)} all-to-all(f32[16,32,128]{2,1,0:T(8,128)S(1)} %body.23), channel_id=1, replica_groups=mesh['chips'=8,'core'=2,'genes'=2] {'chips','genes'}, dimensions={0} | all-to-all | bytes 524288 | tf_op jit(solution)/shard_map/while/body/all_to_all | solution.py:512
  269.6 4.9 %body.24 = (f32[16,48,128]{2,1,0:T(8,128)S(1)}, bf16[64,512]{1,0:T(8,128)(2,1)S(1)}, f32[64,128]{1,0:T(8,128)S(1)}) custom-call(s32[2]{0:T(128)S(1)} %pad_add_fusion.place_ref, f32[16,32,128]{2,1,0:T(8,128)S(1)} %all_to_all.66.half_ref, f32[16,32,128]{2,1,0:T(8,128)S(1)} %collective-permute-done.4.rest_ref, bf16[16,2,32,1024]{3,2,1,0:T(8,128)(2,1)S(1)} %bitcast.26, ...), custom_call_target="tpu_custom_call" | custom-call | tf_op jit(solution)/shard_map/while/body/pallas_call | solution.py:586
  276.3 16.2 %all_to_all.67.chunks_ref.arrived_ref = f32[16,48,128]{2,1,0:T(8,128)S(1)} all-to-all(f32[16,48,128]{2,1,0:T(8,128)S(1)} %body.26), channel_id=1, replica_groups=mesh['chips'=8,'core'=2,'genes'=2] {'chips','genes'}, dimensions={0} | all-to-all | bytes 786432 | tf_op jit(solution)/shard_map/while/body/all_to_all | solution.py:512
  292.6 12.7 %all_to_all.68.half_ref = f32[16,32,128]{2,1,0:T(8,128)S(1)} all-to-all(f32[16,32,128]{2,1,0:T(8,128)S(1)} %body.27), channel_id=1, replica_groups=mesh['chips'=8,'core'=2,'genes'=2] {'chips','genes'}, dimensions={0} | all-to-all | bytes 524288 | tf_op jit(solution)/shard_map/while/body/all_to_all | solution.py:512
  305.3 1.5 body.28
  306.8 3.2 %body.29 = (f32[64,1000]{1,0:T(8,128)}, s32[1]{0:T(128)}) custom-call(s32[2]{0:T(128)S(1)} %pad_add_fusion.place_ref, f32[16,32,128]{2,1,0:T(8,128)S(1)} %all_to_all.68.half_ref, f32[16,32,128]{2,1,0:T(8,128)S(1)} %collective-permute-done.6.rest_ref, f32[64,64]{1,0:T(8,128)S(1)} %get-tuple-element.45.gram_ref, f32[64,128]{1,0:T(8,128)S(1)} %get-tuple-element.46.refs_0_, ...), custom_call_target="tpu_custom_call" | custom-call | tf_op jit(solution)/shard_map/while/body/pallas_call | solution.py:606
  (60 shorter events, 17.2 us)
Async XLA Ops:
  3.8 7.3 %copy-start = (f32[1000,64]{0,1:T(8,128)S(1)}, f32[1000,64]{0,1:T(8,128)}, u32[]{:S(2)}) copy-start(f32[1000,64]{0,1:T(8,128)} %param.8) | copy-start | bytes 768004
  3.8 56.1 %all-to-all-start.7 = ((bf16[32,32,1024]{2,1,0:T(8,128)(2,1)}), bf16[32,32,1024]{2,1,0:T(8,128)(2,1)S(1)}, u32[]{:S(2)}, u32[]{:S(2)}) async-start(bf16[32,32,1024]{2,1,0:T(8,128)(2,1)} %shard_map.68), calls=%async_computation.7 | async-start | bytes 4194304 | tf_op jit(solution)/shard_map/all_to_all | solution.py:538
  11.1 21.0 %collective-permute-start.7 = (bf16[64,1024]{1,0:T(8,128)(2,1)S(1)}, bf16[64,1024]{1,0:T(8,128)(2,1)S(1)}, u32[]{:S(2)}, u32[]{:S(2)}) collective-permute-start(bf16[64,1024]{1,0:T(8,128)(2,1)S(1)} %get-tuple-element.114), channel_id=1, source_target_pairs={{0,1},{1,0},{2,3},{3,2},{4,5},{5,4},{6,7},{7,6},{8,9},{9,8},{10,11... | collective-permute-start | bytes 393224 | tf_op jit(solution)/shard_map/ppermute | solution.py:521
  62.3 1.4 collective-permute-start.8
  86.7 1.3 collective-permute-start.9
  90.9 1.4 collective-permute-start.10
  113.8 1.3 collective-permute-start.11
  118.0 1.5 collective-permute-start.12
  118.2 29.2 %copy-start.1 = (s32[4,8]{1,0:T(4,128)S(1)}, s32[4,8]{1,0:T(4,128)}, u32[]{:S(2)}) copy-start(s32[4,8]{1,0:T(4,128)} %dev_any.1) | copy-start | bytes 388
  118.2 29.2 %copy-start.2 = (s32[4,8]{1,0:T(4,128)S(1)}, s32[4,8]{1,0:T(4,128)}, u32[]{:S(2)}) copy-start(s32[4,8]{1,0:T(4,128)} %slot_any.1) | copy-start | bytes 388
  118.3 29.2 %copy-start.3 = (s32[4,8]{1,0:T(4,128)S(1)}, s32[4,8]{1,0:T(4,128)}, u32[]{:S(2)}) copy-start(s32[4,8]{1,0:T(4,128)} %weight_any.1) | copy-start | bytes 388
  142.4 1.5 collective-permute-start.13
  150.8 51.5 %all-to-all-start = ((bf16[32,32,1024]{2,1,0:T(8,128)(2,1)}), bf16[32,32,1024]{2,1,0:T(8,128)(2,1)S(1)}, u32[]{:S(2)}, u32[]{:S(2)}) async-start(bf16[32,32,1024]{2,1,0:T(8,128)(2,1)} %body.15), calls=%async_computation | async-start | bytes 4194304 | tf_op jit(solution)/shard_map/while/body/all_to_all | solution.py:538
  153.6 21.0 %collective-permute-start = (bf16[64,1024]{1,0:T(8,128)(2,1)S(1)}, bf16[64,1024]{1,0:T(8,128)(2,1)S(1)}, u32[]{:S(2)}, u32[]{:S(2)}) collective-permute-start(bf16[64,1024]{1,0:T(8,128)(2,1)S(1)} %get-tuple-element.110), channel_id=1, source_target_pairs={{0,1},{1,0},{2,3},{3,2},{4,5},{5,4},{6,7},{7,6},{8,9},{9,8},{10,11... | collective-permute-start | bytes 393224 | tf_op jit(solution)/shard_map/while/body/ppermute | solution.py:521
  204.7 1.6 collective-permute-start.1
  233.7 1.5 collective-permute-start.2
  240.1 1.6 collective-permute-start.3
  268.1 1.5 collective-permute-start.4
  274.5 1.8 collective-permute-start.5
  305.3 1.5 collective-permute-start.6
